TPU v7x, 32 devices: a whole 2x2x4 slice. The times are simulated.
32 devices in a mesh: dp: 8 (over y, x, core), band: 4 (over z).
Axes of the slice: x: 2, y: 2, z: 4, core: 2. Of those that a mesh axis runs over, the one named last changes fastest.
Arguments:
- images: float32 [12, 16, 16, 2048], P(None, 'band', None, 'dp'), may hold values from -0.5 to 0.46875
- noise: float32 [12, 16, 16, 2048], P(None, 'band', None, 'dp'), may hold values from 0 to 0.03125
- labels: int32 [2048], P('dp'), may hold values from 0 to 9, as said below
- conv_in: float32 [9, 512, 6], replicated, may hold values from -0.875 to 0.875
- mixer: float32 [512, 512], replicated, may hold values from -0.25 to 0.25
- conv_out: float32 [9, 12, 512], replicated, may hold values from -0.09375 to 0.09375
- prior_conv: float32 [9, 48, 24], replicated, may hold values from -0.21875 to 0.21875
- hidden_bias: float32 [2, 512], replicated, may hold values from -1 to 1
- step_gains: float32 [3, 12], replicated, may hold values from -0.5 to 0.8
- lu_parts: float32 [12, 12], replicated, may hold values from -0.9 to 0.9
- class_table: float32 [10, 96], replicated, may hold values from -1.2 to 1.2
- first_conv_in: float32 [9, 512, 6], replicated, may hold values from -7.357695e-06 to 7.357695e-06
- first_mixer: float32 [512, 512], replicated, may hold values from -7.357695e-06 to 7.357695e-06
- first_conv_out: float32 [9, 12, 512], replicated, may hold values from -7.357695e-06 to 7.357695e-06
- first_prior: float32 [9, 48, 24], replicated, may hold values from -7.357695e-06 to 7.357695e-06
- first_hidden_bias: float32 [2, 512], replicated, may hold values from -2.1738644e-05 to 2.1738644e-05
- first_gains: float32 [3, 12], replicated, may hold values from -2.1738644e-05 to 2.1738644e-05
- first_lu: float32 [12, 12], replicated, may hold values from -2.1738644e-05 to 2.1738644e-05
- first_table: float32 [10, 96], replicated, may hold values from -2.1738644e-05 to 2.1738644e-05
- second_conv_in: float32 [9, 512, 6], replicated, may hold values from 1.3981321e-13 to 2.2370114e-12
- second_mixer: float32 [512, 512], replicated, may hold values from 1.3981321e-13 to 2.2370114e-12
- second_conv_out: float32 [9, 12, 512], replicated, may hold values from 1.3981321e-13 to 2.2370114e-12
- second_prior: float32 [9, 48, 24], replicated, may hold values from 1.3981321e-13 to 2.2370114e-12
- second_hidden_bias: float32 [2, 512], replicated, may hold values from 1.2583189e-12 to 2.0133102e-11
- second_gains: float32 [3, 12], replicated, may hold values from 1.2583189e-12 to 2.0133102e-11
- second_lu: float32 [12, 12], replicated, may hold values from 1.2583189e-12 to 2.0133102e-11
- second_table: float32 [10, 96], replicated, may hold values from 1.2583189e-12 to 2.0133102e-11
Outputs:
- loss: float32 [], replicated
- grad_norm: float32 [], replicated
- new_conv_in: float32 [9, 512, 6], replicated
- new_mixer: float32 [512, 512], replicated
- new_conv_out: float32 [9, 12, 512], replicated
- new_prior: float32 [9, 48, 24], replicated
- new_hidden_bias: float32 [2, 512], replicated
- new_gains: float32 [3, 12], replicated
- new_lu: float32 [12, 12], replicated
- new_table: float32 [10, 96], replicated
- new_first_conv_in: float32 [9, 512, 6], replicated
- new_first_mixer: float32 [512, 512], replicated
- new_first_conv_out: float32 [9, 12, 512], replicated
- new_first_prior: float32 [9, 48, 24], replicated
- new_first_hidden_bias: float32 [2, 512], replicated
- new_first_gains: float32 [3, 12], replicated
- new_first_lu: float32 [12, 12], replicated
- new_first_table: float32 [10, 96], replicated
- new_second_conv_in: float32 [9, 512, 6], replicated
- new_second_mixer: float32 [512, 512], replicated
- new_second_conv_out: float32 [9, 12, 512], replicated
- new_second_prior: float32 [9, 48, 24], replicated
- new_second_hidden_bias: float32 [2, 512], replicated
- new_second_gains: float32 [3, 12], replicated
- new_second_lu: float32 [12, 12], replicated
- new_second_table: float32 [10, 96], replicated
Inputs may be any that keep to these rules, and one draw needn't show every extreme that they name: `labels`: one class, drawn from the seed, has no image at all; the first image has class 0 and the last class 10 - 1.
All inputs are finite; a program needn't handle non-finite values.
Results may differ from a plain program's by a relative error of at most 0.003.
Values may be sent and summed in bfloat16 or wider, within the bound.
No kernel may reach another device: no remote copies, remote signals or barrier semaphores. Data moves between devices by JAX's collectives and lax.ppermute only.
A program may use at most 320 MiB of HBM per device.

v0:
```python
import math

import jax
import jax.numpy as jnp
from jax import lax
from jax.sharding import PartitionSpec as P

STEP = 10


HIGH = lax.Precision.HIGHEST
LOG_TWO = math.log(2.0)
CLIP_NORM = 0.01
RATE = 0.05
BETA_ONE = 0.9
BETA_TWO = 0.999
EPSILON = 1e-08
DECAY = 0.01
BITS = 5.0


def padded_2(cells, sides, width):
    for axis, dim in sides:
        count = lax.axis_size(axis)
        ends = count - 1
        head = lax.slice_in_dim(cells, 0, width, axis=dim)
        tail = lax.slice_in_dim(cells, cells.shape[dim] - width, cells.shape[dim], axis=dim)
        cells = jnp.concatenate(
            [
                lax.ppermute(tail, axis, [(i, (i + 1) % count) for i in range(ends)]),
                cells,
                lax.ppermute(head, axis, [((i + 1) % count, i) for i in range(ends)]),
            ],
            axis=dim,
        )
    return cells


def shortened(array):

    def short(part):
        return part.astype(jnp.bfloat16) if part.dtype == jnp.float32 else part

    return jax.tree.map(short, array)


def dot_nt(left, right):
    return lax.dot_general(
        left, right, (((1,), (1,)), ((), ())), preferred_element_type=jnp.float32
    )


def dot_tn(left, right):
    return lax.dot_general(
        left, right, (((0,), (0,)), ((), ())), preferred_element_type=jnp.float32
    )


def lu_matrix(parts):
    eye = jnp.eye(parts.shape[0], dtype=parts.dtype)
    lower = jnp.tril(parts, -1) + eye
    upper = jnp.triu(parts, 1) + jnp.diag(jnp.exp(jnp.diagonal(parts)))
    return jnp.dot(lower, upper, precision=HIGH)[::-1]


def gauss(value, mean, logs):
    return -0.5 * (
        math.log(2.0 * math.pi) + 2.0 * logs + (value - mean) ** 2 * jnp.exp(-2.0 * logs)
    )


def squeeze(field):
    chans, rows, cols, count = field.shape
    split = field.reshape(chans, rows // 2, 2, cols // 2, 2, count)
    return split.transpose(0, 2, 4, 1, 3, 5).reshape(chans * 4, rows // 2, cols // 2, count)


def unsqueeze(field):
    chans, rows, cols, count = field.shape
    split = field.reshape(chans // 4, 2, 2, rows, cols, count)
    return split.transpose(0, 3, 1, 4, 2, 5).reshape(chans // 4, rows * 2, cols * 2, count)


def column(vector):
    return vector[:, None, None, None]


def pad_cols(value):
    return jnp.pad(value, ((0, 0), (0, 0), (1, 1), (0, 0)))


def patches(padded, sign):
    rows = padded.shape[1] - 2
    cols = padded.shape[2] - 2
    return jnp.concatenate(
        [
            padded[:, 1 + sign * dy : 1 + sign * dy + rows, 1 + sign * dx : 1 + sign * dx + cols]
            for dy in (-1, 0, 1)
            for dx in (-1, 0, 1)
        ],
        axis=0,
    )


def tap_sum(taps, sign):
    rows, cols = (taps.shape[2], taps.shape[3])
    padded = jnp.pad(taps, ((0, 0), (0, 0), (2, 2), (1, 1), (0, 0)))
    total = jnp.zeros(taps.shape[1:2] + (rows + 2, cols) + taps.shape[4:], jnp.float32)
    for dy in (-1, 0, 1):
        for dx in (-1, 0, 1):
            index = (dy + 1) * 3 + dx + 1
            total = (
                total
                + padded[
                    index,
                    :,
                    1 + sign * dy : 1 + sign * dy + rows + 2,
                    1 + sign * dx : 1 + sign * dx + cols,
                ]
            )
    return total


def row_halo(value):
    value = padded_2(value, (("band", 1),), 1)
    return pad_cols(value)


def fold_rims(extended):
    inner = extended[:, 1:-1]
    edges = jnp.stack([extended[:, 0], extended[:, -1]], axis=1)
    got = padded_2(edges.astype(jnp.bfloat16), (("band", 1),), 1).astype(edges.dtype)
    inner = inner.at[:, 0].add(got[:, 0])
    inner = inner.at[:, -1].add(got[:, 3])
    return inner


def head_terms(field, gains, parts):
    shifted = (field + column(gains[0])) * column(jnp.exp(gains[1]))
    mixed = jnp.einsum("oc,crwb->orwb", lu_matrix(parts), shifted, precision=HIGH)
    area = field.shape[1] * field.shape[2]
    logdet = (
        (jnp.sum(gains[1]) + jnp.sum(jnp.diagonal(parts)))
        * area
        * jnp.ones((field.shape[3],), jnp.float32)
    )
    half = field.shape[0] // 2
    return (mixed[:half], mixed[half:], logdet)


def coupling(passive, network):
    half = passive.shape[0]
    raw = network[half:] + 2.0
    moved = (passive + network[:half]) * jax.nn.sigmoid(raw)
    return (moved, jnp.sum(jax.nn.log_sigmoid(raw), axis=(0, 1, 2)))


def prior_terms(padded_first, second, weight, table, onehot):
    first = padded_first[:, 1:-1, 1:-1]
    chans = second.shape[0]
    flat = weight.transpose(1, 0, 2).reshape(weight.shape[1], -1)
    cls = jnp.dot(onehot, table, precision=HIGH)
    stats = jnp.einsum("ok,krwb->orwb", flat, patches(padded_first, 1), precision=HIGH)
    stats = stats + cls[:, : 2 * chans].T[:, None, None, :]
    top = cls[:, 2 * chans :].T[:, None, None, :]
    logp = gauss(second, stats[:chans], stats[chans:]) + gauss(first, top[:chans], top[chans:])
    return jnp.sum(logp, axis=(0, 1, 2))


def silu_grad(value):
    sig = jax.nn.sigmoid(value)
    return sig * (1.0 + value * (1.0 - sig))


def adamw(weight, first, second, grad):
    first_new = BETA_ONE * first + (1.0 - BETA_ONE) * grad
    second_new = BETA_TWO * second + (1.0 - BETA_TWO) * grad * grad
    first_hat = first_new / (1.0 - BETA_ONE**STEP)
    second_hat = second_new / (1.0 - BETA_TWO**STEP)
    return (
        weight - RATE * (first_hat / (jnp.sqrt(second_hat) + EPSILON) + DECAY * weight),
        first_new,
        second_new,
    )


def body(
    images,
    noise,
    labels,
    conv_in,
    mixer,
    conv_out,
    prior_conv,
    hidden_bias,
    step_gains,
    lu_parts,
    class_table,
    first_conv_in,
    first_mixer,
    first_conv_out,
    first_prior,
    first_hidden_bias,
    first_gains,
    first_lu,
    first_table,
    second_conv_in,
    second_mixer,
    second_conv_out,
    second_prior,
    second_hidden_bias,
    second_gains,
    second_lu,
    second_table,
):
    field = images + noise
    classes = class_table.shape[0]
    dims = field.shape[0] * field.shape[2] * field.shape[2]
    hits = labels[:, None] == jnp.arange(classes, dtype=jnp.int32)[None, :]
    counts = lax.psum(jnp.sum(hits.astype(jnp.int32), axis=0), "dp")
    present = jnp.maximum(counts, 1).astype(jnp.float32)
    onehot = hits.astype(jnp.float32)
    coef_all = jnp.sum(onehot / (classes * present * dims * LOG_TWO)[None, :], axis=1)
    (active, passive, logdet_head), head_back = jax.vjp(
        lambda gains, parts: head_terms(field, gains, parts), step_gains, lu_parts
    )
    hidden = mixer.shape[0]
    chans = active.shape[0]
    shape = active.shape
    pixels = shape[1] * shape[2] * shape[3]
    in_flat = conv_in.transpose(1, 0, 2).reshape(hidden, -1).astype(jnp.bfloat16)
    out_flat = conv_out.reshape(-1, hidden).astype(jnp.bfloat16)
    mix_low = mixer.astype(jnp.bfloat16)
    in_taps = patches(row_halo(active.astype(jnp.bfloat16)), 1).reshape(-1, pixels)
    pre_one = (
        jnp.dot(in_flat, in_taps, preferred_element_type=jnp.float32) + hidden_bias[0][:, None]
    )
    act_one = jax.nn.silu(pre_one).astype(jnp.bfloat16)
    pre_two = (
        jnp.dot(mix_low, act_one, preferred_element_type=jnp.float32) + hidden_bias[1][:, None]
    )
    act_two = jax.nn.silu(pre_two).astype(jnp.bfloat16)
    taps_out = jnp.dot(out_flat, act_two, preferred_element_type=jnp.float32)
    taps_out = taps_out.reshape((9, conv_out.shape[1]) + shape[1:])
    network = fold_rims(tap_sum(taps_out, 1)) + column(step_gains[2])
    (moved, logdet_coup), coup_back = jax.vjp(coupling, passive, network)
    squeezed = squeeze(jnp.concatenate([active, moved], axis=0))
    half = squeezed.shape[0] // 2
    padded = pad_cols(
        padded_2(squeezed[:half].astype(jnp.bfloat16), (("band", 1),), 1).astype(jnp.float32)
    )
    prior_hot, coef_prior = (onehot, coef_all)
    logp, prior_back = jax.vjp(
        lambda first, second, weight, table: prior_terms(first, second, weight, table, prior_hot),
        padded,
        squeezed[half:],
        prior_conv,
        class_table,
    )
    d_padded, d_second, d_prior, d_table = prior_back(-coef_prior)
    d_first = d_padded[:, 1:-1, 1:-1]
    edges = jnp.stack([d_padded[:, 0, 1:-1], d_padded[:, -1, 1:-1]], axis=1)
    got = padded_2(shortened(edges), (("band", 1),), 1).astype(edges.dtype)
    d_first = d_first.at[:, 0].add(got[:, 0])
    d_first = d_first.at[:, -1].add(got[:, 3])
    d_whole = jnp.concatenate([d_first, d_second], axis=0)
    d_field = unsqueeze(d_whole)
    loss_part = -(jnp.sum(coef_all * (logdet_head + logdet_coup)) + jnp.sum(coef_prior * logp))
    d_passive, d_network = coup_back((d_field[chans:], -coef_all))
    grad_net = d_network.astype(jnp.bfloat16)
    d_out_bias = jnp.sum(grad_net.astype(jnp.float32), axis=(1, 2, 3))
    grad_taps = patches(row_halo(grad_net), -1).reshape(-1, pixels)
    d_conv_out = dot_nt(grad_taps, act_two).reshape(conv_out.shape)
    d_act_two = dot_tn(out_flat, grad_taps)
    grad_two = (d_act_two * silu_grad(pre_two)).astype(jnp.bfloat16)
    d_mixer = dot_nt(grad_two, act_one)
    d_act_one = dot_tn(mix_low, grad_two)
    grad_one = (d_act_one * silu_grad(pre_one)).astype(jnp.bfloat16)
    d_conv_in = dot_nt(grad_one, in_taps).reshape(hidden, 9, -1).transpose(1, 0, 2)
    d_hidden_bias = jnp.stack(
        [
            jnp.sum(grad_one.astype(jnp.float32), axis=1),
            jnp.sum(grad_two.astype(jnp.float32), axis=1),
        ]
    )
    back_taps = dot_tn(in_flat, grad_one).reshape((9, chans) + shape[1:])
    d_active = fold_rims(tap_sum(back_taps, -1)) + d_field[:chans]
    d_gains, d_lu = head_back((d_active, d_passive, -coef_all))
    d_gains = d_gains.at[2].add(d_out_bias)
    summed = lax.psum(
        (d_conv_in, d_mixer, d_conv_out, d_prior, d_hidden_bias, d_gains, d_lu, d_table, loss_part),
        ("dp", "band"),
    )
    grads = tuple(summed[:8])
    loss_sum = summed[8]
    loss = loss_sum + jnp.sum(BITS * counts.astype(jnp.float32) / present) / classes
    squares = sum((jnp.sum(grad * grad) for grad in grads))
    grad_norm = jnp.sqrt(squares)
    factor = jnp.minimum(1.0, CLIP_NORM / (grad_norm + 1e-06))
    params = (conv_in, mixer, conv_out, prior_conv, hidden_bias, step_gains, lu_parts, class_table)
    firsts = (
        first_conv_in,
        first_mixer,
        first_conv_out,
        first_prior,
        first_hidden_bias,
        first_gains,
        first_lu,
        first_table,
    )
    seconds = (
        second_conv_in,
        second_mixer,
        second_conv_out,
        second_prior,
        second_hidden_bias,
        second_gains,
        second_lu,
        second_table,
    )
    results = [adamw(w, m, v, factor * g) for w, m, v, g in zip(params, firsts, seconds, grads)]
    return (
        (loss, grad_norm)
        + tuple((r[0] for r in results))
        + tuple((r[1] for r in results))
        + tuple((r[2] for r in results))
    )


def solution(mesh):
    placed = (
        P(None, "band", None, "dp"),
        P(None, "band", None, "dp"),
        P("dp"),
        P(),
        P(),
        P(),
        P(),
        P(),
        P(),
        P(),
        P(),
        P(),
        P(),
        P(),
        P(),
        P(),
        P(),
        P(),
        P(),
        P(),
        P(),
        P(),
        P(),
        P(),
        P(),
        P(),
        P(),
    )
    return jax.shard_map(
        body,
        mesh=mesh,
        in_specs=placed,
        out_specs=(
            P(),
            P(),
            P(),
            P(),
            P(),
            P(),
            P(),
            P(),
            P(),
            P(),
            P(),
            P(),
            P(),
            P(),
            P(),
            P(),
            P(),
            P(),
            P(),
            P(),
            P(),
            P(),
            P(),
            P(),
            P(),
            P(),
        ),
        check_vma=False,
    )
```

profile of v0, /device:TPU:0, one launch (start us, length us, event | category | flops | bytes accessed | tf_op | source)
XLA Modules:
  0.0 519.5 jit_solution(2969736584277975417)
XLA Ops:
  12.2 3.3 fusion.39
  16.6 4.9 collective-permute-start
  24.8 8.4 %psum.70 = s32[10]{0:T(128)S(1)} all-reduce(s32[10]{0:T(128)S(1)} %convert_reduce_fusion.3), channel_id=1, replica_groups=mesh['dp'=8,'band'=4] {'dp'}, use_global_device_ids=true, to_apply=%region_1.0 | all-reduce | flops 10 | bytes 80 | tf_op jit(solution)/shard_map/psum | solution.py:220
  37.5 10.6 %concatenate.72 = bf16[54,4,16,256]{3,0,2,1:T(8,128)(2,1)S(1)} concatenate(bf16[6,4,16,256]{3,0,2,1:T(8,128)(2,1)S(1)} %get-tuple-element.333, bf16[6,4,16,256]{3,0,2,1:T(8,128)(2,1)S(1)} %get-tuple-element.299, bf16[6,4,16,256]{3,0,2,1:T(8,128)(2,1)S(1)} %get-tuple-element.334, bf16[6,4,16,256]{3,0,2,1:T(8,128)(2,1)S(1)} %get-tuple-element.335, ...), dimensions={0} | concatenate | bytes 3538944 | tf_op jit(solution)/shard_map/concatenate | solution.py:95
  51.1 19.3 %fusion.11 = (bf16[512,16384]{0,1:T(8,128)(2,1)}, f32[16384,512]{1,0:T(8,128)}) fusion(f32[512]{0:T(512)S(1)} %bitcast.216, bf16[54,16384]{1,0:T(8,128)(2,1)S(1)} %bitcast.211, bf16[512,54]{0,1:T(8,128)(2,1)S(1)} %copy-done.28), kind=kOutput, calls=%fused_computation.30 | convolution fusion | flops 956301312 | bytes 52158464 | tf_op jit(solution)/shard_map/dot_general | solution.py:236
  70.4 39.5 %fusion.5 = (bf16[512,16384]{0,1:T(8,128)(2,1)}, f32[16384,512]{1,0:T(8,128)}) fusion(f32[512]{0:T(512)S(1)} %bitcast.218, bf16[512,16384]{0,1:T(8,128)(2,1)} %get-tuple-element.323, f32[512,512]{1,0:T(8,128)S(1)} %copy-done.15), kind=kOutput, calls=%fused_computation.21 | convolution fusion | flops 8640528384 | bytes 68159488 | tf_op jit(solution)/shard_map/dot_general | solution.py:240
  109.9 11.0 %fusion.155 = f32[16384,108]{0,1:T(8,128)S(1)} fusion(bf16[512,16384]{0,1:T(8,128)(2,1)} %get-tuple-element.325, bf16[108,512]{1,0:T(8,128)(2,1)S(1)} %convert_element_type.104), kind=kOutput, calls=%fused_computation.308 | convolution fusion | flops 1811939328 | bytes 23965696 | tf_op jit(solution)/shard_map/dot_general | solution.py:243
  120.9 2.2 copy.174
  124.0 6.3 %copy.138 = f32[9,12,4,16,256]{4,1,3,2,0:T(8,128)S(1)} copy(f32[9,12,4,16,256]{4,3,2,1,0:T(8,128)S(1)} %bitcast.198) | data formatting | bytes 14155776 | tf_op jit(solution)/shard_map/reshape | solution.py:244
  131.5 4.7 collective-permute-start.2
  138.7 4.4 collective-permute-done.3
  145.1 3.5 collective-permute-start.4
  152.3 3.5 dot_general.88
  158.6 2.5 fusion.28
  162.1 2.9 convolution_bitcast_fusion
  165.1 3.5 fusion.68
  169.4 4.5 collective-permute-start.6
  176.1 4.3 collective-permute-done.7
  182.2 2.6 fusion.125
  185.6 3.5 collective-permute-start.8
  189.1 1.5 collective-permute-start.9
  191.6 4.4 collective-permute-done.9
  198.5 39.8 %concatenate.82 = bf16[108,4,16,256]{3,0,2,1:T(8,128)(2,1)} concatenate(bf16[12,4,16,256]{3,0,2,1:T(8,128)(2,1)} %get-tuple-element.279, bf16[12,4,16,256]{3,0,2,1:T(8,128)(2,1)} %get-tuple-element.285, bf16[12,4,16,256]{3,0,2,1:T(8,128)(2,1)} %get-tuple-element.278, bf16[12,4,16,256]{3,0,2,1:T(8,128)(2,1)S(1)} %get-tuple-element.277, ...), dimensions={0} | concatenate | bytes 7077888 | tf_op jit(solution)/shard_map/concatenate | solution.py:95
  238.3 3.3 copy.144
  241.5 3.9 dot_general.91
  245.4 10.5 %fusion.14 = f32[9,12,512]{2,1,0:T(8,128)} fusion(bf16[9,12,16384]{2,1,0:T(8,128)(2,1)} %dot_general.91, bf16[512,16384]{0,1:T(8,128)(2,1)} %get-tuple-element.325), kind=kOutput, calls=%fused_computation.44 | convolution fusion | flops 1811939328 | bytes 20537344 | tf_op jit(solution)/shard_map/dot_general | solution.py:48
  256.2 2.5 copy.175
  258.7 21.8 %convert_reduce_fusion = (f32[512]{0:T(512)S(1)}, bf16[512,16384]{0,1:T(8,128)(2,1)}) fusion(f32[16384,512]{1,0:T(8,128)} %get-tuple-element.326, f32[512]{0:T(512)S(1)} %bitcast.219, bf16[108,16384]{1,0:T(8,128)(2,1)S(1)} %bitcast.206, bf16[108,512]{1,0:T(8,128)(2,1)S(1)} %copy-done.23), kind=kOutput, calls=%fused_computation.33 | convolution fusion | flops 1912602112 | bytes 53985280 | tf_op jit(solution)/shard_map/dot_general | solution.py:54
  280.5 18.3 %fusion.156 = f32[512,512]{1,0:T(8,128)} fusion(bf16[512,16384]{0,1:T(8,128)(2,1)} %get-tuple-element.330, bf16[512,16384]{0,1:T(8,128)(2,1)} %get-tuple-element.323), kind=kOutput, calls=%fused_computation.309 | convolution fusion | flops 8589934592 | bytes 34603008 | tf_op jit(solution)/shard_map/dot_general | solution.py:48
  298.9 29.5 %convert_reduce_fusion.1 = (f32[512]{0:T(512)S(1)}, bf16[512,16384]{0,1:T(8,128)(2,1)}) fusion(f32[16384,512]{1,0:T(8,128)} %get-tuple-element.324, f32[512]{0:T(512)S(1)} %bitcast.217, bf16[512,16384]{0,1:T(8,128)(2,1)} %get-tuple-element.330, f32[512,512]{1,0:T(8,128)S(1)} %copy-done.16), kind=kOutput, calls=%fused_computation.34 | convolution fusion | flops 8690860032 | bytes 68161536 | tf_op jit(solution)/shard_map/dot_general | solution.py:54
  328.4 12.8 %fusion.157 = f32[16384,54]{0,1:T(8,128)} fusion(bf16[512,16384]{0,1:T(8,128)(2,1)} %get-tuple-element.332, bf16[512,54]{0,1:T(8,128)(2,1)S(1)} %copy-done.29), kind=kOutput, calls=%fused_computation.310 | convolution fusion | flops 905969664 | bytes 20371456 | tf_op jit(solution)/shard_map/dot_general | solution.py:54
  341.2 3.7 fusion.29
  344.9 3.1 copy.176
  348.3 3.2 copy.152
  351.8 2.7 collective-permute-start.10
  354.5 1.5 collective-permute-start.11
  356.7 4.1 collective-permute-done.11
  363.9 3.1 convolution_bitcast_fusion.2
  366.9 3.3 multiply_reduce_fusion.1
  378.8 2.2 scatter_fusion
  382.5 40.4 %all-reduce.29 = (f32[]{:T(128)}, f32[9,48,24]{1,2,0:T(8,128)S(1)}, f32[2,512]{1,0:T(2,128)S(1)}, f32[3,12]{1,0:T(4,128)S(1)}, f32[12,12]{1,0:T(8,128)S(1)}, /*index=5*/f32[10,96]{1,0:T(8,128)S(1)}) all-reduce(f32[]{:T(128)S(6)} %neg.53, f32[9,48,24]{1,2,0:T(8,128)} %bitcast.214, ...), channel_id=1, replica_groups=mesh['dp'=8,'band'=4] {'dp','band'}, use_global_device_ids=true, to_apply=%region_9.11 | all-reduce | flops 12533 | bytes 100264 | tf_op jit(solution)/shard_map/psum | solution.py:290
  426.6 61.2 %all-reduce.33.cloned.1.call-done = (f32[9,512,6]{1,2,0:T(8,128)}, f32[512,512]{1,0:T(8,128)}, f32[9,12,512]{2,1,0:T(8,128)}) async-done(((f32[9,512,6]{1,2,0:T(8,128)}, f32[512,512]{1,0:T(8,128)}, f32[9,12,512]{2,1,0:T(8,128)}), (f32[9,512,6]{1,2,0:T(8,128)}, f32[512,512]{1,0:T(8,128)}, f32[9,12,512]{2,1,0:T(8,128)})) %all-reduce.33.cloned.1.call-update) | async-done | bytes 1380368 | tf_op jit(solution)/shard_map/psum | solution.py:290
  487.8 2.2 multiply_reduce_fusion.2
  490.0 1.6 multiply_reduce_fusion.6
  491.5 1.6 multiply_reduce_fusion.5
  501.7 1.8 multiply_subtract_fusion.3
  503.5 2.3 multiply_subtract_fusion.1
  505.8 3.5 multiply_subtract_fusion
  (256 shorter events, 56.8 us)
Async XLA Ops:
  7.2 16.6 %copy-start.47 = (s32[256]{0:T(256)S(1)}, s32[256]{0:T(256)}, u32[]{:S(2)}) copy-start(s32[256]{0:T(256)} %param.44) | copy-start | bytes 3076
  7.2 16.7 %copy-start.38 = (f32[10,96]{1,0:T(8,128)S(1)}, f32[10,96]{1,0:T(8,128)}, u32[]{:S(2)}) copy-start(f32[10,96]{1,0:T(8,128)} %param.52) | copy-start | bytes 11524
  7.2 17.6 %copy-start.44 = (f32[2,512]{1,0:T(2,128)S(1)}, f32[2,512]{1,0:T(2,128)}, u32[]{:S(2)}) copy-start(f32[2,512]{1,0:T(2,128)} %param.49) | copy-start | bytes 12292
  7.2 29.1 %copy-start.13 = (f32[9,12,512]{2,1,0:T(8,128)S(1)}, f32[9,12,512]{2,1,0:T(8,128)}, u32[]{:S(2)}) copy-start(f32[9,12,512]{2,1,0:T(8,128)} %param.47) | copy-start | bytes 663556
  7.2 480.5 %all-reduce.33.cloned.1.call-start = ((), (), s32[]{:S(2)}) async-start(), calls=%async_computation | async-start | bytes 2981888 | tf_op jit(solution)/shard_map/psum | solution.py:290
  8.1 15.6 %copy-start.30 = (f32[12,12]{0,1:T(8,128)}, f32[12,12]{0,1:T(8,128)S(1)}, u32[]{:S(2)}) copy-start(f32[12,12]{0,1:T(8,128)S(1)} %copy.133) | copy-start | bytes 1732
  10.9 12.8 %copy-start.37 = (f32[12,12]{1,0:T(8,128)}, f32[12,12]{1,0:T(8,128)S(1)}, u32[]{:S(2)}) copy-start(f32[12,12]{1,0:T(8,128)S(1)} %rev.6) | copy-start | bytes 1732
  16.6 19.9 %collective-permute-start = (bf16[6,1,16,256]{3,0,2,1:T(8,128)(2,1)S(1)}, bf16[6,1,16,256]{3,0,2,1:T(8,128)(2,1)S(1)}, u32[]{:S(2)}, u32[]{:S(2)}) collective-permute-start(bf16[6,1,16,256]{3,0,2,1:T(8,128)(2,1)S(1)} %get-tuple-element.300), channel_id=1, source_target_pairs={{0,1},{1,2},{2,3},{4,5},{5,6},{6,7},{8,9},{9,10},{10,11},{12,13},{... | collective-permute-start | bytes 147464 | tf_op jit(solution)/shard_map/ppermute | solution.py:30
  21.5 14.9 %collective-permute-start.1 = (bf16[6,1,16,256]{3,0,2,1:T(8,128)(2,1)S(1)}, bf16[6,1,16,256]{3,0,2,1:T(8,128)(2,1)S(1)}, u32[]{:S(2)}, u32[]{:S(2)}) collective-permute-start(bf16[6,1,16,256]{3,0,2,1:T(8,128)(2,1)S(1)} %get-tuple-element.301), channel_id=1, source_target_pairs={{1,0},{2,1},{3,2},{5,4},{6,5},{7,6},{9,8},{10,9},{11,10},{13,12},{... | collective-permute-start | bytes 147464 | tf_op jit(solution)/shard_map/ppermute | solution.py:32
  24.8 26.2 %copy-start.65 = (f32[1,512]{1,0:T(1,128)}, f32[1,512]{1,0:T(1,128)S(1)}, u32[]{:S(2)}) copy-start(f32[1,512]{1,0:T(1,128)S(1)} %get-tuple-element.310) | copy-start | bytes 6148
  36.4 73.5 %copy-start.22 = (bf16[108,512]{1,0:T(8,128)(2,1)}, bf16[108,512]{1,0:T(8,128)(2,1)S(1)}, u32[]{:S(2)}) copy-start(bf16[108,512]{1,0:T(8,128)(2,1)S(1)} %convert_element_type.104) | copy-start | bytes 331780
  51.1 19.3 %copy-start.15 = (f32[512,512]{1,0:T(8,128)S(1)}, f32[512,512]{1,0:T(8,128)}, u32[]{:S(2)}) copy-start(f32[512,512]{1,0:T(8,128)} %param.46) | copy-start | bytes 3145732
  131.5 7.2 %collective-permute-start.2 = (bf16[12,1,16,256]{3,0,2,1:T(8,128)(2,1)S(1)}, bf16[12,1,16,256]{3,0,2,1:T(8,128)(2,1)S(1)}, u32[]{:S(2)}, u32[]{:S(2)}) collective-permute-start(bf16[12,1,16,256]{3,0,2,1:T(8,128)(2,1)S(1)} %get-tuple-element.282), channel_id=1, source_target_pairs={{0,1},{1,2},{2,3},{4,5},{5,6},{6,7},{8,9},{9,10},{10,11},{12,13},{... | collective-permute-start | bytes 294920 | tf_op jit(solution)/shard_map/ppermute | solution.py:30
  136.2 6.9 %collective-permute-start.3 = (bf16[12,1,16,256]{3,0,2,1:T(8,128)(2,1)S(1)}, bf16[12,1,16,256]{3,0,2,1:T(8,128)(2,1)S(1)}, u32[]{:S(2)}, u32[]{:S(2)}) collective-permute-start(bf16[12,1,16,256]{3,0,2,1:T(8,128)(2,1)S(1)} %get-tuple-element.283), channel_id=1, source_target_pairs={{1,0},{2,1},{3,2},{5,4},{6,5},{7,6},{9,8},{10,9},{11,10},{13,12},{... | collective-permute-start | bytes 294920 | tf_op jit(solution)/shard_map/ppermute | solution.py:32
  145.1 12.5 %collective-permute-start.4 = (bf16[24,1,8,256]{3,0,2,1:T(8,128)(2,1)S(1)}, bf16[24,1,8,256]{3,0,2,1:T(8,128)(2,1)S(1)}, u32[]{:S(2)}, u32[]{:S(2)}) collective-permute-start(bf16[24,1,8,256]{3,0,2,1:T(8,128)(2,1)S(1)} %get-tuple-element.302), channel_id=1, source_target_pairs={{0,1},{1,2},{2,3},{4,5},{5,6},{6,7},{8,9},{9,10},{10,11},{12,13},{... | collective-permute-start | bytes 294920 | tf_op jit(solution)/shard_map/ppermute | solution.py:30
  148.6 9.0 %collective-permute-start.5 = (bf16[24,1,8,256]{3,0,2,1:T(8,128)(2,1)S(1)}, bf16[24,1,8,256]{3,0,2,1:T(8,128)(2,1)S(1)}, u32[]{:S(2)}, u32[]{:S(2)}) collective-permute-start(bf16[24,1,8,256]{3,0,2,1:T(8,128)(2,1)S(1)} %get-tuple-element.303), channel_id=1, source_target_pairs={{1,0},{2,1},{3,2},{5,4},{6,5},{7,6},{9,8},{10,9},{11,10},{13,12},{... | collective-permute-start | bytes 294920 | tf_op jit(solution)/shard_map/ppermute | solution.py:32
  169.4 12.8 %copy-start.42 = (f32[256]{0:T(256)S(1)}, f32[256]{0:T(256)}, u32[]{:S(2)}) copy-start(f32[256]{0:T(256)} %copy-done.41) | copy-start | bytes 3076
  169.4 6.7 %collective-permute-start.6 = (bf16[24,1,8,256]{3,0,2,1:T(8,128)(2,1)S(1)}, bf16[24,1,8,256]{3,0,2,1:T(8,128)(2,1)S(1)}, u32[]{:S(2)}, u32[]{:S(2)}) collective-permute-start(bf16[24,1,8,256]{3,0,2,1:T(8,128)(2,1)S(1)} %get-tuple-element.288), channel_id=1, source_target_pairs={{0,1},{1,2},{2,3},{4,5},{5,6},{6,7},{8,9},{9,10},{10,11},{12,13},{... | collective-permute-start | bytes 294920 | tf_op jit(solution)/shard_map/ppermute | solution.py:30
  173.9 6.5 %collective-permute-start.7 = (bf16[24,1,8,256]{3,0,2,1:T(8,128)(2,1)S(1)}, bf16[24,1,8,256]{3,0,2,1:T(8,128)(2,1)S(1)}, u32[]{:S(2)}, u32[]{:S(2)}) collective-permute-start(bf16[24,1,8,256]{3,0,2,1:T(8,128)(2,1)S(1)} %get-tuple-element.289), channel_id=1, source_target_pairs={{1,0},{2,1},{3,2},{5,4},{6,5},{7,6},{9,8},{10,9},{11,10},{13,12},{... | collective-permute-start | bytes 294920 | tf_op jit(solution)/shard_map/ppermute | solution.py:32
  184.7 12.6 %copy-start.6 = (f32[6,4,16,256]{3,0,2,1:T(8,128)}, f32[6,4,16,256]{3,0,2,1:T(8,128)S(1)}, u32[]{:S(2)}) copy-start(f32[6,4,16,256]{3,0,2,1:T(8,128)S(1)} %get-tuple-element.264) | copy-start | bytes 1179652
  185.6 6.0 %collective-permute-start.8 = (bf16[12,1,16,256]{3,0,2,1:T(8,128)(2,1)S(1)}, bf16[12,1,16,256]{3,0,2,1:T(8,128)(2,1)S(1)}, u32[]{:S(2)}, u32[]{:S(2)}) collective-permute-start(bf16[12,1,16,256]{3,0,2,1:T(8,128)(2,1)S(1)} %get-tuple-element.286), channel_id=1, source_target_pairs={{0,1},{1,2},{2,3},{4,5},{5,6},{6,7},{8,9},{9,10},{10,11},{12,13},{... | collective-permute-start | bytes 294920 | tf_op jit(solution)/shard_map/ppermute | solution.py:30
  189.1 6.9 %collective-permute-start.9 = (bf16[12,1,16,256]{3,0,2,1:T(8,128)(2,1)S(1)}, bf16[12,1,16,256]{3,0,2,1:T(8,128)(2,1)S(1)}, u32[]{:S(2)}, u32[]{:S(2)}) collective-permute-start(bf16[12,1,16,256]{3,0,2,1:T(8,128)(2,1)S(1)} %get-tuple-element.287), channel_id=1, source_target_pairs={{1,0},{2,1},{3,2},{5,4},{6,5},{7,6},{9,8},{10,9},{11,10},{13,12},{... | collective-permute-start | bytes 294920 | tf_op jit(solution)/shard_map/ppermute | solution.py:32
  280.5 18.3 %copy-start.16 = (f32[512,512]{1,0:T(8,128)S(1)}, f32[512,512]{1,0:T(8,128)}, u32[]{:S(2)}) copy-start(f32[512,512]{1,0:T(8,128)} %param.46) | copy-start | bytes 3145732
  280.5 18.3 %copy-start.66 = (f32[1,512]{1,0:T(1,128)S(1)}, f32[1,512]{1,0:T(1,128)}, u32[]{:S(2)}) copy-start(f32[1,512]{1,0:T(1,128)} %copy-done.65) | copy-start | bytes 6148
  298.9 29.5 %copy-start.29 = (bf16[512,54]{0,1:T(8,128)(2,1)S(1)}, bf16[512,54]{0,1:T(8,128)(2,1)}, u32[]{:S(2)}) copy-start(bf16[512,54]{0,1:T(8,128)(2,1)} %convert_element_type.99) | copy-start | bytes 165892
  328.4 12.8 %copy-start.1 = (bf16[512,16384]{0,1:T(8,128)(2,1)S(1)}, bf16[512,16384]{0,1:T(8,128)(2,1)}, u32[]{:S(2)}) copy-start(bf16[512,16384]{0,1:T(8,128)(2,1)} %get-tuple-element.332) | copy-start | bytes 50331652
  328.4 12.8 %copy-start.12 = (bf16[9,6,16384]{2,1,0:T(8,128)(2,1)S(1)}, bf16[9,6,16384]{2,1,0:T(8,128)(2,1)}, u32[]{:S(2)}) copy-start(bf16[9,6,16384]{2,1,0:T(8,128)(2,1)} %dot_general.88) | copy-start | bytes 5308420
  351.5 12.2 %copy-start.4 = (f32[12,4,16,256]{3,2,1,0:T(8,128)S(1)}, f32[12,4,16,256]{3,2,1,0:T(8,128)}, u32[]{:S(2)}) copy-start(f32[12,4,16,256]{3,2,1,0:T(8,128)} %param.43) | copy-start | bytes 2359300
  351.8 4.8 collective-permute-start.10
  354.5 6.3 %collective-permute-start.11 = (bf16[6,1,16,256]{3,0,2,1:T(8,128)(2,1)S(1)}, bf16[6,1,16,256]{3,0,2,1:T(8,128)(2,1)}, u32[]{:S(2)}, u32[]{:S(2)}) collective-permute-start(bf16[6,1,16,256]{3,0,2,1:T(8,128)(2,1)S(1)} %get-tuple-element.297), channel_id=1, source_target_pairs={{1,0},{2,1},{3,2},{5,4},{6,5},{7,6},{9,8},{10,9},{11,10},{13,12},{... | collective-permute-start | bytes 147464 | tf_op jit(solution)/shard_map/ppermute | solution.py:32
  356.6 19.6 %copy-start.43 = (f32[256]{0:T(256)S(1)}, f32[256]{0:T(256)}, u32[]{:S(2)}) copy-start(f32[256]{0:T(256)} %copy-done.41) | copy-start | bytes 3076
  356.7 22.2 %copy-start.27 = (s32[24]{0:T(128)S(1)}, s32[24]{0:T(128)}, u32[]{:S(2)}) copy-start(s32[24]{0:T(128)} %fusion.116) | copy-start | bytes 292
  362.5 19.9 %copy-start.40 = (f32[10,96]{1,0:T(8,128)S(1)}, f32[10,96]{1,0:T(8,128)}, u32[]{:S(2)}) copy-start(f32[10,96]{1,0:T(8,128)} %fusion.90) | copy-start | bytes 11524
  362.6 19.9 %copy-start.46 = (f32[2,512]{1,0:T(2,128)S(1)}, f32[2,512]{1,0:T(2,128)}, u32[]{:S(2)}) copy-start(f32[2,512]{1,0:T(2,128)} %pad_maximum_fusion.15) | copy-start | bytes 12292
  363.7 134.7 %copy-start.39 = (f32[10,96]{1,0:T(8,128)S(1)}, f32[10,96]{1,0:T(8,128)}, u32[]{:S(2)}) copy-start(f32[10,96]{1,0:T(8,128)} %param.52) | copy-start | bytes 11524
  363.7 134.7 %copy-start.49 = (f32[10,96]{1,0:T(8,128)S(1)}, f32[10,96]{1,0:T(8,128)}, u32[]{:S(2)}) copy-start(f32[10,96]{1,0:T(8,128)} %param.60) | copy-start | bytes 11524
  363.7 134.7 %copy-start.50 = (f32[10,96]{1,0:T(8,128)S(1)}, f32[10,96]{1,0:T(8,128)}, u32[]{:S(2)}) copy-start(f32[10,96]{1,0:T(8,128)} %param.68) | copy-start | bytes 11524
  363.8 135.3 %copy-start = (f32[12,12]{1,0:T(8,128)S(1)}, f32[12,12]{1,0:T(8,128)}, u32[]{:S(2)}) copy-start(f32[12,12]{1,0:T(8,128)} %param.51) | copy-start | bytes 1732
  363.8 135.3 %copy-start.51 = (f32[12,12]{1,0:T(8,128)S(1)}, f32[12,12]{1,0:T(8,128)}, u32[]{:S(2)}) copy-start(f32[12,12]{1,0:T(8,128)} %param.59) | copy-start | bytes 1732
  363.8 135.3 %copy-start.52 = (f32[12,12]{1,0:T(8,128)S(1)}, f32[12,12]{1,0:T(8,128)}, u32[]{:S(2)}) copy-start(f32[12,12]{1,0:T(8,128)} %param.67) | copy-start | bytes 1732
  363.8 135.9 %copy-start.53 = (f32[3,12]{1,0:T(4,128)S(1)}, f32[3,12]{1,0:T(4,128)}, u32[]{:S(2)}) copy-start(f32[3,12]{1,0:T(4,128)} %param.50) | copy-start | bytes 436
  363.8 137.2 %copy-start.45 = (f32[2,512]{1,0:T(2,128)S(1)}, f32[2,512]{1,0:T(2,128)}, u32[]{:S(2)}) copy-start(f32[2,512]{1,0:T(2,128)} %param.49) | copy-start | bytes 12292
  363.8 137.2 %copy-start.60 = (f32[2,512]{1,0:T(2,128)S(1)}, f32[2,512]{1,0:T(2,128)}, u32[]{:S(2)}) copy-start(f32[2,512]{1,0:T(2,128)} %param.57) | copy-start | bytes 12292
  363.8 137.2 %copy-start.61 = (f32[2,512]{1,0:T(2,128)S(1)}, f32[2,512]{1,0:T(2,128)}, u32[]{:S(2)}) copy-start(f32[2,512]{1,0:T(2,128)} %param.65) | copy-start | bytes 12292
  363.8 139.7 %copy-start.14 = (f32[9,12,512]{2,1,0:T(8,128)S(1)}, f32[9,12,512]{2,1,0:T(8,128)}, u32[]{:S(2)}) copy-start(f32[9,12,512]{2,1,0:T(8,128)} %param.47) | copy-start | bytes 663556
  366.9 138.9 %copy-start.17 = (f32[512,512]{1,0:T(8,128)S(1)}, f32[512,512]{1,0:T(8,128)}, u32[]{:S(2)}) copy-start(f32[512,512]{1,0:T(8,128)} %param.46) | copy-start | bytes 3145732
  370.2 135.6 %copy-start.18 = (f32[512,512]{1,0:T(8,128)S(1)}, f32[512,512]{1,0:T(8,128)}, u32[]{:S(2)}) copy-start(f32[512,512]{1,0:T(8,128)} %param.54) | copy-start | bytes 3145732
  487.8 18.0 %copy-start.10 = (f32[512,512]{1,0:T(8,128)S(1)}, f32[512,512]{1,0:T(8,128)}, u32[]{:S(2)}) copy-start(f32[512,512]{1,0:T(8,128)} %get-tuple-element.217) | copy-start | bytes 3145732
  (32 other events, 171.9 us)
Sparse Core Ops, SparseCore 0:
  356.8 130.9 all-reduce.32
where the time goes:
time: 521 us; the launch traced here: 519 us
  matrix products  188 us (36%)
  local copies, waits for them, and re-layouts  97.9 us (19%)
  waiting for transfers between devices  80.5 us (15%)
  blocking collectives  48.7 us (9%)
  other arithmetic  44.4 us (9%)
  starting transfers between devices  31.9 us (6%)
  between operations  27.7 us (5%)
    dot_general x3, matrix products, dot_tn(): lax.dot_general(left, right, (((0,), (0,)), ((), ())), preferred_element_...  64.1 us
    psum x1, waiting for transfers between devices, body(): lax.psum((d_conv_in, d_mixer, d_conv_out, d_prior, d_hidden_bias, d_gains...  61.2 us
    concatenate x5, local copies, waits for them, and re-layouts, patches(): jnp.concatenate([padded[:, 1 + sign * dy:1 + sign * dy + rows, 1 + sign *...  54 us
    psum x1, blocking collectives, body(): lax.psum((d_conv_in, d_mixer, d_conv_out, d_prior, d_hidden_bias, d_gains...  40.4 us
    dot_general x1, matrix products, body(): jnp.dot(mix_low, act_one, preferred_element_type=jnp.float32)  39.5 us
    dot_general x3, matrix products, dot_nt(): lax.dot_general(left, right, (((1,), (1,)), ((), ())), preferred_element_...  32.5 us
    ppermute x6, starting transfers between devices, padded_2(): lax.ppermute(tail, axis, [(i, (i + 1) % count) for i in range(ends)])  23.8 us
    dot_general x1, matrix products, body(): jnp.dot(in_flat, in_taps, preferred_element_type=jnp.float32)  19.3 us
  transfers between devices with their start and end apart: 13, of which 8 were waited for; matrix products, arithmetic and copies ran while one was open for 7% of the time, Pallas kernels for 0%

commit v1 on v0

v1 whole, which is shorter than its diff:
```python
import functools
import math

import jax
import jax.numpy as jnp
from jax import lax
from jax.experimental import pallas as pl
from jax.experimental.pallas import tpu as pltpu
from jax.sharding import PartitionSpec as P

STEP = 10
HIGH = lax.Precision.HIGHEST
LOG_TWO = math.log(2.0)
LOG_TWO_PI = math.log(2.0 * math.pi)
CLIP_NORM = 0.01
RATE = 0.05
BETA_ONE = 0.9
BETA_TWO = 0.999
EPSILON = 1e-08
DECAY = 0.01
BITS = 5.0
F32 = jnp.float32
BF16 = jnp.bfloat16
MIB = 1024 * 1024
NN = (((1,), (0,)), ((), ()))
NT = (((1,), (1,)), ((), ()))
TN = (((0,), (0,)), ((), ()))

ROW_MIX = 0
ROW_OUT = 512
ROW_IN = ROW_OUT + 144
ROW_PRIOR = ROW_IN + 96
ROW_SMALL = ROW_PRIOR + 72
ROWS = ROW_SMALL + 24


def dot(left, right, dims=NN, precision=None):
    return lax.dot_general(left, right, dims, precision=precision, preferred_element_type=F32)


def iota(shape, dim):
    return lax.broadcasted_iota(jnp.int32, shape, dim)


def as_f32(mask):
    return jnp.where(mask, 1.0, 0.0).astype(F32)


def prior_out_map():
    row, col = iota((48, 64), 0), iota((48, 64), 1)
    kind, d, c = col >> 5, (col >> 3) & 3, col & 7
    return as_f32((c < 6) & (row == kind * 24 + 4 * c + d))


def prior_in_map():
    row, col = iota((288, 216), 0), iota((288, 216), 1)
    tap, d, c = row >> 5, (row >> 3) & 3, row & 7
    return as_f32((c < 6) & (col == tap * 24 + 4 * c + d))


def channel_map():
    row, col = iota((16, 128), 0), iota((16, 128), 1)
    return as_f32(((row < 6) & (col == 11 - row)) | ((row >= 8) & (row < 14) & (col == 13 - row)))


def half_map():
    row, col = iota((16, 128), 0), iota((16, 128), 1)
    return as_f32(((row < 6) & (col == row)) | ((row >= 8) & (row < 14) & (col == row - 2)))


def lu_factors(lu):
    row, col = iota((128, 128), 0), iota((128, 128), 1)
    eye = (row == col) & (row < 12)
    lower = jnp.where(row > col, lu, 0.0) + as_f32(eye)
    upper = jnp.where(row < col, lu, 0.0) + jnp.where(eye, jnp.exp(lu), 0.0)
    return lower, upper, eye


def spread_weight(lu, gains):
    lower, upper, _ = lu_factors(lu)
    weight = dot(channel_map(), dot(lower, upper, NN, HIGH), NN, HIGH)
    scaled = weight * jnp.exp(gains[1:2])
    shift = jnp.sum(scaled * gains[0:1], axis=1, keepdims=True)
    return jnp.where(iota((16, 128), 1) == 12, shift, scaled)


def weights_kernel(cin, mix, cout, prior, bias, gains, lu, table,
                   win, wt, mixh, mixth, bias2, wout, woutt, weff, wpt, wp, tablep,
                   big, square, strip):
    hidden = mix.shape[0]
    wt[...] = jnp.zeros_like(wt)
    for dy in range(3):
        for dx in range(3):
            wt[pl.ds(dy * 32 + dx * 8, 6), :] = (
                0.5 * cin[dy * 3 + dx]
            ).astype(BF16).astype(F32)
    half = 0.5 * bias[0:1, :]
    first = half.astype(BF16).astype(F32)
    rest = half - first
    second = rest.astype(BF16).astype(F32)
    wt[46:47, :] = first
    wt[38:39, :] = second
    wt[54:55, :] = rest - second
    win[...] = wt[...].T.astype(BF16)
    mixh[...] = (0.5 * mix[...]).astype(BF16)
    mixth[...] = (0.5 * mix[...]).T.astype(BF16)
    bias2[...] = jnp.broadcast_to(0.5 * bias[1:2, :], (128, hidden)).T
    big[...] = jnp.zeros_like(big)
    for tap in range(9):
        big[pl.ds(tap * 16, 6), :] = cout[tap, 0:6, :]
        big[pl.ds(tap * 16 + 8, 6), :] = cout[tap, 6:12, :]
    wout[...] = big[0:144, :].astype(BF16)
    woutt[...] = (0.5 * big[0:256, :]).T.astype(BF16)
    square[...] = jnp.zeros_like(square)
    square[0:12, 0:12] = lu[...]
    strip[...] = jnp.zeros_like(strip)
    strip[0:3, 0:12] = gains[...]
    weff[...] = spread_weight(square[...], strip[0:8, :])
    out_map = prior_out_map()
    flat = dot(prior_in_map(), dot(prior[...].reshape(216, 48), out_map, NN, HIGH), NN, HIGH)
    flat_hi = flat.astype(BF16)
    flat_lo = (flat - flat_hi.astype(F32)).astype(BF16)
    wpt[...] = jnp.zeros_like(wpt)
    wpt[:, 0:64] = flat_hi
    wpt[:, 64:128] = flat_lo
    wpt[:, 128:192] = flat_hi
    big[...] = jnp.zeros_like(big)
    big[0:288, 0:64] = flat_hi.astype(F32)
    big[0:288, 64:128] = flat_lo.astype(F32)
    wp[...] = big[0:384, 0:128].T.astype(BF16)
    tablep[...] = jnp.zeros_like(tablep)
    tablep[0:10, 0:64] = dot(table[:, 0:48], out_map, NN, HIGH)
    tablep[0:10, 64:128] = dot(table[:, 48:96], out_map, NN, HIGH)


def hidden_unit(u):
    wide = 1.0 + jnp.tanh(u)
    act = u * wide
    return act.astype(BF16), (wide + act * (2.0 - wide)).astype(BF16)


def forward_kernel(cols, sub, images, noise, top, bottom, flags, weff, win, mixh, bias2, wout,
                   act1, sg1, act2, sg2, xa2, xt, xaf, xbf, nn, edge_top, edge_bottom,
                   xs, taps, acc):
    step = pl.program_id(0)
    rows, width, count = images.shape[1:]
    groups = width // cols

    @pl.when(step == 0)
    def _():
        xs[:, 0:2] = top[...]
        xs[:, 2 : rows + 2] = images[...] + noise[...]
        xs[:, rows + 2 : rows + 4] = bottom[...]
        xaf[...] = jnp.zeros_like(xaf)
        xt[...] = jnp.zeros_like(xt)
        acc[...] = jnp.zeros_like(acc)
        row8 = iota((8, count), 0)
        ones = jnp.where((iota((16, count), 0) & 7) == 6, 1.0, 0.0)
        col_a = [jnp.broadcast_to(weff[0:8, c : c + 1], (8, count)) for c in range(13)]
        col_b = [jnp.broadcast_to(weff[8:16, c : c + 1], (8, count)) for c in range(13)]

        def per_row(er, carry):
            own = (er >= 2) & (er < rows + 2)
            valid = jnp.where(er < 2, flags[0], jnp.where(er >= rows + 2, flags[1], 1.0))
            inner = jnp.clip(er - 2, 0, rows - 1)
            for c in range(width):
                a, b = col_a[12], col_b[12]
                t0 = jnp.zeros((8, count), F32)
                t1 = jnp.where(row8 == 4, valid, 0.0)
                for ch in range(12):
                    x = jnp.broadcast_to(xs[ch, er, c : c + 1, :], (8, count))
                    a = a + col_a[ch] * x
                    b = b + col_b[ch] * x
                    if ch < 8:
                        t0 = jnp.where(row8 == ch, x, t0)
                    else:
                        t1 = jnp.where(row8 == ch - 8, x, t1)
                xaf[er, c + 2] = a * valid
                xt[er, c + 1] = jnp.concatenate([t0, t1], axis=0).astype(BF16)

                @pl.when(own)
                def _():
                    xbf[inner, c] = b

            for c in range(width + 2):
                pair = jnp.concatenate([xaf[er, c + 1], xaf[er, c + 2]], axis=0)
                xa2[er, c] = (pair + ones).astype(BF16)
            return carry

        lax.fori_loop(0, rows + 4, per_row, 0)

    row = step // groups
    start = (step % groups) * cols
    for i in range(cols):
        lanes = pl.ds(i * count, count)
        for dy in range(3):
            for j in range(2):
                taps[pl.ds((dy * 2 + j) * 16, 16), lanes] = xa2[row + 1 + dy, start + i + 2 * j]
        taps[96:112, lanes] = xt[row + 2, start + i + 1]
        taps[112:128, lanes] = xt[row + 2, start + i + 1]
    size = sub * count
    for s in range(cols // sub):
        lanes = pl.ds(s * size, size)
        one, slope1 = hidden_unit(dot(win[...], taps[:, lanes]))
        act1[0, :, lanes] = one
        sg1[0, :, lanes] = slope1
        bias = jnp.concatenate([bias2[...]] * (size // 128), axis=1)
        two, slope2 = hidden_unit(dot(mixh[...], one) + bias)
        act2[0, :, lanes] = two
        sg2[0, :, lanes] = slope2
        out = dot(wout[...], two)
        for i in range(sub):
            for dy in range(3):
                for dx in range(3):
                    r = row + 2 - dy
                    c = start + s * sub + i + 2 - dx
                    tap = dy * 3 + dx
                    acc[r, c] += out[tap * 16 : tap * 16 + 16, i * count : (i + 1) * count]

    @pl.when(step == rows * groups - 1)
    def _():
        nn[...] = acc[1 : rows + 1, 1 : width + 1]
        edge_top[...] = acc[0, 1 : width + 1].astype(BF16)
        edge_bottom[...] = acc[rows + 1, 1 : width + 1].astype(BF16)


def coupling_kernel(nn, edge_top, edge_bottom, xaf, xbf, xt, labels, counts, wp, wpt, tablep, weff_gains,
                    dn, dprior, small, taps_hi, taps_lo, stats, dstats, dtaps, dxa, dxb, total,
                    loss_acc, gain_acc, table_acc):
    rows, width, _, count = nn.shape
    half = width // 2
    classes = 10
    hot = as_f32(iota((16, count), 0) == jnp.broadcast_to(labels[...], (16, count)))
    present = jnp.maximum(counts[...], 1.0)
    dims = 12.0 * width * width
    scale16 = 1.0 / (classes * present * (dims * LOG_TWO))
    coef = jnp.sum(hot * scale16[:, 0:1], axis=0, keepdims=True)
    coef = jnp.broadcast_to(coef, (8, count))
    cls = dot(tablep[...], hot, TN, HIGH)
    dxa[...] = jnp.zeros_like(dxa)
    loss_acc[...] = jnp.zeros_like(loss_acc)
    gain_acc[...] = jnp.zeros_like(gain_acc)
    table_acc[...] = jnp.zeros_like(table_acc)
    dprior[...] = jnp.zeros_like(dprior)
    dstats[...] = jnp.zeros_like(dstats)
    keep = iota((8, count), 0) < 6
    net_bias = weff_gains[...]
    bias_a = jnp.broadcast_to(net_bias[0:8, 0:1], (8, count))
    bias_b = jnp.broadcast_to(net_bias[8:16, 0:1], (8, count))

    def per_row(r2, carry):
        for w in range(half):
            lanes = pl.ds(w * count, count)
            for ty in range(3):
                for tx in range(3):
                    for dy in range(2):
                        er, ec = 2 * r2 + 2 * ty + dy, 2 * w + 2 * tx
                        pair = jnp.concatenate([xaf[er, ec], xaf[er, ec + 1]], axis=0)
                        high = pair.astype(BF16)
                        at = pl.ds((ty * 3 + tx) * 32 + dy * 16, 16)
                        taps_hi[at, lanes] = high
                        taps_lo[at, lanes] = (pair - high.astype(F32)).astype(BF16)
        main = dot(wp[:, 0:288], taps_hi[...])
        stats[...] = main[0:64] + main[64:128] + dot(wp[0:64, 0:288], taps_lo[...])
        for w in range(half):
            lanes = pl.ds(w * count, count)
            for dy in range(2):
                for dx in range(2):
                    d = 2 * dy + dx
                    r, c = 2 * r2 + dy, 2 * w + dx
                    tile = nn[r, c]
                    shift = tile[0:8] + bias_a
                    raw = tile[8:16] + bias_b
                    sig = jax.nn.sigmoid(raw)
                    log_sig = jnp.minimum(raw, 0.0) - jnp.log(1.0 + jnp.exp(-jnp.abs(raw)))
                    base = xbf[r, c] + shift
                    second = base * sig
                    mean = stats[pl.ds(8 * d, 8), lanes] + cls[8 * d : 8 * d + 8]
                    logs = stats[pl.ds(32 + 8 * d, 8), lanes] + cls[32 + 8 * d : 40 + 8 * d]
                    diff = second - mean
                    weighted = diff * jnp.exp(-2.0 * logs)
                    quad = diff * weighted
                    first = xaf[r + 2, c + 2]
                    mean1 = cls[64 + 8 * d : 72 + 8 * d]
                    logs1 = cls[96 + 8 * d : 104 + 8 * d]
                    diff1 = first - mean1
                    weighted1 = diff1 * jnp.exp(-2.0 * logs1)
                    quad1 = diff1 * weighted1
                    value = log_sig - 0.5 * (
                        2.0 * LOG_TWO_PI + 2.0 * (logs + logs1) + quad + quad1
                    )
                    loss_acc[...] += jnp.where(keep, value, 0.0)
                    dv = coef * weighted
                    ds_ = coef - coef * quad
                    dv1 = coef * weighted1
                    table_acc[pl.ds(8 * d, 8), :] -= dv
                    table_acc[pl.ds(32 + 8 * d, 8), :] += ds_
                    table_acc[pl.ds(64 + 8 * d, 8), :] -= dv1
                    table_acc[pl.ds(96 + 8 * d, 8), :] += coef - coef * quad1
                    dstats[pl.ds(8 * d, 8), lanes] = -dv
                    dstats[pl.ds(32 + 8 * d, 8), lanes] = ds_
                    dxa[r + 2, c + 2] += dv1
                    passed = dv * sig
                    dxb[r, c] = passed
                    draw = (passed * base - coef) * (1.0 - sig)
                    net = jnp.concatenate([passed, draw], axis=0).astype(BF16)
                    dn[r, c] = net
                    gain_acc[...] += net.astype(F32)
        grads = dstats[0:64, :]
        high = grads.astype(BF16)
        low = (grads - high.astype(F32)).astype(BF16)
        dprior[:, 0:64] += (
            dot(taps_hi[...], high, NT) + dot(taps_hi[...], low, NT) + dot(taps_lo[...], high, NT)
        )
        stack = jnp.concatenate([high, high, low], axis=0)
        dtaps[...] = dot(wpt[:, 0:192], stack)
        for w in range(half):
            lanes = pl.ds(w * count, count)
            for ty in range(3):
                for tx in range(3):
                    for dy in range(2):
                        for dx in range(2):
                            k = (ty * 3 + tx) * 32 + dy * 16 + dx * 8
                            dxa[2 * r2 + 2 * ty + dy, 2 * w + 2 * tx + dx] += dtaps[pl.ds(k, 8), lanes]
        return carry

    lax.fori_loop(0, rows // 2, per_row, 0)

    total[...] = jnp.zeros_like(total)
    for er in range(rows + 4):
        field = xt[er, 1 : width + 1].reshape(width * 16, count)
        part_a = dxa[er, 2 : width + 2].reshape(width * 8, count)
        if 2 <= er < rows + 2:
            part_b = dxb[er - 2].reshape(width * 8, count)
            part = jnp.concatenate([part_a, part_b], axis=0)
        else:
            part = part_a
        size = part.shape[0]
        high = part.astype(BF16)
        low = (part - high.astype(F32)).astype(BF16)
        total[0:size, :] += dot(high, field, NT) + dot(low, field, NT)
    row, col = iota((256, 256), 0), iota((256, 256), 1)
    masked = jnp.where(((row & 127) >> 3) == (col >> 4), total[...], 0.0)
    gather = as_f32((iota((16, 256), 0) == ((iota((16, 256), 1) & 7) + 8 * (iota((16, 256), 1) >> 7))))
    fold = as_f32((iota((256, 128), 0) & 15) == iota((256, 128), 1))
    small[...] = jnp.zeros_like(small)
    small[8:24, 128:256] = dot(dot(gather, masked, NN, HIGH), fold, NN, HIGH)
    small[8:24, 0:128] = dot(hot, table_acc[...], NT, HIGH)
    lone = jnp.ones((8, count), F32)
    gain_row = dot(dot(lone, gain_acc[...], NT, HIGH), half_map(), NN, HIGH)
    small[8:16, 256:384] = gain_row
    value = jnp.sum(jnp.sum(loss_acc[...], axis=0, keepdims=True) * coef[0:1], axis=1, keepdims=True)
    small[16:24, 256:384] = jnp.broadcast_to(-value, (8, 128))


def backward_kernel(cols, sub, act1, sg1, act2, sg2, dn, dn_top, dn_bottom, xa2, xt, mixth, woutt, wt,
                    dprior, small, packed, dnp, taps, gtaps, bias_acc, wfield):
    step = pl.program_id(0)
    rows, width, _, count = dn.shape
    groups = width // cols

    @pl.when(step == 0)
    def _():
        packed[...] = jnp.zeros_like(packed)
        bias_acc[...] = jnp.zeros_like(bias_acc)
        wfield[...] = jnp.zeros_like(wfield)
        dnp[...] = jnp.zeros_like(dnp)
        dnp[0, 1 : width + 1] = dn_top[...]
        dnp[1 : rows + 1, 1 : width + 1] = dn[...]
        dnp[rows + 1, 1 : width + 1] = dn_bottom[...]
        taps[240:256, :] = jnp.zeros_like(taps[240:256, :])
        gtaps[144:256, :] = jnp.zeros_like(gtaps[144:256, :])

    row = step // groups
    start = (step % groups) * cols
    for i in range(cols):
        lanes = pl.ds(i * count, count)
        for dy in range(3):
            for j in range(2):
                taps[pl.ds((dy * 2 + j) * 16, 16), lanes] = xa2[row + 1 + dy, start + i + 2 * j]
            for dx in range(3):
                tap = dy * 3 + dx
                taps[pl.ds(96 + tap * 16, 16), lanes] = xt[row + 1 + dy, start + i + dx]
                gtaps[pl.ds(tap * 16, 16), lanes] = dnp[row + 2 - dy, start + i + 2 - dx]
    size = sub * count
    for s in range(cols // sub):
        lanes = pl.ds(s * size, size)
        grad2 = (dot(woutt[...], gtaps[:, lanes]) * sg2[0, :, lanes].astype(F32)).astype(BF16)
        grad1 = (dot(mixth[...], grad2) * sg1[0, :, lanes].astype(F32)).astype(BF16)
        wide = grad2.astype(F32)
        bias = wide[:, 0:128]
        for k in range(1, size // 128):
            bias = bias + wide[:, k * 128 : (k + 1) * 128]
        bias_acc[...] += bias
        packed[ROW_OUT:ROW_IN, :] += dot(gtaps[0:144, lanes], act2[0, :, lanes], NT)
        packed[ROW_MIX:ROW_OUT, :] += dot(grad2, act1[0, :, lanes], NT)
        gathered = dot(taps[0:240, lanes], grad1, NT)
        packed[ROW_IN:ROW_PRIOR, :] += gathered[0:96]
        wfield[...] += gathered[96:240]

    @pl.when(step == rows * groups - 1)
    def _():
        for k in range(4):
            packed[ROW_PRIOR:ROW_SMALL, 128 * k : 128 * k + 128] = dprior[72 * k : 72 * k + 72, :]
        packed[ROW_SMALL:ROWS, :] = small[...]
        lone = jnp.ones((8, 128), F32)
        packed[ROW_SMALL : ROW_SMALL + 8, :] = dot(lone, bias_acc[...], NT, HIGH)
        cross = dot(wt[0:96, :], wfield[...], NT, HIGH)
        row, col = iota((96, 144), 0), iota((96, 144), 1)
        slot = (row >> 3) & 3
        same = (slot < 3) & ((row >> 5) * 3 + slot == col >> 4) & ((row & 7) < 6)
        gather = as_f32(iota((8, 96), 0) == (iota((8, 96), 1) & 7))
        fold = as_f32((iota((144, 128), 0) & 15) == iota((144, 128), 1))
        field_terms = dot(dot(gather, jnp.where(same, cross, 0.0), NN, HIGH), fold, NN, HIGH)
        packed[ROW_SMALL + 8 : ROW_SMALL + 16, 128:256] += 2.0 * field_terms


def adamw(weight, first, second, grad, out, out_first, out_second, at=Ellipsis):
    first_new = BETA_ONE * first[at] + (1.0 - BETA_ONE) * grad
    second_new = BETA_TWO * second[at] + (1.0 - BETA_TWO) * grad * grad
    first_hat = first_new / (1.0 - BETA_ONE**STEP)
    second_hat = second_new / (1.0 - BETA_TWO**STEP)
    out[at] = weight[at] - RATE * (
        first_hat / (jnp.sqrt(second_hat) + EPSILON) + DECAY * weight[at]
    )
    out_first[at] = first_new
    out_second[at] = second_new


def update_kernel(area, dims, *refs):
    grads, counts = refs[:2]
    params, firsts, seconds = refs[2:10], refs[10:18], refs[18:26]
    loss, norm = refs[26:28]
    news, new_firsts, new_seconds = refs[28:36], refs[36:44], refs[44:52]
    square, strip, gin, gout, flat = refs[52:]
    bias, gains_ref, lu_ref = params[4:7]
    hidden = grads.shape[1]
    square[...] = jnp.zeros_like(square)
    square[0:12, 0:12] = lu_ref[...]
    strip[...] = jnp.zeros_like(strip)
    strip[0:3, 0:12] = gains_ref[...]
    gains = strip[...]
    lower, upper, eye = lu_factors(square[...])
    weight = spread_weight(square[...], gains)
    field = grads[ROW_SMALL + 8 : ROWS, 128:256]
    lane = iota((16, 128), 1)
    level = jnp.sum(jnp.where(lane == 12, field, 0.0), axis=1, keepdims=True)
    real = iota((16, 128), 0) & 7
    moved = jnp.where((lane < 12) & (real < 6), field + level * gains[0:1], 0.0)
    level = jnp.where(real < 6, level, 0.0)
    present = counts[...] / jnp.maximum(counts[...], 1.0)
    share = jnp.sum(present[:, 0:1], axis=0, keepdims=True)
    coef = share * (1.0 / (10.0 * dims * LOG_TWO)) * area
    weight = jnp.where(lane < 12, weight, 0.0)
    d_shift = jnp.sum(weight * level, axis=0, keepdims=True)
    d_scale = jnp.sum(weight * moved, axis=0, keepdims=True) - coef
    d_product = dot(channel_map(), moved * jnp.exp(gains[1:2]), TN, HIGH)
    d_lower = dot(d_product, upper, NT, HIGH)
    d_upper = dot(lower, d_product, TN, HIGH)
    row, col = iota((128, 128), 0), iota((128, 128), 1)
    d_lu = jnp.where(row > col, d_lower, 0.0) + jnp.where(row < col, d_upper, 0.0)
    d_lu = d_lu + jnp.where(eye, d_upper * jnp.exp(square[...]) - coef, 0.0)
    d_lu = jnp.where((row < 12) & (col < 12), d_lu, 0.0)
    diag = jnp.sum(jnp.sum(jnp.where(eye, square[...], 0.0), axis=0, keepdims=True), axis=1, keepdims=True)
    logs = jnp.sum(jnp.where(lane[0:1] < 12, gains[1:2], 0.0), axis=1, keepdims=True)
    d_bias_out = grads[ROW_SMALL + 8 : ROW_SMALL + 9, 256:384]
    row8 = iota((8, 128), 0)
    d_gains = jnp.where(row8 == 0, d_shift, jnp.where(row8 == 1, d_scale, jnp.where(row8 == 2, d_bias_out, 0.0)))
    d_gains = jnp.where(iota((8, 128), 1) < 12, d_gains, 0.0)
    for tap in range(9):
        dy, dx = tap // 3, tap % 3
        gin[tap] = grads[ROW_IN + dy * 32 + dx * 8 : ROW_IN + dy * 32 + dx * 8 + 6, :]
        at = ROW_OUT + tap * 16
        gout[tap, 0:6, :] = grads[at : at + 6, :]
        gout[tap, 6:12, :] = grads[at + 8 : at + 14, :]
    for k in range(4):
        flat[72 * k : 72 * k + 72, :] = grads[ROW_PRIOR:ROW_SMALL, 128 * k : 128 * k + 128]
    out_map = prior_out_map()
    d_prior = dot(dot(prior_in_map(), flat[...], TN, HIGH)[:, 0:64], out_map, NT, HIGH)
    d_table = grads[ROW_SMALL + 8 : ROWS, 0:128]
    d_table = [dot(d_table[:, 0:64], out_map, NT, HIGH), dot(d_table[:, 64:128], out_map, NT, HIGH)]
    d_table = [part[0:10] for part in d_table]
    d_bias = [grads[ROW_IN + 46 : ROW_IN + 47, :], grads[ROW_SMALL : ROW_SMALL + 1, :]]
    d_mix = grads[0:ROW_OUT, :]

    def squares(value):
        value = value * value
        if value.ndim == 3:
            value = jnp.sum(value, axis=0)
        return jnp.sum(jnp.sum(value, axis=0, keepdims=True), axis=1, keepdims=True)

    squared = squares(d_mix) + squares(gin[...]) + squares(gout[...]) + squares(d_prior)
    squared = squared + squares(d_bias[0]) + squares(d_bias[1]) + squares(d_gains) + squares(d_lu)
    squared = squared + squares(d_table[0]) + squares(d_table[1])
    total_norm = jnp.sqrt(squared)
    factor = jnp.minimum(1.0, CLIP_NORM / (total_norm + 1e-06))
    norm[...] = total_norm
    loss[...] = (
        grads[ROW_SMALL + 16 : ROW_SMALL + 17, 256:257] - coef * (logs + diag) + BITS * share / 10.0
    )

    def put(k, grad, at=Ellipsis):
        adamw(params[k], firsts[k], seconds[k], grad, news[k], new_firsts[k], new_seconds[k], at)

    put(0, factor * gin[...])
    put(1, factor * d_mix)
    put(2, factor * gout[...])
    put(3, (factor * d_prior).reshape(9, 24, 48))
    put(4, factor * d_bias[0], (slice(0, 1), slice(None)))
    put(4, factor * d_bias[1], (slice(1, 2), slice(None)))
    put(5, (factor * d_gains)[0:3, 0:12])
    put(6, (factor * d_lu)[0:12, 0:12])
    put(7, factor * d_table[0], (slice(None), slice(0, 48)))
    put(7, factor * d_table[1], (slice(None), slice(48, 96)))


def shape(dims, dtype=F32):
    return jax.ShapeDtypeStruct(dims, dtype)


def params_of(limit):
    return pltpu.CompilerParams(vmem_limit_bytes=limit * MIB)


def exchange_rows(up, down):
    count = lax.axis_size("band")
    before = lax.ppermute(down, "band", [(i, i + 1) for i in range(count - 1)])
    after = lax.ppermute(up, "band", [(i + 1, i) for i in range(count - 1)])
    return before, after


def body(images, noise, labels, *rest):
    params, firsts, seconds = (list(rest[8 * k : 8 * k + 8]) for k in range(3))
    for group in (params, firsts, seconds):
        group[0] = group[0].transpose(0, 2, 1)
        group[3] = group[3].transpose(0, 2, 1)
    chans, rows, width, count = images.shape
    hidden = params[1].shape[0]
    band = lax.axis_index("band")
    bands = lax.axis_size("band")
    whole = pl.BlockSpec(memory_space=pltpu.VMEM)

    top, bottom = exchange_rows(
        images[:, :2] + noise[:, :2], images[:, rows - 2 :] + noise[:, rows - 2 :]
    )
    flags = jnp.stack([band > 0, band < bands - 1]).astype(F32)
    hits = (labels[None, :] == jnp.arange(16, dtype=jnp.int32)[:, None]).astype(F32)
    counts = lax.psum(jnp.sum(hits, axis=1), "dp")
    counts = jnp.broadcast_to(counts[:, None], (16, 128))

    win, wt, mixh, mixth, bias2, wout, woutt, weff, wpt, wp, tablep = pl.pallas_call(
        weights_kernel,
        out_shape=(
            shape((hidden, 128), BF16),
            shape((128, hidden)),
            shape((hidden, hidden), BF16),
            shape((hidden, hidden), BF16),
            shape((hidden, 128)),
            shape((144, hidden), BF16),
            shape((hidden, 256), BF16),
            shape((16, 128)),
            shape((288, 256), BF16),
            shape((128, 384), BF16),
            shape((16, 128)),
        ),
        in_specs=[whole] * 8,
        out_specs=(whole,) * 11,
        scratch_shapes=[
            pltpu.VMEM((512, hidden), F32),
            pltpu.VMEM((128, 128), F32),
            pltpu.VMEM((8, 128), F32),
        ],
        compiler_params=params_of(40),
        name="weights",
    )(*params)

    cols, sub = 4, 2
    groups = width // cols
    steps = rows * groups
    size = cols * count
    full = lambda dims: pl.BlockSpec(dims, lambda i: (0,) * len(dims))
    chunk = pl.BlockSpec((1, hidden, size), lambda i: (i, 0, 0))
    ext = (rows + 4, width + 2, 16, count)
    exta = (rows + 4, width + 4, 8, count)
    act1, sg1, act2, sg2, xa2, xt, xaf, xbf, nn, edge_top, edge_bottom = pl.pallas_call(
        functools.partial(forward_kernel, cols, sub),
        grid=(steps,),
        out_shape=(shape((steps, hidden, size), BF16),) * 4
        + (
            shape(ext, BF16),
            shape(ext, BF16),
            shape(exta),
            shape((rows, width, 8, count)),
            shape((rows, width, 16, count)),
            shape((width, 16, count), BF16),
            shape((width, 16, count), BF16),
        ),
        in_specs=[full(images.shape)] * 2
        + [full(top.shape)] * 2
        + [pl.BlockSpec(memory_space=pltpu.SMEM)]
        + [full(a.shape) for a in (weff, win, mixh, bias2, wout)],
        out_specs=(chunk,) * 4
        + (
            full(ext),
            full(ext),
            full(exta),
            full((rows, width, 8, count)),
            full((rows, width, 16, count)),
            full((width, 16, count)),
            full((width, 16, count)),
        ),
        scratch_shapes=[
            pltpu.VMEM((chans, rows + 4, width, count), F32),
            pltpu.VMEM((128, size), BF16),
            pltpu.VMEM((rows + 2, width + 2, 16, count), F32),
        ],
        compiler_params=params_of(56),
        name="forward",
    )(images, noise, top, bottom, flags, weff, win, mixh, bias2, wout)

    got_top, got_bottom = exchange_rows(edge_top, edge_bottom)
    nn = nn.at[0].add(got_top.astype(F32))
    nn = nn.at[rows - 1].add(got_bottom.astype(F32))
    gain3 = params[5][2]
    zero = jnp.zeros((2,), F32)
    net_bias = jnp.concatenate([gain3[:6], zero, gain3[6:] + 2.0, zero])[:, None]
    pixels = (width // 2) * count
    dn, dprior, small = pl.pallas_call(
        coupling_kernel,
        out_shape=(
            shape((rows, width, 16, count), BF16),
            shape((288, 128)),
            shape((24, 512)),
        ),
        in_specs=[whole] * 12,
        out_specs=(whole,) * 3,
        scratch_shapes=[
            pltpu.VMEM((288, pixels), BF16),
            pltpu.VMEM((288, pixels), BF16),
            pltpu.VMEM((64, pixels), F32),
            pltpu.VMEM((64, pixels), F32),
            pltpu.VMEM((288, pixels), F32),
            pltpu.VMEM(exta, F32),
            pltpu.VMEM((rows, width, 8, count), F32),
            pltpu.VMEM((256, 256), F32),
            pltpu.VMEM((8, count), F32),
            pltpu.VMEM((16, count), F32),
            pltpu.VMEM((128, count), F32),
        ],
        compiler_params=params_of(48),
        name="coupling",
    )(nn, edge_top, edge_bottom, xaf, xbf, xt, labels[None, :], counts, wp, wpt, tablep, net_bias)

    dn_top, dn_bottom = exchange_rows(dn[0], dn[rows - 1])
    packed = pl.pallas_call(
        functools.partial(backward_kernel, cols, sub),
        grid=(steps,),
        out_shape=shape((ROWS, hidden)),
        in_specs=[chunk] * 4
        + [full(a.shape) for a in (dn, dn_top, dn_bottom, xa2, xt, mixth, woutt, wt, dprior, small)],
        out_specs=full((ROWS, hidden)),
        scratch_shapes=[
            pltpu.VMEM((rows + 2, width + 2, 16, count), BF16),
            pltpu.VMEM((256, size), BF16),
            pltpu.VMEM((256, size), BF16),
            pltpu.VMEM((hidden, 128), F32),
            pltpu.VMEM((144, hidden), F32),
        ],
        compiler_params=params_of(56),
        name="backward",
    )(act1, sg1, act2, sg2, dn, dn_top, dn_bottom, xa2, xt, mixth, woutt, wt, dprior, small)

    both = ("dp", "band")
    devices = lax.axis_size(both)
    lanes = ROWS * hidden // 128
    per = -(-lanes // devices)
    flat = jnp.pad(packed.reshape(lanes, 128), ((0, per * devices - lanes), (0, 0)))
    parts = lax.all_to_all(flat.reshape(devices, per, 128), both, 0, 0, tiled=True)
    mine = jnp.sum(parts, axis=0)
    spread = jnp.broadcast_to(mine[None], (devices, per, 128))
    grads = lax.all_to_all(spread, both, 0, 0, tiled=True)
    grads = grads.reshape(devices * per, 128)[:lanes].reshape(ROWS, hidden)

    area = float(width * width)
    results = pl.pallas_call(
        functools.partial(update_kernel, area, 12.0 * width * width),
        out_shape=(shape((1, 1)), shape((1, 1))) + tuple(shape(p.shape) for p in params) * 3,
        in_specs=[whole] * 26,
        out_specs=(whole,) * 26,
        scratch_shapes=[
            pltpu.VMEM((128, 128), F32),
            pltpu.VMEM((8, 128), F32),
            pltpu.VMEM((9, 6, hidden), F32),
            pltpu.VMEM((9, 12, hidden), F32),
            pltpu.VMEM((288, 128), F32),
        ],
        compiler_params=params_of(48),
        name="update",
    )(grads, counts, *params, *firsts, *seconds)
    outs = [results[0][0, 0], results[1][0, 0]]
    for k in range(3):
        group = list(results[2 + 8 * k : 10 + 8 * k])
        group[0] = group[0].transpose(0, 2, 1)
        group[3] = group[3].transpose(0, 2, 1)
        outs += group
    return tuple(outs)


def solution(mesh):
    field = P(None, "band", None, "dp")
    return jax.shard_map(
        body,
        mesh=mesh,
        in_specs=(field, field, P("dp")) + (P(),) * 24,
        out_specs=(P(),) * 26,
        check_vma=False,
    )
```

time: 521 us -> 269 us (0.52)
  matrix products: 188 us -> 0 us
  Pallas kernels: 0 us -> 100 us
  local copies, waits for them, and re-layouts: 97.9 us -> 25.3 us
  waiting for transfers between devices: 80.5 us -> 13.3 us
  blocking collectives: 48.7 us -> 104 us
  other arithmetic: 44.4 us -> 7.44 us
  between operations: 27.7 us -> 1.22 us
  starting transfers between devices: 31.9 us -> 15.9 us
    dot_general x20 -> x0, matrix products: 188 us -> none  [the longest x3 64.1 us: dot_tn(): lax.dot_general(left, right, (((0,), (0,)), ((), ())), preferred_element_...]
    pallas_call x0 -> x5, Pallas kernels: none -> 100 us  [the longest x1 44.3 us: body(): pl.pallas_call(functools.partial(backward_kernel, cols, sub), grid=(steps...]
    all_to_all x0 -> x2, blocking collectives: none -> 91.9 us  [the longest x1 46.3 us: body(): grads = lax.all_to_all(spread, both, 0, 0, tiled=True)]
    psum x1 -> x0, waiting for transfers between devices: 61.2 us -> none  [body(): lax.psum((d_conv_in, d_mixer, d_conv_out, d_prior, d_hidden_bias, d_gains...]
    concatenate x5 -> x0, local copies, waits for them, and re-layouts: 54 us -> none  [patches(): jnp.concatenate([padded[:, 1 + sign * dy:1 + sign * dy + rows, 1 + sign *...]
    psum x2 -> x1, blocking collectives: 48.7 us -> 12.2 us  [body(): counts = lax.psum(jnp.sum(hits, axis=1), 'dp')]
    ppermute x12 -> x6, starting transfers between devices: 31.9 us -> 15.9 us  [the longest x3 12 us: exchange_rows(): before = lax.ppermute(down, 'band', [(i, i + 1) for i in range(count - 1)])]
    sub x8 -> x0, other arithmetic: 11.6 us -> none  [adamw(): weight - RATE * (first_hat / (jnp.sqrt(second_hat) + EPSILON) + DECAY * w...]
  transfers between devices with their start and end apart: 13 -> 6, of which waited for: 8 -> 4; matrix products, arithmetic and copies ran while one was open for 7% -> 1% of each run, Pallas kernels for 0% -> 1%
where the time goes in v1:
time: 269 us; the launch traced here: 267 us
  blocking collectives  104 us (39%)
  Pallas kernels  100 us (37%)
  local copies, waits for them, and re-layouts  25.3 us (9%)
  starting transfers between devices  15.9 us (6%)
  waiting for transfers between devices  13.3 us (5%)
  other arithmetic  7.44 us (3%)
    all_to_all x1, blocking collectives, body(): grads = lax.all_to_all(spread, both, 0, 0, tiled=True)  46.3 us
    all_to_all x1, blocking collectives, body(): lax.all_to_all(flat.reshape(devices, per, 128), both, 0, 0, tiled=True)  45.5 us
    pallas_call x1, Pallas kernels, body(): pl.pallas_call(functools.partial(backward_kernel, cols, sub), grid=(steps...  44.3 us
    pallas_call x1, Pallas kernels, body(): pl.pallas_call(functools.partial(forward_kernel, cols, sub), grid=(steps,...  39.8 us
    unnamed x92, local copies, waits for them, and re-layouts  19 us
    psum x1, blocking collectives, body(): counts = lax.psum(jnp.sum(hits, axis=1), 'dp')  12.2 us
    ppermute x3, waiting for transfers between devices, exchange_rows(): after = lax.ppermute(up, 'band', [(i + 1, i) for i in range(count - 1)])  12.1 us
    ppermute x3, starting transfers between devices, exchange_rows(): before = lax.ppermute(down, 'band', [(i, i + 1) for i in range(count - 1)])  12 us
  transfers between devices with their start and end apart: 6, of which 4 were waited for; matrix products, arithmetic and copies ran while one was open for 1% of the time, Pallas kernels for 1%

profile of v1, /device:TPU:0, one launch (start us, length us, event | category | flops | bytes accessed | tf_op | source)
XLA Modules:
  0.0 267.4 jit_solution(955194649824644377)
XLA Ops:
  0.8 1.6 slice_add_fusion
  2.4 5.0 %collective-permute-start = (f32[12,2,16,256]{3,2,1,0:T(8,128)S(1)}, f32[12,2,16,256]{3,2,1,0:T(8,128)S(1)}, u32[]{:S(2)}, u32[]{:S(2)}) collective-permute-start(f32[12,2,16,256]{3,2,1,0:T(8,128)S(1)} %get-tuple-element.153), channel_id=1, source_target_pairs={{0,1},{1,2},{2,3},{4,5},{5,6},{6,7},{8,9},{9,10},{10,11},{12,13},{... | collective-permute-start | bytes 1179656 | tf_op jit(solution)/shard_map/ppermute | solution.py:527
  7.3 1.3 collective-permute-start.1
  8.7 1.7 weights.1
  10.4 0.8 copy-done.9
  11.2 0.8 copy-done.11
  12.0 0.7 copy-done.15
  12.7 0.7 copy-done.16
  13.4 0.7 copy-done.17
  14.1 0.7 copy-done.21
  14.8 0.7 copy-done.24
  15.4 0.6 add_convert_fusion.flags
  16.2 3.7 %collective-permute-done.1.bottom = f32[12,2,16,256]{3,2,1,0:T(8,128)S(1)} collective-permute-done((f32[12,2,16,256]{3,2,1,0:T(8,128)S(1)}, f32[12,2,16,256]{3,2,1,0:T(8,128)S(1)}, u32[]{:S(2)}, u32[]{:S(2)}) %collective-permute-start.1) | collective-permute-done | bytes 393248 | tf_op jit(solution)/shard_map/ppermute | solution.py:528
  19.8 0.8 copy-done.43
  20.6 39.8 %forward.1 = (bf16[16,512,1024]{2,1,0:T(8,128)(2,1)}, bf16[16,512,1024]{2,1,0:T(8,128)(2,1)}, bf16[16,512,1024]{2,1,0:T(8,128)(2,1)}, bf16[16,512,1024]{2,1,0:T(...) custom-call(f32[12,4,16,256]{3,2,1,0:T(8,128)} %images.1, ...), custom_call_target="tpu_custom_call" | custom-call | tf_op jit(solution)/shard_map/forward/pallas_call | solution.py:585
  60.4 3.6 %collective-permute-start.2 = (bf16[16,16,256]{2,1,0:T(8,128)(2,1)}, bf16[16,16,256]{2,1,0:T(8,128)(2,1)S(1)}, u32[]{:S(2)}, u32[]{:S(2)}) collective-permute-start(bf16[16,16,256]{2,1,0:T(8,128)(2,1)} %get-tuple-element.111.edge_bottom), channel_id=1, source_target_pairs={{0,1},{1,2},{2,3},{4,5},{5,6},{6,7},{8,9},{9,10},{10,11},{12,13},{... | collective-permute-start | bytes 393224 | tf_op jit(solution)/shard_map/ppermute | solution.py:527
  64.1 12.2 %psum.7 = f32[16]{0:T(128)S(1)} all-reduce(f32[16]{0:T(128)S(1)} %convert_reduce_fusion), channel_id=1, replica_groups=mesh['dp'=8,'band'=4] {'dp'}, use_global_device_ids=true, to_apply=%region_1.0 | all-reduce | flops 16 | bytes 128 | tf_op jit(solution)/shard_map/psum | solution.py:548
  76.4 1.3 collective-permute-start.3
  77.7 1.7 fusion.1
  79.4 4.1 %collective-permute-done.3 = bf16[16,16,256]{2,1,0:T(8,128)(2,1)S(1)} collective-permute-done((bf16[16,16,256]{2,1,0:T(8,128)(2,1)}, bf16[16,16,256]{2,1,0:T(8,128)(2,1)S(1)}, u32[]{:S(2)}, u32[]{:S(2)}) %collective-permute-start.3) | collective-permute-done | bytes 131104 | tf_op jit(solution)/shard_map/ppermute | solution.py:528
  83.5 1.7 fusion.nn
  85.2 1.2 copy-done.2
  86.4 1.3 copy-done.3
  87.8 1.0 copy-done.10
  88.8 0.9 copy-done.22
  89.7 0.9 copy-done.23
  90.6 6.7 %coupling.1 = (bf16[4,16,16,256]{3,2,1,0:T(8,128)(2,1)S(1)}, f32[288,128]{1,0:T(8,128)S(1)}, f32[24,512]{1,0:T(8,128)S(1)}) custom-call(f32[4,16,16,256]{3,2,1,0:T(8,128)S(1)} %copy-done.2, bf16[16,16,256]{2,1,0:T(8,128)(2,1)S(1)} %copy-done.22, bf16[16,16,256]{2,1,0:T(8,128)(2,1)S(1)} %copy-done.23, f32[8,20,8,256]{3,2,1,0:T(8,128)S(1)} %copy-done.3, ...), custom_call_target="tpu_custom_call" | custom-call | tf_op jit(solution)/shard_map/coupling/pallas_call | solution.py:628
  97.3 0.7 copy-done.18
  98.0 0.6 copy-done.27
  98.6 3.5 %collective-permute-start.4 = (bf16[16,16,256]{2,1,0:T(8,128)(2,1)S(1)}, bf16[16,16,256]{2,1,0:T(8,128)(2,1)S(1)}, u32[]{:S(2)}, u32[]{:S(2)}) collective-permute-start(bf16[16,16,256]{2,1,0:T(8,128)(2,1)S(1)} %get-tuple-element.155), channel_id=1, source_target_pairs={{0,1},{1,2},{2,3},{4,5},{5,6},{6,7},{8,9},{9,10},{10,11},{12,13},{... | collective-permute-start | bytes 393224 | tf_op jit(solution)/shard_map/ppermute | solution.py:527
  102.1 1.3 collective-permute-start.5
  103.4 1.2 collective-permute-done.4.dn_top
  104.6 4.4 %collective-permute-done.5.dn_bottom = bf16[16,16,256]{2,1,0:T(8,128)(2,1)S(1)} collective-permute-done((bf16[16,16,256]{2,1,0:T(8,128)(2,1)S(1)}, bf16[16,16,256]{2,1,0:T(8,128)(2,1)S(1)}, u32[]{:S(2)}, u32[]{:S(2)}) %collective-permute-start.5) | collective-permute-done | bytes 131104 | tf_op jit(solution)/shard_map/ppermute | solution.py:528
  109.0 0.6 copy-done.45
  109.6 44.3 %backward.1 = f32[848,512]{1,0:T(8,128)} custom-call(bf16[16,512,1024]{2,1,0:T(8,128)(2,1)} %get-tuple-element.106.act1, bf16[16,512,1024]{2,1,0:T(8,128)(2,1)} %get-tuple-element.107.sg1, bf16[16,512,1024]{2,1,0:T(8,128)(2,1)} %get-tuple-element.108.act2, bf16[16,512,1024]{2,1,0:T(8,128)(2,1)} %get-tuple-element.109.sg2, ...), custom_call_target="tpu_custom_call" | custom-call | tf_op jit(solution)/shard_map/backward/pallas_call | solution.py:655
  153.9 2.9 %reshape.140 = f32[32,106,128]{2,1,0:T(8,128)} reshape(f32[848,512]{1,0:T(8,128)} %backward.1) | data formatting | bytes 3473408 | tf_op jit(solution)/shard_map/reshape | solution.py:678
  156.8 45.5 %all_to_all.10 = f32[32,106,128]{2,1,0:T(8,128)} all-to-all(f32[32,106,128]{2,1,0:T(8,128)} %reshape.140), channel_id=1, replica_groups=mesh['dp'=8,'band'=4] {'dp','band'}, dimensions={0} | all-to-all | bytes 3473408 | tf_op jit(solution)/shard_map/all_to_all | solution.py:678
  202.3 1.6 reduce_sum.19
  204.0 46.3 %all_to_all.11 = f32[32,106,128]{2,1,0:T(8,128)} all-to-all(f32[32,106,128]{2,1,0:T(8,128)S(1)} %broadcast_in_dim.11), channel_id=1, replica_groups=mesh['dp'=8,'band'=4] {'dp','band'}, dimensions={0} | all-to-all | bytes 3473408 | tf_op jit(solution)/shard_map/all_to_all | solution.py:681
  250.5 3.2 %reshape_reshape.3.refs_0_ = f32[848,512]{1,0:T(8,128)} reshape(f32[32,106,128]{2,1,0:T(8,128)} %all_to_all.11) | data formatting | bytes 3473408 | tf_op jit(solution)/shard_map/reshape;reshape | solution.py:682
  253.7 1.2 copy-done.7
  254.9 0.9 copy-done.20
  255.8 0.9 copy-done.26
  256.7 0.7 copy-done.34
  257.4 0.7 copy-done.35
  258.1 0.7 copy-done.39
  258.8 0.7 copy-done.40
  259.5 7.7 %update.1 = (f32[1,1]{1,0:T(1,128)}, f32[1,1]{1,0:T(1,128)}, f32[9,6,512]{2,1,0:T(8,128)}, f32[512,512]{1,0:T(8,128)}, f32[9,12,512]{2,1,0:T(8,128)}, /*index=5*...) custom-call(f32[848,512]{1,0:T(8,128)} %reshape_reshape.3.refs_0_, ...), custom_call_target="tpu_custom_call" | custom-call | tf_op jit(solution)/shard_map/update/pallas_call | solution.py:685
  (79 shorter events, 0.7 us)
Async XLA Ops:
  0.7 8.0 %copy-start.8 = (f32[9,512,6]{1,2,0:T(8,128)S(1)}, f32[9,512,6]{1,2,0:T(8,128)}, u32[]{:S(2)}) copy-start(f32[9,512,6]{1,2,0:T(8,128)} %param.34) | copy-start | bytes 331780
  0.7 8.0 %copy-start.12 = (f32[9,48,24]{1,2,0:T(8,128)S(1)}, f32[9,48,24]{1,2,0:T(8,128)}, u32[]{:S(2)}) copy-start(f32[9,48,24]{1,2,0:T(8,128)} %param.37) | copy-start | bytes 124420
  0.7 8.0 %copy-start.1 = (f32[512,512]{1,0:T(8,128)S(1)}, f32[512,512]{1,0:T(8,128)}, u32[]{:S(2)}) copy-start(f32[512,512]{1,0:T(8,128)} %refs_3_.1) | copy-start | bytes 3145732
  0.7 8.0 %copy-start.5 = (f32[9,12,512]{2,1,0:T(8,128)S(1)}, f32[9,12,512]{2,1,0:T(8,128)}, u32[]{:S(2)}) copy-start(f32[9,12,512]{2,1,0:T(8,128)} %refs_4_.1) | copy-start | bytes 663556
  0.7 8.0 %copy-start.30 = (f32[2,512]{1,0:T(2,128)S(1)}, f32[2,512]{1,0:T(2,128)}, u32[]{:S(2)}) copy-start(f32[2,512]{1,0:T(2,128)} %refs_6_.1) | copy-start | bytes 12292
  0.7 8.0 %copy-start.31 = (f32[3,12]{1,0:T(4,128)S(1)}, f32[3,12]{1,0:T(4,128)}, u32[]{:S(2)}) copy-start(f32[3,12]{1,0:T(4,128)} %refs_7_.1) | copy-start | bytes 436
  0.7 8.0 %copy-start.28 = (f32[12,12]{1,0:T(8,128)S(1)}, f32[12,12]{1,0:T(8,128)}, u32[]{:S(2)}) copy-start(f32[12,12]{1,0:T(8,128)} %refs_8_.1) | copy-start | bytes 1732
  0.7 8.0 %copy-start.29 = (f32[10,96]{1,0:T(8,128)S(1)}, f32[10,96]{1,0:T(8,128)}, u32[]{:S(2)}) copy-start(f32[10,96]{1,0:T(8,128)} %refs_9_.1) | copy-start | bytes 11524
  0.8 15.3 %copy-start.41 = (s32[256]{0:T(256)S(1)}, s32[256]{0:T(256)}, u32[]{:S(2)}) copy-start(s32[256]{0:T(256)} %param.33) | copy-start | bytes 3076
  2.4 13.8 %collective-permute-start = (f32[12,2,16,256]{3,2,1,0:T(8,128)S(1)}, f32[12,2,16,256]{3,2,1,0:T(8,128)S(1)}, u32[]{:S(2)}, u32[]{:S(2)}) collective-permute-start(f32[12,2,16,256]{3,2,1,0:T(8,128)S(1)} %get-tuple-element.153), channel_id=1, source_target_pairs={{0,1},{1,2},{2,3},{4,5},{5,6},{6,7},{8,9},{9,10},{10,11},{12,13},{... | collective-permute-start | bytes 1179656 | tf_op jit(solution)/shard_map/ppermute | solution.py:527
  7.3 12.5 %collective-permute-start.1 = (f32[12,2,16,256]{3,2,1,0:T(8,128)S(1)}, f32[12,2,16,256]{3,2,1,0:T(8,128)S(1)}, u32[]{:S(2)}, u32[]{:S(2)}) collective-permute-start(f32[12,2,16,256]{3,2,1,0:T(8,128)S(1)} %get-tuple-element.152), channel_id=1, source_target_pairs={{1,0},{2,1},{3,2},{5,4},{6,5},{7,6},{9,8},{10,9},{11,10},{13,12},{... | collective-permute-start | bytes 1179656 | tf_op jit(solution)/shard_map/ppermute | solution.py:528
  10.4 0.8 copy-start.9
  11.2 0.8 copy-start.11
  12.0 0.7 copy-start.15
  12.7 0.7 copy-start.16
  13.4 0.7 copy-start.17
  15.4 4.4 %copy-start.36 = (f32[16,128]{1,0:T(8,128)}, f32[16,128]{1,0:T(8,128)S(1)}, u32[]{:S(2)}) copy-start(f32[16,128]{1,0:T(8,128)S(1)} %get-tuple-element.101.weff) | copy-start | bytes 24580
  16.1 3.7 %copy-start.42 = (f32[12,2,16,256]{3,2,1,0:T(8,128)}, f32[12,2,16,256]{3,2,1,0:T(8,128)S(1)}, u32[]{:S(2)}) copy-start(f32[12,2,16,256]{3,2,1,0:T(8,128)S(1)} %collective-permute-done.top) | copy-start | bytes 1179652
  19.8 0.8 copy-start.43
  60.4 24.8 %copy-start = (bf16[8,18,16,256]{3,2,1,0:T(8,128)(2,1)S(1)}, bf16[8,18,16,256]{3,2,1,0:T(8,128)(2,1)}, u32[]{:S(2)}) copy-start(bf16[8,18,16,256]{3,2,1,0:T(8,128)(2,1)} %get-tuple-element.115.xt) | copy-start | bytes 3538948
  60.4 17.3 %collective-permute-start.2 = (bf16[16,16,256]{2,1,0:T(8,128)(2,1)}, bf16[16,16,256]{2,1,0:T(8,128)(2,1)S(1)}, u32[]{:S(2)}, u32[]{:S(2)}) collective-permute-start(bf16[16,16,256]{2,1,0:T(8,128)(2,1)} %get-tuple-element.111.edge_bottom), channel_id=1, source_target_pairs={{0,1},{1,2},{2,3},{4,5},{5,6},{6,7},{8,9},{9,10},{10,11},{12,13},{... | collective-permute-start | bytes 393224 | tf_op jit(solution)/shard_map/ppermute | solution.py:527
  76.4 7.1 %collective-permute-start.3 = (bf16[16,16,256]{2,1,0:T(8,128)(2,1)}, bf16[16,16,256]{2,1,0:T(8,128)(2,1)S(1)}, u32[]{:S(2)}, u32[]{:S(2)}) collective-permute-start(bf16[16,16,256]{2,1,0:T(8,128)(2,1)} %get-tuple-element.112.edge_top), channel_id=1, source_target_pairs={{1,0},{2,1},{3,2},{5,4},{6,5},{7,6},{9,8},{10,9},{11,10},{13,12},{... | collective-permute-start | bytes 393224 | tf_op jit(solution)/shard_map/ppermute | solution.py:528
  85.2 1.2 copy-start.2
  86.4 1.3 copy-start.3
  87.8 1.0 copy-start.10
  88.8 0.9 copy-start.22
  89.7 0.9 copy-start.23
  97.3 0.7 copy-start.18
  98.6 10.4 %copy-start.4 = (bf16[4,16,16,256]{3,2,1,0:T(8,128)(2,1)}, bf16[4,16,16,256]{3,2,1,0:T(8,128)(2,1)S(1)}, u32[]{:S(2)}) copy-start(bf16[4,16,16,256]{3,2,1,0:T(8,128)(2,1)S(1)} %get-tuple-element.119.dn) | copy-start | bytes 1572868
  98.6 6.0 %collective-permute-start.4 = (bf16[16,16,256]{2,1,0:T(8,128)(2,1)S(1)}, bf16[16,16,256]{2,1,0:T(8,128)(2,1)S(1)}, u32[]{:S(2)}, u32[]{:S(2)}) collective-permute-start(bf16[16,16,256]{2,1,0:T(8,128)(2,1)S(1)} %get-tuple-element.155), channel_id=1, source_target_pairs={{0,1},{1,2},{2,3},{4,5},{5,6},{6,7},{8,9},{9,10},{10,11},{12,13},{... | collective-permute-start | bytes 393224 | tf_op jit(solution)/shard_map/ppermute | solution.py:527
  102.1 6.9 %collective-permute-start.5 = (bf16[16,16,256]{2,1,0:T(8,128)(2,1)S(1)}, bf16[16,16,256]{2,1,0:T(8,128)(2,1)S(1)}, u32[]{:S(2)}, u32[]{:S(2)}) collective-permute-start(bf16[16,16,256]{2,1,0:T(8,128)(2,1)S(1)} %get-tuple-element.154), channel_id=1, source_target_pairs={{1,0},{2,1},{3,2},{5,4},{6,5},{7,6},{9,8},{10,9},{11,10},{13,12},{... | collective-permute-start | bytes 393224 | tf_op jit(solution)/shard_map/ppermute | solution.py:528
  104.6 4.4 %copy-start.44 = (bf16[16,16,256]{2,1,0:T(8,128)(2,1)}, bf16[16,16,256]{2,1,0:T(8,128)(2,1)S(1)}, u32[]{:S(2)}) copy-start(bf16[16,16,256]{2,1,0:T(8,128)(2,1)S(1)} %collective-permute-done.4.dn_top) | copy-start | bytes 393220
  250.4 3.2 %copy-start.6 = (f32[512,512]{1,0:T(8,128)S(1)}, f32[512,512]{1,0:T(8,128)}, u32[]{:S(2)}) copy-start(f32[512,512]{1,0:T(8,128)} %refs_11_.1) | copy-start | bytes 3145732
  250.4 3.2 %copy-start.13 = (f32[9,12,512]{2,1,0:T(8,128)S(1)}, f32[9,12,512]{2,1,0:T(8,128)}, u32[]{:S(2)}) copy-start(f32[9,12,512]{2,1,0:T(8,128)} %refs_12_.1) | copy-start | bytes 663556
  250.4 3.2 %copy-start.14 = (f32[9,12,512]{2,1,0:T(8,128)S(1)}, f32[9,12,512]{2,1,0:T(8,128)}, u32[]{:S(2)}) copy-start(f32[9,12,512]{2,1,0:T(8,128)} %refs_20_.1) | copy-start | bytes 663556
  250.4 3.2 %copy-start.19 = (f32[9,512,6]{1,2,0:T(8,128)S(1)}, f32[9,512,6]{1,2,0:T(8,128)}, u32[]{:S(2)}) copy-start(f32[9,512,6]{1,2,0:T(8,128)} %param.42) | copy-start | bytes 331780
  250.4 3.2 %copy-start.25 = (f32[9,48,24]{1,2,0:T(8,128)S(1)}, f32[9,48,24]{1,2,0:T(8,128)}, u32[]{:S(2)}) copy-start(f32[9,48,24]{1,2,0:T(8,128)} %param.45) | copy-start | bytes 124420
  250.4 3.2 %copy-start.32 = (f32[12,12]{1,0:T(8,128)S(1)}, f32[12,12]{1,0:T(8,128)}, u32[]{:S(2)}) copy-start(f32[12,12]{1,0:T(8,128)} %refs_16_.1) | copy-start | bytes 1732
  250.4 3.2 %copy-start.33 = (f32[10,96]{1,0:T(8,128)S(1)}, f32[10,96]{1,0:T(8,128)}, u32[]{:S(2)}) copy-start(f32[10,96]{1,0:T(8,128)} %refs_17_.1) | copy-start | bytes 11524
  250.4 3.2 %copy-start.37 = (f32[2,512]{1,0:T(2,128)S(1)}, f32[2,512]{1,0:T(2,128)}, u32[]{:S(2)}) copy-start(f32[2,512]{1,0:T(2,128)} %refs_14_.1) | copy-start | bytes 12292
  250.5 3.2 %copy-start.38 = (f32[2,512]{1,0:T(2,128)S(1)}, f32[2,512]{1,0:T(2,128)}, u32[]{:S(2)}) copy-start(f32[2,512]{1,0:T(2,128)} %refs_22_.1) | copy-start | bytes 12292
  253.7 1.2 copy-start.7
  254.9 0.9 copy-start.20
  255.8 0.9 copy-start.26
  256.7 0.7 copy-start.34
  257.4 0.7 copy-start.35
  258.1 0.7 copy-start.39
  258.8 0.7 copy-start.40
  (4 other events, 2.6 us)

commit v2 on v1

--- a/solution.py
+++ b/solution.py
@@ -28,10 +28,11 @@
 
 ROW_MIX = 0
 ROW_OUT = 512
-ROW_IN = ROW_OUT + 144
-ROW_PRIOR = ROW_IN + 96
+ROW_IN = ROW_OUT + 108
+ROW_BIAS = ROW_IN + 54
+ROW_PRIOR = ROW_BIAS + 6
 ROW_SMALL = ROW_PRIOR + 72
-ROWS = ROW_SMALL + 24
+ROWS = ROW_SMALL + 16
 
 
 def dot(left, right, dims=NN, precision=None):
@@ -224,7 +225,7 @@
         edge_bottom[...] = acc[rows + 1, 1 : width + 1].astype(BF16)
 
 
-def coupling_kernel(nn, edge_top, edge_bottom, xaf, xbf, xt, labels, counts, wp, wpt, tablep, weff_gains,
+def coupling_kernel(nn, edge_top, edge_bottom, xaf, xbf, xt, labels, counts, wp, wpt, tablep, net_bias_ref,
                     dn, dprior, small, taps_hi, taps_lo, stats, dstats, dtaps, dxa, dxb, total,
                     loss_acc, gain_acc, table_acc):
     rows, width, _, count = nn.shape
@@ -244,7 +245,7 @@
     dprior[...] = jnp.zeros_like(dprior)
     dstats[...] = jnp.zeros_like(dstats)
     keep = iota((8, count), 0) < 6
-    net_bias = weff_gains[...]
+    net_bias = net_bias_ref[...]
     bias_a = jnp.broadcast_to(net_bias[0:8, 0:1], (8, count))
     bias_b = jnp.broadcast_to(net_bias[8:16, 0:1], (8, count))
 
@@ -269,6 +270,8 @@
                     d = 2 * dy + dx
                     r, c = 2 * r2 + dy, 2 * w + dx
                     tile = nn[r, c]
+                    tile = tile + jnp.where(r == 0, edge_top[c].astype(F32), 0.0)
+                    tile = tile + jnp.where(r == rows - 1, edge_bottom[c].astype(F32), 0.0)
                     shift = tile[0:8] + bias_a
                     raw = tile[8:16] + bias_b
                     sig = jax.nn.sigmoid(raw)
@@ -344,17 +347,17 @@
     gather = as_f32((iota((16, 256), 0) == ((iota((16, 256), 1) & 7) + 8 * (iota((16, 256), 1) >> 7))))
     fold = as_f32((iota((256, 128), 0) & 15) == iota((256, 128), 1))
     small[...] = jnp.zeros_like(small)
-    small[8:24, 128:256] = dot(dot(gather, masked, NN, HIGH), fold, NN, HIGH)
-    small[8:24, 0:128] = dot(hot, table_acc[...], NT, HIGH)
+    small[:, 128:256] = dot(dot(gather, masked, NN, HIGH), fold, NN, HIGH)
+    small[:, 0:128] = dot(hot, table_acc[...], NT, HIGH)
     lone = jnp.ones((8, count), F32)
     gain_row = dot(dot(lone, gain_acc[...], NT, HIGH), half_map(), NN, HIGH)
-    small[8:16, 256:384] = gain_row
+    small[0:8, 256:384] = gain_row
     value = jnp.sum(jnp.sum(loss_acc[...], axis=0, keepdims=True) * coef[0:1], axis=1, keepdims=True)
-    small[16:24, 256:384] = jnp.broadcast_to(-value, (8, 128))
-
-
-def backward_kernel(cols, sub, act1, sg1, act2, sg2, dn, dn_top, dn_bottom, xa2, xt, mixth, woutt, wt,
-                    dprior, small, packed, dnp, taps, gtaps, bias_acc, wfield):
+    small[8:16, 256:384] = jnp.broadcast_to(-value, (8, 128))
+
+
+def backward_kernel(cols, sub, act1, sg1, act2, sg2, place, dn, dn_top, dn_bottom, xa2, xt, mixth, woutt, wt,
+                    dprior, small, keep, send, packed, dnp, taps, gtaps, bias_acc, wfield, gout, gin):
     step = pl.program_id(0)
     rows, width, _, count = dn.shape
     groups = width // cols
@@ -362,6 +365,8 @@
     @pl.when(step == 0)
     def _():
         packed[...] = jnp.zeros_like(packed)
+        gout[...] = jnp.zeros_like(gout)
+        gin[...] = jnp.zeros_like(gin)
         bias_acc[...] = jnp.zeros_like(bias_acc)
         wfield[...] = jnp.zeros_like(wfield)
         dnp[...] = jnp.zeros_like(dnp)
@@ -392,19 +397,27 @@
         for k in range(1, size // 128):
             bias = bias + wide[:, k * 128 : (k + 1) * 128]
         bias_acc[...] += bias
-        packed[ROW_OUT:ROW_IN, :] += dot(gtaps[0:144, lanes], act2[0, :, lanes], NT)
+        gout[...] += dot(gtaps[0:144, lanes], act2[0, :, lanes], NT)
         packed[ROW_MIX:ROW_OUT, :] += dot(grad2, act1[0, :, lanes], NT)
         gathered = dot(taps[0:240, lanes], grad1, NT)
-        packed[ROW_IN:ROW_PRIOR, :] += gathered[0:96]
+        gin[...] += gathered[0:96]
         wfield[...] += gathered[96:240]
 
     @pl.when(step == rows * groups - 1)
     def _():
+        for tap in range(9):
+            at = ROW_OUT + 12 * tap
+            packed[at : at + 6, :] = gout[16 * tap : 16 * tap + 6, :]
+            packed[at + 6 : at + 12, :] = gout[16 * tap + 8 : 16 * tap + 14, :]
+            at = ROW_IN + 6 * tap
+            from_row = (tap // 3) * 32 + (tap % 3) * 8
+            packed[at : at + 6, :] = gin[from_row : from_row + 6, :]
+        packed[ROW_BIAS : ROW_BIAS + 1, :] = gin[46:47, :]
+        lone = jnp.ones((8, 128), F32)
+        packed[ROW_BIAS + 1 : ROW_BIAS + 2, :] = dot(lone, bias_acc[...], NT, HIGH)[0:1]
         for k in range(4):
             packed[ROW_PRIOR:ROW_SMALL, 128 * k : 128 * k + 128] = dprior[72 * k : 72 * k + 72, :]
         packed[ROW_SMALL:ROWS, :] = small[...]
-        lone = jnp.ones((8, 128), F32)
-        packed[ROW_SMALL : ROW_SMALL + 8, :] = dot(lone, bias_acc[...], NT, HIGH)
         cross = dot(wt[0:96, :], wfield[...], NT, HIGH)
         row, col = iota((96, 144), 0), iota((96, 144), 1)
         slot = (row >> 3) & 3
@@ -412,7 +425,58 @@
         gather = as_f32(iota((8, 96), 0) == (iota((8, 96), 1) & 7))
         fold = as_f32((iota((144, 128), 0) & 15) == iota((144, 128), 1))
         field_terms = dot(dot(gather, jnp.where(same, cross, 0.0), NN, HIGH), fold, NN, HIGH)
-        packed[ROW_SMALL + 8 : ROW_SMALL + 16, 128:256] += 2.0 * field_terms
+        packed[ROW_SMALL : ROW_SMALL + 8, 128:256] += 2.0 * field_terms
+        chunks, each = keep.shape[:2]
+        core = place[0]
+        for k in range(2 * chunks):
+            block = packed[k * each : (k + 1) * each, :]
+            mine = core == k // chunks
+
+            @pl.when(mine)
+            def _():
+                keep[k % chunks] = block
+
+            @pl.when(jnp.logical_not(mine))
+            def _():
+                send[k % chunks] = block
+
+
+def halve_kernel(place, keep, got, mine, *sends):
+    count = len(sends) + 1
+    bands = keep.shape[0] // count
+    here = place[1]
+    for m in range(count):
+        target = mine if m == 0 else sends[m - 1]
+        at = pl.ds((here ^ m) * bands, bands)
+        target[...] = keep[at] + got[at]
+
+
+def spread_kernel(place, bands, first, *refs):
+    gots, mine, sends = refs[: -bands], refs[-bands], refs[1 - bands :]
+    here = place[2]
+    for k in range(bands):
+        target = mine if k == 0 else sends[k - 1]
+        at = lax.rem(here + k, bands)
+        value = first[at]
+        for got in gots:
+            value = value + got[at]
+        target[...] = value
+
+
+def sum_kernel(*refs):
+    value = refs[0][...]
+    for ref in refs[1:-1]:
+        value = value + ref[...]
+    refs[-1][...] = value
+
+
+def gather_kernel(place, which, xor, mine, *refs):
+    out = refs[-1]
+    here = place[which]
+    count = len(refs)
+    for k in range(count):
+        at = (here ^ k) if xor else lax.rem(here - k + count, count)
+        out[at] = (mine if k == 0 else refs[k - 1])[...]
 
 
 def adamw(weight, first, second, grad, out, out_first, out_second, at=Ellipsis):
@@ -428,11 +492,16 @@
 
 
 def update_kernel(area, dims, *refs):
-    grads, counts = refs[:2]
-    params, firsts, seconds = refs[2:10], refs[10:18], refs[18:26]
-    loss, norm = refs[26:28]
-    news, new_firsts, new_seconds = refs[28:36], refs[36:44], refs[44:52]
-    square, strip, gin, gout, flat = refs[52:]
+    place, own, other, counts = refs[:4]
+    refs = refs[4:]
+    params, firsts, seconds = refs[:8], refs[8:16], refs[16:24]
+    loss, norm = refs[24:26]
+    news, new_firsts, new_seconds = refs[26:34], refs[34:42], refs[42:50]
+    square, strip, gin, gout, flat, grads = refs[50:]
+    chunks, each = own.shape[:2]
+    for k in range(2 * chunks):
+        mine = place[0] == k // chunks
+        grads[k * each : (k + 1) * each, :] = jnp.where(mine, own[k % chunks], other[k % chunks])
     bias, gains_ref, lu_ref = params[4:7]
     hidden = grads.shape[1]
     square[...] = jnp.zeros_like(square)
@@ -442,7 +511,7 @@
     gains = strip[...]
     lower, upper, eye = lu_factors(square[...])
     weight = spread_weight(square[...], gains)
-    field = grads[ROW_SMALL + 8 : ROWS, 128:256]
+    field = grads[ROW_SMALL:ROWS, 128:256]
     lane = iota((16, 128), 1)
     level = jnp.sum(jnp.where(lane == 12, field, 0.0), axis=1, keepdims=True)
     real = iota((16, 128), 0) & 7
@@ -463,24 +532,21 @@
     d_lu = jnp.where((row < 12) & (col < 12), d_lu, 0.0)
     diag = jnp.sum(jnp.sum(jnp.where(eye, square[...], 0.0), axis=0, keepdims=True), axis=1, keepdims=True)
     logs = jnp.sum(jnp.where(lane[0:1] < 12, gains[1:2], 0.0), axis=1, keepdims=True)
-    d_bias_out = grads[ROW_SMALL + 8 : ROW_SMALL + 9, 256:384]
+    d_bias_out = grads[ROW_SMALL : ROW_SMALL + 1, 256:384]
     row8 = iota((8, 128), 0)
     d_gains = jnp.where(row8 == 0, d_shift, jnp.where(row8 == 1, d_scale, jnp.where(row8 == 2, d_bias_out, 0.0)))
     d_gains = jnp.where(iota((8, 128), 1) < 12, d_gains, 0.0)
     for tap in range(9):
-        dy, dx = tap // 3, tap % 3
-        gin[tap] = grads[ROW_IN + dy * 32 + dx * 8 : ROW_IN + dy * 32 + dx * 8 + 6, :]
-        at = ROW_OUT + tap * 16
-        gout[tap, 0:6, :] = grads[at : at + 6, :]
-        gout[tap, 6:12, :] = grads[at + 8 : at + 14, :]
+        gin[tap] = grads[ROW_IN + 6 * tap : ROW_IN + 6 * tap + 6, :]
+        gout[tap] = grads[ROW_OUT + 12 * tap : ROW_OUT + 12 * tap + 12, :]
     for k in range(4):
         flat[72 * k : 72 * k + 72, :] = grads[ROW_PRIOR:ROW_SMALL, 128 * k : 128 * k + 128]
     out_map = prior_out_map()
     d_prior = dot(dot(prior_in_map(), flat[...], TN, HIGH)[:, 0:64], out_map, NT, HIGH)
-    d_table = grads[ROW_SMALL + 8 : ROWS, 0:128]
+    d_table = grads[ROW_SMALL:ROWS, 0:128]
     d_table = [dot(d_table[:, 0:64], out_map, NT, HIGH), dot(d_table[:, 64:128], out_map, NT, HIGH)]
     d_table = [part[0:10] for part in d_table]
-    d_bias = [grads[ROW_IN + 46 : ROW_IN + 47, :], grads[ROW_SMALL : ROW_SMALL + 1, :]]
+    d_bias = [grads[ROW_BIAS : ROW_BIAS + 1, :], grads[ROW_BIAS + 1 : ROW_BIAS + 2, :]]
     d_mix = grads[0:ROW_OUT, :]
 
     def squares(value):
@@ -496,7 +562,7 @@
     factor = jnp.minimum(1.0, CLIP_NORM / (total_norm + 1e-06))
     norm[...] = total_norm
     loss[...] = (
-        grads[ROW_SMALL + 16 : ROW_SMALL + 17, 256:257] - coef * (logs + diag) + BITS * share / 10.0
+        grads[ROW_SMALL + 8 : ROW_SMALL + 9, 256:257] - coef * (logs + diag) + BITS * share / 10.0
     )
 
     def put(k, grad, at=Ellipsis):
@@ -518,6 +584,14 @@
     return jax.ShapeDtypeStruct(dims, dtype)
 
 
+def near(dims, dtype=F32):
+    return pltpu.HBM(dims, dtype)
+
+
+def far(array):
+    return pltpu.with_memory_space_constraint(array, pltpu.HBM)
+
+
 def params_of(limit):
     return pltpu.CompilerParams(vmem_limit_bytes=limit * MIB)
 
@@ -544,24 +618,28 @@
         images[:, :2] + noise[:, :2], images[:, rows - 2 :] + noise[:, rows - 2 :]
     )
     flags = jnp.stack([band > 0, band < bands - 1]).astype(F32)
+    dp = lax.axis_index("dp")
+    place = jnp.stack([dp & 1, dp >> 1, band]).astype(jnp.int32)
+    smem = pl.BlockSpec(memory_space=pltpu.SMEM)
     hits = (labels[None, :] == jnp.arange(16, dtype=jnp.int32)[:, None]).astype(F32)
-    counts = lax.psum(jnp.sum(hits, axis=1), "dp")
-    counts = jnp.broadcast_to(counts[:, None], (16, 128))
+    groups = lax.axis_size("dp")
+    counts = jnp.broadcast_to(jnp.sum(hits, axis=1)[None, :, None], (groups, 16, 128))
+    counts = jnp.sum(lax.all_to_all(counts, "dp", 0, 0, tiled=True), axis=0)
 
     win, wt, mixh, mixth, bias2, wout, woutt, weff, wpt, wp, tablep = pl.pallas_call(
         weights_kernel,
         out_shape=(
-            shape((hidden, 128), BF16),
-            shape((128, hidden)),
-            shape((hidden, hidden), BF16),
-            shape((hidden, hidden), BF16),
-            shape((hidden, 128)),
-            shape((144, hidden), BF16),
-            shape((hidden, 256), BF16),
-            shape((16, 128)),
-            shape((288, 256), BF16),
-            shape((128, 384), BF16),
-            shape((16, 128)),
+            near((hidden, 128), BF16),
+            near((128, hidden)),
+            near((hidden, hidden), BF16),
+            near((hidden, hidden), BF16),
+            near((hidden, 128)),
+            near((144, hidden), BF16),
+            near((hidden, 256), BF16),
+            near((16, 128)),
+            near((288, 256), BF16),
+            near((128, 384), BF16),
+            near((16, 128)),
         ),
         in_specs=[whole] * 8,
         out_specs=(whole,) * 11,
@@ -570,57 +648,42 @@
             pltpu.VMEM((128, 128), F32),
             pltpu.VMEM((8, 128), F32),
         ],
-        compiler_params=params_of(40),
+        compiler_params=params_of(26),
         name="weights",
-    )(*params)
-
-    cols, sub = 4, 2
+    )(*[far(p) for p in params])
+
+    cols, sub = 4, 4
     groups = width // cols
     steps = rows * groups
     size = cols * count
-    full = lambda dims: pl.BlockSpec(dims, lambda i: (0,) * len(dims))
     chunk = pl.BlockSpec((1, hidden, size), lambda i: (i, 0, 0))
     ext = (rows + 4, width + 2, 16, count)
     exta = (rows + 4, width + 4, 8, count)
     act1, sg1, act2, sg2, xa2, xt, xaf, xbf, nn, edge_top, edge_bottom = pl.pallas_call(
         functools.partial(forward_kernel, cols, sub),
         grid=(steps,),
-        out_shape=(shape((steps, hidden, size), BF16),) * 4
+        out_shape=(pltpu.HBM((steps, hidden, size), BF16),) * 4
         + (
-            shape(ext, BF16),
-            shape(ext, BF16),
-            shape(exta),
-            shape((rows, width, 8, count)),
-            shape((rows, width, 16, count)),
-            shape((width, 16, count), BF16),
-            shape((width, 16, count), BF16),
+            near(ext, BF16),
+            near(ext, BF16),
+            near(exta),
+            near((rows, width, 8, count)),
+            near((rows, width, 16, count)),
+            near((width, 16, count), BF16),
+            near((width, 16, count), BF16),
         ),
-        in_specs=[full(images.shape)] * 2
-        + [full(top.shape)] * 2
-        + [pl.BlockSpec(memory_space=pltpu.SMEM)]
-        + [full(a.shape) for a in (weff, win, mixh, bias2, wout)],
-        out_specs=(chunk,) * 4
-        + (
-            full(ext),
-            full(ext),
-            full(exta),
-            full((rows, width, 8, count)),
-            full((rows, width, 16, count)),
-            full((width, 16, count)),
-            full((width, 16, count)),
-        ),
+        in_specs=[whole] * 4 + [smem] + [whole] * 5,
+        out_specs=(chunk,) * 4 + (whole,) * 7,
         scratch_shapes=[
             pltpu.VMEM((chans, rows + 4, width, count), F32),
             pltpu.VMEM((128, size), BF16),
             pltpu.VMEM((rows + 2, width + 2, 16, count), F32),
         ],
-        compiler_params=params_of(56),
+        compiler_params=params_of(26),
         name="forward",
-    )(images, noise, top, bottom, flags, weff, win, mixh, bias2, wout)
-
-    got_top, got_bottom = exchange_rows(edge_top, edge_bottom)
-    nn = nn.at[0].add(got_top.astype(F32))
-    nn = nn.at[rows - 1].add(got_bottom.astype(F32))
+    )(*map(far, (images, noise, top, bottom)), flags, *map(far, (weff, win, mixh, bias2, wout)))
+
+    edge_top, edge_bottom = exchange_rows(edge_top, edge_bottom)
     gain3 = params[5][2]
     zero = jnp.zeros((2,), F32)
     net_bias = jnp.concatenate([gain3[:6], zero, gain3[6:] + 2.0, zero])[:, None]
@@ -628,9 +691,9 @@
     dn, dprior, small = pl.pallas_call(
         coupling_kernel,
         out_shape=(
-            shape((rows, width, 16, count), BF16),
-            shape((288, 128)),
-            shape((24, 512)),
+            near((rows, width, 16, count), BF16),
+            near((288, 128)),
+            near((16, 512)),
         ),
         in_specs=[whole] * 12,
         out_specs=(whole,) * 3,
@@ -647,45 +710,85 @@
             pltpu.VMEM((16, count), F32),
             pltpu.VMEM((128, count), F32),
         ],
-        compiler_params=params_of(48),
+        compiler_params=params_of(26),
         name="coupling",
-    )(nn, edge_top, edge_bottom, xaf, xbf, xt, labels[None, :], counts, wp, wpt, tablep, net_bias)
+    )(*map(far, (nn, edge_top, edge_bottom, xaf, xbf, xt, labels[None, :], counts, wp, wpt, tablep, net_bias)))
 
     dn_top, dn_bottom = exchange_rows(dn[0], dn[rows - 1])
-    packed = pl.pallas_call(
+    both = ("dp", "band")
+    devices = lax.axis_size(both)
+    each = -(-ROWS // devices)
+    half_shape = (devices // 2, each, hidden)
+    keep, send = pl.pallas_call(
         functools.partial(backward_kernel, cols, sub),
         grid=(steps,),
-        out_shape=shape((ROWS, hidden)),
-        in_specs=[chunk] * 4
-        + [full(a.shape) for a in (dn, dn_top, dn_bottom, xa2, xt, mixth, woutt, wt, dprior, small)],
-        out_specs=full((ROWS, hidden)),
+        out_shape=(near(half_shape),) * 2,
+        in_specs=[chunk] * 4 + [smem] + [whole] * 10,
+        out_specs=(whole,) * 2,
         scratch_shapes=[
+            pltpu.VMEM((devices * each, hidden), F32),
             pltpu.VMEM((rows + 2, width + 2, 16, count), BF16),
             pltpu.VMEM((256, size), BF16),
             pltpu.VMEM((256, size), BF16),
             pltpu.VMEM((hidden, 128), F32),
             pltpu.VMEM((144, hidden), F32),
+            pltpu.VMEM((144, hidden), F32),
+            pltpu.VMEM((96, hidden), F32),
         ],
-        compiler_params=params_of(56),
+        compiler_params=params_of(26),
         name="backward",
-    )(act1, sg1, act2, sg2, dn, dn_top, dn_bottom, xa2, xt, mixth, woutt, wt, dprior, small)
-
-    both = ("dp", "band")
-    devices = lax.axis_size(both)
-    lanes = ROWS * hidden // 128
-    per = -(-lanes // devices)
-    flat = jnp.pad(packed.reshape(lanes, 128), ((0, per * devices - lanes), (0, 0)))
-    parts = lax.all_to_all(flat.reshape(devices, per, 128), both, 0, 0, tiled=True)
-    mine = jnp.sum(parts, axis=0)
-    spread = jnp.broadcast_to(mine[None], (devices, per, 128))
-    grads = lax.all_to_all(spread, both, 0, 0, tiled=True)
-    grads = grads.reshape(devices * per, 128)[:lanes].reshape(ROWS, hidden)
+    )(*map(far, (act1, sg1, act2, sg2)), place, *map(far, (dn, dn_top, dn_bottom, xa2, xt, mixth, woutt, wt, dprior, small)))
+
+    def call(kernel, name, outs, *inputs):
+        return pl.pallas_call(
+            kernel,
+            out_shape=outs,
+            in_specs=[smem if a is place else whole for a in inputs],
+            out_specs=jax.tree.map(lambda _: whole, outs),
+            compiler_params=params_of(26),
+            name=name,
+        )(*inputs)
+
+    def swap(array, mask):
+        pairs = [(i, i ^ mask) for i in range(groups_dp)]
+        return lax.ppermute(array, "dp", pairs)
+
+    def turn(array, k):
+        return lax.ppermute(array, "band", [(i, (i + k) % bands) for i in range(bands)])
+
+    groups_dp = lax.axis_size("dp")
+    chips = groups_dp // 2
+    got = swap(send, 1)
+    block = shape((bands, each, hidden))
+    tile = shape((each, hidden))
+    mine, *sends = call(halve_kernel, "halve", (block,) * chips, place, keep, got)
+    gots = [swap(a, 2 * (m + 1)) for m, a in enumerate(sends)]
+    mine, *sends = call(
+        lambda p, *refs: spread_kernel(p, bands, *refs), "spread", (tile,) * bands, place, mine, *gots
+    )
+    gots = [turn(a, k + 1) for k, a in enumerate(sends)]
+    mine = call(sum_kernel, "total", tile, mine, *gots)
+    gots = [turn(mine, k + 1) for k in range(bands - 1)]
+    mine = call(
+        lambda p, *refs: gather_kernel(p, 2, False, *refs), "gather_band", block, place, mine, *gots
+    )
+    gots = [swap(mine, 2 * (m + 1)) for m in range(chips - 1)]
+    mine = call(
+        lambda p, *refs: gather_kernel(p, 1, True, *refs),
+        "gather_chips",
+        shape((chips,) + block.shape),
+        place,
+        mine,
+        *gots,
+    )
+    mine = mine.reshape(half_shape)
+    other = swap(mine, 1)
 
     area = float(width * width)
     results = pl.pallas_call(
         functools.partial(update_kernel, area, 12.0 * width * width),
         out_shape=(shape((1, 1)), shape((1, 1))) + tuple(shape(p.shape) for p in params) * 3,
-        in_specs=[whole] * 26,
+        in_specs=[smem] + [whole] * 27,
         out_specs=(whole,) * 26,
         scratch_shapes=[
             pltpu.VMEM((128, 128), F32),
@@ -693,10 +796,11 @@
             pltpu.VMEM((9, 6, hidden), F32),
             pltpu.VMEM((9, 12, hidden), F32),
             pltpu.VMEM((288, 128), F32),
+            pltpu.VMEM((devices * each, hidden), F32),
         ],
-        compiler_params=params_of(48),
+        compiler_params=params_of(26),
         name="update",
-    )(grads, counts, *params, *firsts, *seconds)
+    )(place, mine, other, counts, *params, *firsts, *seconds)
     outs = [results[0][0, 0], results[1][0, 0]]
     for k in range(3):
         group = list(results[2 + 8 * k : 10 + 8 * k])

time: 269 us -> 188 us (0.70)
  blocking collectives: 104 us -> 0 us
  waiting for transfers between devices: 13.3 us -> 36.5 us
  local copies, waits for them, and re-layouts: 25.3 us -> 5.75 us
  starting transfers between devices: 15.9 us -> 35.3 us
  Pallas kernels: 100 us -> 104 us
  other arithmetic: 7.44 us -> 3.98 us
    all_to_all x2 -> x0, blocking collectives: 91.9 us -> none  [the longest x1 46.3 us: body(): grads = lax.all_to_all(spread, both, 0, 0, tiled=True)]
    ppermute x0 -> x14, waiting for transfers between devices: none -> 25.7 us  [the longest x8 19.5 us: swap(): return lax.ppermute(array, 'dp', pairs)]
    ppermute x0 -> x14, starting transfers between devices: none -> 15.7 us  [the longest x6 8.5 us: turn(): lax.ppermute(array, 'band', [(i, (i + k) % bands) for i in range(bands)])]
    unnamed x92 -> x64, local copies, waits for them, and re-layouts: 19 us -> 3.37 us
    psum x1 -> x0, blocking collectives: 12.2 us -> none  [body(): counts = lax.psum(jnp.sum(hits, axis=1), 'dp')]
    pallas_call x2 -> x7, Pallas kernels: 8.35 us -> 16.3 us  [the longest x1 9.85 us: body(): pl.pallas_call(coupling_kernel, out_shape=(near((rows, width, 16, count),...]
    all_to_all x0 -> x1, starting transfers between devices: none -> 3.72 us  [body(): counts = jnp.sum(lax.all_to_all(counts, 'dp', 0, 0, tiled=True), axis=0)]
    scatter-add x2 -> x0, other arithmetic: 3.37 us -> none  [the longest x1 1.69 us: body(): nn = nn.at[0].add(got_top.astype(F32))]
  transfers between devices with their start and end apart: 6 -> 21, of which waited for: 4 -> 15; matrix products, arithmetic and copies ran while one was open for 1% -> 2% of each run, Pallas kernels for 1% -> 23%
where the time goes in v2:
time: 188 us; the launch traced here: 187 us
  Pallas kernels  104 us (55%)
  waiting for transfers between devices  36.5 us (19%)
  starting transfers between devices  35.3 us (19%)
  local copies, waits for them, and re-layouts  5.75 us (3%)
  other arithmetic  3.98 us (2%)
    pallas_call x1, Pallas kernels, body(): pl.pallas_call(functools.partial(backward_kernel, cols, sub), grid=(steps...  42.4 us
    pallas_call x1, Pallas kernels, body(): pl.pallas_call(functools.partial(forward_kernel, cols, sub), grid=(steps,...  38.2 us
    ppermute x8, waiting for transfers between devices, swap(): return lax.ppermute(array, 'dp', pairs)  19.5 us
    ppermute x3, starting transfers between devices, exchange_rows(): before = lax.ppermute(down, 'band', [(i, i + 1) for i in range(count - 1)])  11.9 us
    pallas_call x1, Pallas kernels, body(): pl.pallas_call(coupling_kernel, out_shape=(near((rows, width, 16, count),...  9.85 us
    ppermute x3, waiting for transfers between devices, exchange_rows(): after = lax.ppermute(up, 'band', [(i + 1, i) for i in range(count - 1)])  9.8 us
    ppermute x6, starting transfers between devices, turn(): lax.ppermute(array, 'band', [(i, (i + k) % bands) for i in range(bands)])  8.5 us
    pallas_call x1, Pallas kernels, body(): pl.pallas_call(functools.partial(update_kernel, area, 12.0 * width * widt...  7.3 us
  transfers between devices with their start and end apart: 21, of which 15 were waited for; matrix products, arithmetic and copies ran while one was open for 2% of the time, Pallas kernels for 23%

profile of v2, /device:TPU:0, one launch (start us, length us, event | category | flops | bytes accessed | tf_op | source)
XLA Modules:
  0.0 187.0 jit_solution(1915124961859254329)
XLA Ops:
  0.7 1.5 slice_add_fusion
  2.2 5.0 %collective-permute-start = (f32[12,2,16,256]{3,2,1,0:T(8,128)S(1)}, f32[12,2,16,256]{3,2,1,0:T(8,128)S(1)}, u32[]{:S(2)}, u32[]{:S(2)}) collective-permute-start(f32[12,2,16,256]{3,2,1,0:T(8,128)S(1)} %get-tuple-element.149), channel_id=1, source_target_pairs={{0,1},{1,2},{2,3},{4,5},{5,6},{6,7},{8,9},{9,10},{10,11},{12,13},{... | collective-permute-start | bytes 1179656 | tf_op jit(solution)/shard_map/ppermute | solution.py:601
  7.1 1.3 collective-permute-start.1
  8.4 0.8 convert_reduce_fusion
  9.2 0.7 broadcast_in_dim.7
  9.9 3.7 %all-to-all-start = ((f32[8,16,128]{2,1,0:T(8,128)}), f32[8,16,128]{2,1,0:T(8,128)S(1)}, u32[]{:S(2)}, u32[]{:S(2)}) async-start(f32[8,16,128]{2,1,0:T(8,128)} %broadcast_in_dim.7), calls=%async_computation | async-start | bytes 131072 | tf_op jit(solution)/shard_map/all_to_all | solution.py:627
  13.7 4.0 %weights.1 = (bf16[512,128]{1,0:T(8,128)(2,1)}, f32[128,512]{1,0:T(8,128)}, bf16[512,512]{1,0:T(8,128)(2,1)}, bf16[512,512]{1,0:T(8,128)(2,1)}, f32[512,128]{1,0...) custom-call(f32[9,6,512]{2,1,0:T(8,128)} %bitcast.33, ...), custom_call_target="tpu_custom_call" | custom-call | tf_op jit(solution)/shard_map/weights/pallas_call | solution.py:629
  17.8 1.9 collective-permute-done.1.bottom
  19.6 0.8 copy-done.27
  20.4 38.2 %forward.1 = (bf16[16,512,1024]{2,1,0:T(8,128)(2,1)}, bf16[16,512,1024]{2,1,0:T(8,128)(2,1)}, bf16[16,512,1024]{2,1,0:T(8,128)(2,1)}, bf16[16,512,1024]{2,1,0:T(...) custom-call(f32[12,4,16,256]{3,2,1,0:T(8,128)} %images.1, ...), custom_call_target="tpu_custom_call" | custom-call | tf_op jit(solution)/shard_map/forward/pallas_call | solution.py:662
  58.6 3.5 %collective-permute-start.2 = (bf16[16,16,256]{2,1,0:T(8,128)(2,1)}, bf16[16,16,256]{2,1,0:T(8,128)(2,1)S(1)}, u32[]{:S(2)}, u32[]{:S(2)}) collective-permute-start(bf16[16,16,256]{2,1,0:T(8,128)(2,1)} %get-tuple-element.97), channel_id=1, source_target_pairs={{0,1},{1,2},{2,3},{4,5},{5,6},{6,7},{8,9},{9,10},{10,11},{12,13},{... | collective-permute-start | bytes 393224 | tf_op jit(solution)/shard_map/ppermute | solution.py:601
  62.0 1.3 collective-permute-start.3
  63.3 0.8 slice_bitcast_fusion.2
  64.3 0.7 copy.54.net_bias_ref
  65.6 3.6 %collective-permute-done.3.edge_bottom = bf16[16,16,256]{2,1,0:T(8,128)(2,1)S(1)} collective-permute-done((bf16[16,16,256]{2,1,0:T(8,128)(2,1)}, bf16[16,16,256]{2,1,0:T(8,128)(2,1)S(1)}, u32[]{:S(2)}, u32[]{:S(2)}) %collective-permute-start.3) | collective-permute-done | bytes 131104 | tf_op jit(solution)/shard_map/ppermute | solution.py:602
  69.1 0.7 copy-done.31
  69.8 9.8 %coupling.1 = (bf16[4,16,16,256]{3,2,1,0:T(8,128)(2,1)}, f32[288,128]{1,0:T(8,128)}, f32[16,512]{1,0:T(8,128)}) custom-call(f32[4,16,16,256]{3,2,1,0:T(8,128)} %get-tuple-element.96.nn, bf16[16,16,256]{2,1,0:T(8,128)(2,1)} %copy-done.30, bf16[16,16,256]{2,1,0:T(8,128)(2,1)} %copy-done.31, f32[8,20,8,256]{3,2,1,0:T(8,128)} %get-tuple-element.99.xaf, ...), custom_call_target="tpu_custom_call" | custom-call | tf_op jit(solution)/shard_map/coupling/pallas_call | solution.py:691
  79.6 1.0 slice_bitcast_fusion
  80.6 3.5 %collective-permute-start.4 = (bf16[16,16,256]{2,1,0:T(8,128)(2,1)S(1)}, bf16[16,16,256]{2,1,0:T(8,128)(2,1)S(1)}, u32[]{:S(2)}, u32[]{:S(2)}) collective-permute-start(bf16[16,16,256]{2,1,0:T(8,128)(2,1)S(1)} %get-tuple-element.151), channel_id=1, source_target_pairs={{0,1},{1,2},{2,3},{4,5},{5,6},{6,7},{8,9},{9,10},{10,11},{12,13},{... | collective-permute-start | bytes 393224 | tf_op jit(solution)/shard_map/ppermute | solution.py:601
  84.1 1.5 collective-permute-start.5
  85.7 0.9 collective-permute-done.4.dn_top
  86.6 4.4 %collective-permute-done.5.dn_bottom = bf16[16,16,256]{2,1,0:T(8,128)(2,1)S(1)} collective-permute-done((bf16[16,16,256]{2,1,0:T(8,128)(2,1)S(1)}, bf16[16,16,256]{2,1,0:T(8,128)(2,1)S(1)}, u32[]{:S(2)}, u32[]{:S(2)}) %collective-permute-start.5) | collective-permute-done | bytes 131104 | tf_op jit(solution)/shard_map/ppermute | solution.py:602
  91.0 0.7 copy-done.29
  91.9 42.4 %backward.1 = (f32[16,24,512]{2,1,0:T(8,128)}, f32[16,24,512]{2,1,0:T(8,128)}) custom-call(bf16[16,512,1024]{2,1,0:T(8,128)(2,1)} %get-tuple-element.92.act1, bf16[16,512,1024]{2,1,0:T(8,128)(2,1)} %get-tuple-element.93.sg1, bf16[16,512,1024]{2,1,0:T(8,128)(2,1)} %get-tuple-element.94.act2, bf16[16,512,1024]{2,1,0:T(8,128)(2,1)} %get-tuple-element.95.sg2, ...), custom_call_target="tpu_custom_call" | custom-call | tf_op jit(solution)/shard_map/backward/pallas_call | solution.py:722
  134.3 2.5 %collective-permute-done.6.got = f32[16,24,512]{2,1,0:T(8,128)S(1)} collective-permute-done((f32[16,24,512]{2,1,0:T(8,128)}, f32[16,24,512]{2,1,0:T(8,128)S(1)}, u32[]{:S(2)}, u32[]{:S(2)}) %collective-permute-start.6) | collective-permute-done | bytes 786464 | tf_op jit(solution)/shard_map/ppermute | solution.py:754
  136.8 1.1 copy-done.4
  137.9 0.7 halve.1
  138.6 1.7 collective-permute-start.7
  140.3 1.5 collective-permute-start.8
  142.1 4.3 %collective-permute-done.7.refs_1_ = f32[4,24,512]{2,1,0:T(8,128)S(1)} collective-permute-done((f32[4,24,512]{2,1,0:T(8,128)S(1)}, f32[4,24,512]{2,1,0:T(8,128)S(1)}, u32[]{:S(2)}, u32[]{:S(2)}) %collective-permute-start.7) | collective-permute-done | bytes 196640 | tf_op jit(solution)/shard_map/ppermute | solution.py:754
  146.4 4.8 %collective-permute-done.8.refs_2_ = f32[4,24,512]{2,1,0:T(8,128)S(1)} collective-permute-done((f32[4,24,512]{2,1,0:T(8,128)S(1)}, f32[4,24,512]{2,1,0:T(8,128)S(1)}, u32[]{:S(2)}, u32[]{:S(2)}) %collective-permute-start.8) | collective-permute-done | bytes 196640 | tf_op jit(solution)/shard_map/ppermute | solution.py:754
  151.2 0.6 spread.1
  151.8 1.6 collective-permute-start.10
  153.4 2.4 %collective-permute-start.12 = (f32[24,512]{1,0:T(8,128)S(1)}, f32[24,512]{1,0:T(8,128)S(1)}, u32[]{:S(2)}, u32[]{:S(2)}) collective-permute-start(f32[24,512]{1,0:T(8,128)S(1)} %get-tuple-element.121), channel_id=1, source_target_pairs={{0,3},{1,0},{2,1},{3,2},{4,7},{5,4},{6,5},{7,6},{8,11},{9,8},{10,9... | collective-permute-start | bytes 147464 | tf_op jit(solution)/shard_map/ppermute | solution.py:757
  155.9 2.1 %collective-permute-done.10.refs_1_ = f32[24,512]{1,0:T(8,128)S(1)} collective-permute-done((f32[24,512]{1,0:T(8,128)S(1)}, f32[24,512]{1,0:T(8,128)S(1)}, u32[]{:S(2)}, u32[]{:S(2)}) %collective-permute-start.10) | collective-permute-done | bytes 49184 | tf_op jit(solution)/shard_map/ppermute | solution.py:757
  158.0 1.0 collective-permute-done.11.refs_2_
  159.0 1.4 collective-permute-start.13
  160.4 2.0 %collective-permute-start.14 = (f32[24,512]{1,0:T(8,128)S(1)}, f32[24,512]{1,0:T(8,128)S(1)}, u32[]{:S(2)}, u32[]{:S(2)}) collective-permute-start(f32[24,512]{1,0:T(8,128)S(1)} %total.1.refs_0_), channel_id=1, source_target_pairs={{0,2},{1,3},{2,0},{3,1},{4,6},{5,7},{6,4},{7,5},{8,10},{9,11},{10,... | collective-permute-start | bytes 147464 | tf_op jit(solution)/shard_map/ppermute | solution.py:757
  162.4 1.0 collective-permute-start.15
  163.5 1.5 collective-permute-done.13.refs_1_
  165.0 1.0 collective-permute-done.14.refs_2_
  167.1 1.5 collective-permute-start.16
  168.6 0.6 collective-permute-start.17
  169.2 1.5 collective-permute-start.18
  170.7 2.2 %collective-permute-done.16.refs_1_ = f32[4,24,512]{2,1,0:T(8,128)S(1)} collective-permute-done((f32[4,24,512]{2,1,0:T(8,128)S(1)}, f32[4,24,512]{2,1,0:T(8,128)S(1)}, u32[]{:S(2)}, u32[]{:S(2)}) %collective-permute-start.16) | collective-permute-done | bytes 196640 | tf_op jit(solution)/shard_map/ppermute | solution.py:754
  172.9 3.5 %collective-permute-done.17.refs_2_ = f32[4,24,512]{2,1,0:T(8,128)S(1)} collective-permute-done((f32[4,24,512]{2,1,0:T(8,128)S(1)}, f32[4,24,512]{2,1,0:T(8,128)S(1)}, u32[]{:S(2)}, u32[]{:S(2)}) %collective-permute-start.17) | collective-permute-done | bytes 196640 | tf_op jit(solution)/shard_map/ppermute | solution.py:754
  177.1 2.3 %collective-permute-done.19.refs_2_ = f32[16,24,512]{2,1,0:T(8,128)S(1)} collective-permute-done((f32[16,24,512]{2,1,0:T(8,128)S(1)}, f32[16,24,512]{2,1,0:T(8,128)S(1)}, u32[]{:S(2)}, u32[]{:S(2)}) %collective-permute-start.19) | collective-permute-done | bytes 786464 | tf_op jit(solution)/shard_map/ppermute | solution.py:754
  179.6 7.3 %update.1 = (f32[1,1]{1,0:T(1,128)}, f32[1,1]{1,0:T(1,128)}, f32[9,6,512]{2,1,0:T(8,128)}, f32[512,512]{1,0:T(8,128)}, f32[9,12,512]{2,1,0:T(8,128)}, /*index=5*...) custom-call(s32[3]{0:T(128)S(1)} %pad_add_fusion.place.p.refs_0_, ...), custom_call_target="tpu_custom_call" | custom-call | tf_op jit(solution)/shard_map/update/pallas_call | solution.py:788
  (79 shorter events, 3.2 us)
Async XLA Ops:
  2.2 15.6 %collective-permute-start = (f32[12,2,16,256]{3,2,1,0:T(8,128)S(1)}, f32[12,2,16,256]{3,2,1,0:T(8,128)S(1)}, u32[]{:S(2)}, u32[]{:S(2)}) collective-permute-start(f32[12,2,16,256]{3,2,1,0:T(8,128)S(1)} %get-tuple-element.149), channel_id=1, source_target_pairs={{0,1},{1,2},{2,3},{4,5},{5,6},{6,7},{8,9},{9,10},{10,11},{12,13},{... | collective-permute-start | bytes 1179656 | tf_op jit(solution)/shard_map/ppermute | solution.py:601
  7.1 12.5 %collective-permute-start.1 = (f32[12,2,16,256]{3,2,1,0:T(8,128)S(1)}, f32[12,2,16,256]{3,2,1,0:T(8,128)S(1)}, u32[]{:S(2)}, u32[]{:S(2)}) collective-permute-start(f32[12,2,16,256]{3,2,1,0:T(8,128)S(1)} %get-tuple-element.148), channel_id=1, source_target_pairs={{1,0},{2,1},{3,2},{5,4},{6,5},{7,6},{9,8},{10,9},{11,10},{13,12},{... | collective-permute-start | bytes 1179656 | tf_op jit(solution)/shard_map/ppermute | solution.py:602
  9.9 55.0 %all-to-all-start = ((f32[8,16,128]{2,1,0:T(8,128)}), f32[8,16,128]{2,1,0:T(8,128)S(1)}, u32[]{:S(2)}, u32[]{:S(2)}) async-start(f32[8,16,128]{2,1,0:T(8,128)} %broadcast_in_dim.7), calls=%async_computation | async-start | bytes 131072 | tf_op jit(solution)/shard_map/all_to_all | solution.py:627
  58.6 7.0 %collective-permute-start.2 = (bf16[16,16,256]{2,1,0:T(8,128)(2,1)}, bf16[16,16,256]{2,1,0:T(8,128)(2,1)S(1)}, u32[]{:S(2)}, u32[]{:S(2)}) collective-permute-start(bf16[16,16,256]{2,1,0:T(8,128)(2,1)} %get-tuple-element.97), channel_id=1, source_target_pairs={{0,1},{1,2},{2,3},{4,5},{5,6},{6,7},{8,9},{9,10},{10,11},{12,13},{... | collective-permute-start | bytes 393224 | tf_op jit(solution)/shard_map/ppermute | solution.py:601
  62.0 7.1 %collective-permute-start.3 = (bf16[16,16,256]{2,1,0:T(8,128)(2,1)}, bf16[16,16,256]{2,1,0:T(8,128)(2,1)S(1)}, u32[]{:S(2)}, u32[]{:S(2)}) collective-permute-start(bf16[16,16,256]{2,1,0:T(8,128)(2,1)} %get-tuple-element.98), channel_id=1, source_target_pairs={{1,0},{2,1},{3,2},{5,4},{6,5},{7,6},{9,8},{10,9},{11,10},{13,12},{... | collective-permute-start | bytes 393224 | tf_op jit(solution)/shard_map/ppermute | solution.py:602
  65.6 3.6 %copy-start.30 = (bf16[16,16,256]{2,1,0:T(8,128)(2,1)}, bf16[16,16,256]{2,1,0:T(8,128)(2,1)S(1)}, u32[]{:S(2)}) copy-start(bf16[16,16,256]{2,1,0:T(8,128)(2,1)S(1)} %collective-permute-done.2.edge_top) | copy-start | bytes 393220
  80.6 6.0 %collective-permute-start.4 = (bf16[16,16,256]{2,1,0:T(8,128)(2,1)S(1)}, bf16[16,16,256]{2,1,0:T(8,128)(2,1)S(1)}, u32[]{:S(2)}, u32[]{:S(2)}) collective-permute-start(bf16[16,16,256]{2,1,0:T(8,128)(2,1)S(1)} %get-tuple-element.151), channel_id=1, source_target_pairs={{0,1},{1,2},{2,3},{4,5},{5,6},{6,7},{8,9},{9,10},{10,11},{12,13},{... | collective-permute-start | bytes 393224 | tf_op jit(solution)/shard_map/ppermute | solution.py:601
  84.1 6.9 %collective-permute-start.5 = (bf16[16,16,256]{2,1,0:T(8,128)(2,1)S(1)}, bf16[16,16,256]{2,1,0:T(8,128)(2,1)S(1)}, u32[]{:S(2)}, u32[]{:S(2)}) collective-permute-start(bf16[16,16,256]{2,1,0:T(8,128)(2,1)S(1)} %get-tuple-element.150), channel_id=1, source_target_pairs={{1,0},{2,1},{3,2},{5,4},{6,5},{7,6},{9,8},{10,9},{11,10},{13,12},{... | collective-permute-start | bytes 393224 | tf_op jit(solution)/shard_map/ppermute | solution.py:602
  86.6 4.4 %copy-start.28 = (bf16[16,16,256]{2,1,0:T(8,128)(2,1)}, bf16[16,16,256]{2,1,0:T(8,128)(2,1)S(1)}, u32[]{:S(2)}) copy-start(bf16[16,16,256]{2,1,0:T(8,128)(2,1)S(1)} %collective-permute-done.4.dn_top) | copy-start | bytes 393220
  91.6 87.7 %copy-start = (f32[512,512]{1,0:T(8,128)S(1)}, f32[512,512]{1,0:T(8,128)}, u32[]{:S(2)}) copy-start(f32[512,512]{1,0:T(8,128)} %refs_5_.1) | copy-start | bytes 3145732
  91.6 87.7 %copy-start.1 = (f32[9,12,512]{2,1,0:T(8,128)S(1)}, f32[9,12,512]{2,1,0:T(8,128)}, u32[]{:S(2)}) copy-start(f32[9,12,512]{2,1,0:T(8,128)} %refs_6_.1) | copy-start | bytes 663556
  91.6 87.7 %copy-start.2 = (f32[512,512]{1,0:T(8,128)S(1)}, f32[512,512]{1,0:T(8,128)}, u32[]{:S(2)}) copy-start(f32[512,512]{1,0:T(8,128)} %refs_13_.1) | copy-start | bytes 3145732
  91.6 87.7 %copy-start.3 = (f32[512,512]{1,0:T(8,128)S(1)}, f32[512,512]{1,0:T(8,128)}, u32[]{:S(2)}) copy-start(f32[512,512]{1,0:T(8,128)} %refs_21_.1) | copy-start | bytes 3145732
  91.6 87.7 %copy-start.5 = (f32[9,512,6]{1,2,0:T(8,128)S(1)}, f32[9,512,6]{1,2,0:T(8,128)}, u32[]{:S(2)}) copy-start(f32[9,512,6]{1,2,0:T(8,128)} %param.30) | copy-start | bytes 331780
  91.6 87.7 %copy-start.6 = (f32[9,48,24]{1,2,0:T(8,128)S(1)}, f32[9,48,24]{1,2,0:T(8,128)}, u32[]{:S(2)}) copy-start(f32[9,48,24]{1,2,0:T(8,128)} %param.33) | copy-start | bytes 124420
  91.6 87.7 %copy-start.7 = (f32[9,12,512]{2,1,0:T(8,128)S(1)}, f32[9,12,512]{2,1,0:T(8,128)}, u32[]{:S(2)}) copy-start(f32[9,12,512]{2,1,0:T(8,128)} %refs_14_.1) | copy-start | bytes 663556
  91.7 87.7 %copy-start.8 = (f32[9,12,512]{2,1,0:T(8,128)S(1)}, f32[9,12,512]{2,1,0:T(8,128)}, u32[]{:S(2)}) copy-start(f32[9,12,512]{2,1,0:T(8,128)} %refs_22_.1) | copy-start | bytes 663556
  91.7 87.7 %copy-start.9 = (f32[9,512,6]{1,2,0:T(8,128)S(1)}, f32[9,512,6]{1,2,0:T(8,128)}, u32[]{:S(2)}) copy-start(f32[9,512,6]{1,2,0:T(8,128)} %param.38) | copy-start | bytes 331780
  91.7 87.7 %copy-start.10 = (f32[9,512,6]{1,2,0:T(8,128)S(1)}, f32[9,512,6]{1,2,0:T(8,128)}, u32[]{:S(2)}) copy-start(f32[9,512,6]{1,2,0:T(8,128)} %param.46) | copy-start | bytes 331780
  91.7 87.7 %copy-start.11 = (f32[9,48,24]{1,2,0:T(8,128)S(1)}, f32[9,48,24]{1,2,0:T(8,128)}, u32[]{:S(2)}) copy-start(f32[9,48,24]{1,2,0:T(8,128)} %param.41) | copy-start | bytes 124420
  91.7 87.7 %copy-start.12 = (f32[9,48,24]{1,2,0:T(8,128)S(1)}, f32[9,48,24]{1,2,0:T(8,128)}, u32[]{:S(2)}) copy-start(f32[9,48,24]{1,2,0:T(8,128)} %param.49) | copy-start | bytes 124420
  91.7 87.7 %copy-start.13 = (f32[16,128]{1,0:T(8,128)S(1)}, f32[16,128]{1,0:T(8,128)}, u32[]{:S(2)}) copy-start(f32[16,128]{1,0:T(8,128)} %reduce_sum.19.counts.refs_3_) | copy-start | bytes 24580
  91.7 87.7 %copy-start.14 = (f32[12,12]{1,0:T(8,128)S(1)}, f32[12,12]{1,0:T(8,128)}, u32[]{:S(2)}) copy-start(f32[12,12]{1,0:T(8,128)} %refs_10_.1) | copy-start | bytes 1732
  91.7 87.7 %copy-start.15 = (f32[10,96]{1,0:T(8,128)S(1)}, f32[10,96]{1,0:T(8,128)}, u32[]{:S(2)}) copy-start(f32[10,96]{1,0:T(8,128)} %refs_11_.1) | copy-start | bytes 11524
  91.8 87.7 %copy-start.16 = (f32[2,512]{1,0:T(2,128)S(1)}, f32[2,512]{1,0:T(2,128)}, u32[]{:S(2)}) copy-start(f32[2,512]{1,0:T(2,128)} %refs_8_.1) | copy-start | bytes 12292
  91.8 87.7 %copy-start.17 = (f32[3,12]{1,0:T(4,128)S(1)}, f32[3,12]{1,0:T(4,128)}, u32[]{:S(2)}) copy-start(f32[3,12]{1,0:T(4,128)} %refs_9_.1) | copy-start | bytes 436
  91.8 87.7 %copy-start.18 = (f32[12,12]{1,0:T(8,128)S(1)}, f32[12,12]{1,0:T(8,128)}, u32[]{:S(2)}) copy-start(f32[12,12]{1,0:T(8,128)} %refs_18_.1) | copy-start | bytes 1732
  91.8 87.7 %copy-start.19 = (f32[10,96]{1,0:T(8,128)S(1)}, f32[10,96]{1,0:T(8,128)}, u32[]{:S(2)}) copy-start(f32[10,96]{1,0:T(8,128)} %refs_19_.1) | copy-start | bytes 11524
  91.8 87.7 %copy-start.20 = (f32[12,12]{1,0:T(8,128)S(1)}, f32[12,12]{1,0:T(8,128)}, u32[]{:S(2)}) copy-start(f32[12,12]{1,0:T(8,128)} %refs_26_.1) | copy-start | bytes 1732
  91.8 87.7 %copy-start.21 = (f32[10,96]{1,0:T(8,128)S(1)}, f32[10,96]{1,0:T(8,128)}, u32[]{:S(2)}) copy-start(f32[10,96]{1,0:T(8,128)} %refs_27_.1) | copy-start | bytes 11524
  91.8 87.7 %copy-start.22 = (f32[2,512]{1,0:T(2,128)S(1)}, f32[2,512]{1,0:T(2,128)}, u32[]{:S(2)}) copy-start(f32[2,512]{1,0:T(2,128)} %refs_16_.1) | copy-start | bytes 12292
  91.8 87.7 %copy-start.23 = (f32[2,512]{1,0:T(2,128)S(1)}, f32[2,512]{1,0:T(2,128)}, u32[]{:S(2)}) copy-start(f32[2,512]{1,0:T(2,128)} %refs_24_.1) | copy-start | bytes 12292
  91.9 87.7 %copy-start.24 = (f32[3,12]{1,0:T(4,128)S(1)}, f32[3,12]{1,0:T(4,128)}, u32[]{:S(2)}) copy-start(f32[3,12]{1,0:T(4,128)} %refs_17_.1) | copy-start | bytes 436
  91.9 87.7 %copy-start.25 = (f32[3,12]{1,0:T(4,128)S(1)}, f32[3,12]{1,0:T(4,128)}, u32[]{:S(2)}) copy-start(f32[3,12]{1,0:T(4,128)} %refs_25_.1) | copy-start | bytes 436
  134.3 2.5 %collective-permute-start.6 = (f32[16,24,512]{2,1,0:T(8,128)}, f32[16,24,512]{2,1,0:T(8,128)S(1)}, u32[]{:S(2)}, u32[]{:S(2)}) collective-permute-start(f32[16,24,512]{2,1,0:T(8,128)} %get-tuple-element.113), channel_id=1, source_target_pairs={{0,4},{4,0},{8,12},{12,8},{16,20},{20,16},{24,28},{28,24},{1,5},{5... | collective-permute-start | bytes 2359304 | tf_op jit(solution)/shard_map/ppermute | solution.py:754
  138.6 7.8 %collective-permute-start.7 = (f32[4,24,512]{2,1,0:T(8,128)S(1)}, f32[4,24,512]{2,1,0:T(8,128)S(1)}, u32[]{:S(2)}, u32[]{:S(2)}) collective-permute-start(f32[4,24,512]{2,1,0:T(8,128)S(1)} %get-tuple-element.115), channel_id=1, source_target_pairs={{0,8},{4,12},{8,0},{12,4},{16,24},{20,28},{24,16},{28,20},{1,9},{5... | collective-permute-start | bytes 589832 | tf_op jit(solution)/shard_map/ppermute | solution.py:754
  140.3 10.9 %collective-permute-start.8 = (f32[4,24,512]{2,1,0:T(8,128)S(1)}, f32[4,24,512]{2,1,0:T(8,128)S(1)}, u32[]{:S(2)}, u32[]{:S(2)}) collective-permute-start(f32[4,24,512]{2,1,0:T(8,128)S(1)} %get-tuple-element.116), channel_id=1, source_target_pairs={{0,16},{4,20},{8,24},{12,28},{16,0},{20,4},{24,8},{28,12},{1,17},{... | collective-permute-start | bytes 589832 | tf_op jit(solution)/shard_map/ppermute | solution.py:754
  141.8 9.4 %collective-permute-start.9 = (f32[4,24,512]{2,1,0:T(8,128)S(1)}, f32[4,24,512]{2,1,0:T(8,128)S(1)}, u32[]{:S(2)}, u32[]{:S(2)}) collective-permute-start(f32[4,24,512]{2,1,0:T(8,128)S(1)} %get-tuple-element.117), channel_id=1, source_target_pairs={{0,24},{4,28},{8,16},{12,20},{16,8},{20,12},{24,0},{28,4},{1,25},{... | collective-permute-start | bytes 589832 | tf_op jit(solution)/shard_map/ppermute | solution.py:754
  151.8 6.2 %collective-permute-start.10 = (f32[24,512]{1,0:T(8,128)S(1)}, f32[24,512]{1,0:T(8,128)S(1)}, u32[]{:S(2)}, u32[]{:S(2)}) collective-permute-start(f32[24,512]{1,0:T(8,128)S(1)} %get-tuple-element.119), channel_id=1, source_target_pairs={{0,1},{1,2},{2,3},{3,0},{4,5},{5,6},{6,7},{7,4},{8,9},{9,10},{10,1... | collective-permute-start | bytes 147464 | tf_op jit(solution)/shard_map/ppermute | solution.py:757
  153.4 5.6 %collective-permute-start.11 = (f32[24,512]{1,0:T(8,128)S(1)}, f32[24,512]{1,0:T(8,128)S(1)}, u32[]{:S(2)}, u32[]{:S(2)}) collective-permute-start(f32[24,512]{1,0:T(8,128)S(1)} %get-tuple-element.120), channel_id=1, source_target_pairs={{0,2},{1,3},{2,0},{3,1},{4,6},{5,7},{6,4},{7,5},{8,10},{9,11},{10,... | collective-permute-start | bytes 147464 | tf_op jit(solution)/shard_map/ppermute | solution.py:757
  153.4 5.6 %collective-permute-start.12 = (f32[24,512]{1,0:T(8,128)S(1)}, f32[24,512]{1,0:T(8,128)S(1)}, u32[]{:S(2)}, u32[]{:S(2)}) collective-permute-start(f32[24,512]{1,0:T(8,128)S(1)} %get-tuple-element.121), channel_id=1, source_target_pairs={{0,3},{1,0},{2,1},{3,2},{4,7},{5,4},{6,5},{7,6},{8,11},{9,8},{10,9... | collective-permute-start | bytes 147464 | tf_op jit(solution)/shard_map/ppermute | solution.py:757
  159.0 5.9 %collective-permute-start.13 = (f32[24,512]{1,0:T(8,128)S(1)}, f32[24,512]{1,0:T(8,128)S(1)}, u32[]{:S(2)}, u32[]{:S(2)}) collective-permute-start(f32[24,512]{1,0:T(8,128)S(1)} %total.1.refs_0_), channel_id=1, source_target_pairs={{0,1},{1,2},{2,3},{3,0},{4,5},{5,6},{6,7},{7,4},{8,9},{9,10},{10,1... | collective-permute-start | bytes 147464 | tf_op jit(solution)/shard_map/ppermute | solution.py:757
  160.4 5.6 %collective-permute-start.14 = (f32[24,512]{1,0:T(8,128)S(1)}, f32[24,512]{1,0:T(8,128)S(1)}, u32[]{:S(2)}, u32[]{:S(2)}) collective-permute-start(f32[24,512]{1,0:T(8,128)S(1)} %total.1.refs_0_), channel_id=1, source_target_pairs={{0,2},{1,3},{2,0},{3,1},{4,6},{5,7},{6,4},{7,5},{8,10},{9,11},{10,... | collective-permute-start | bytes 147464 | tf_op jit(solution)/shard_map/ppermute | solution.py:757
  162.4 4.1 %collective-permute-start.15 = (f32[24,512]{1,0:T(8,128)S(1)}, f32[24,512]{1,0:T(8,128)S(1)}, u32[]{:S(2)}, u32[]{:S(2)}) collective-permute-start(f32[24,512]{1,0:T(8,128)S(1)} %total.1.refs_0_), channel_id=1, source_target_pairs={{0,3},{1,0},{2,1},{3,2},{4,7},{5,4},{6,5},{7,6},{8,11},{9,8},{10,9... | collective-permute-start | bytes 147464 | tf_op jit(solution)/shard_map/ppermute | solution.py:757
  167.1 5.8 %collective-permute-start.16 = (f32[4,24,512]{2,1,0:T(8,128)S(1)}, f32[4,24,512]{2,1,0:T(8,128)S(1)}, u32[]{:S(2)}, u32[]{:S(2)}) collective-permute-start(f32[4,24,512]{2,1,0:T(8,128)S(1)} %gather_band.1.refs_0_), channel_id=1, source_target_pairs={{0,8},{4,12},{8,0},{12,4},{16,24},{20,28},{24,16},{28,20},{1,9},{5... | collective-permute-start | bytes 589832 | tf_op jit(solution)/shard_map/ppermute | solution.py:754
  168.6 7.8 %collective-permute-start.17 = (f32[4,24,512]{2,1,0:T(8,128)S(1)}, f32[4,24,512]{2,1,0:T(8,128)S(1)}, u32[]{:S(2)}, u32[]{:S(2)}) collective-permute-start(f32[4,24,512]{2,1,0:T(8,128)S(1)} %gather_band.1.refs_0_), channel_id=1, source_target_pairs={{0,16},{4,20},{8,24},{12,28},{16,0},{20,4},{24,8},{28,12},{1,17},{... | collective-permute-start | bytes 589832 | tf_op jit(solution)/shard_map/ppermute | solution.py:754
  169.2 7.2 %collective-permute-start.18 = (f32[4,24,512]{2,1,0:T(8,128)S(1)}, f32[4,24,512]{2,1,0:T(8,128)S(1)}, u32[]{:S(2)}, u32[]{:S(2)}) collective-permute-start(f32[4,24,512]{2,1,0:T(8,128)S(1)} %gather_band.1.refs_0_), channel_id=1, source_target_pairs={{0,24},{4,28},{8,16},{12,20},{16,8},{20,12},{24,0},{28,4},{1,25},{... | collective-permute-start | bytes 589832 | tf_op jit(solution)/shard_map/ppermute | solution.py:754
  177.0 2.4 %collective-permute-start.19 = (f32[16,24,512]{2,1,0:T(8,128)S(1)}, f32[16,24,512]{2,1,0:T(8,128)S(1)}, u32[]{:S(2)}, u32[]{:S(2)}) collective-permute-start(f32[16,24,512]{2,1,0:T(8,128)S(1)} %bitcast.31), channel_id=1, source_target_pairs={{0,4},{4,0},{8,12},{12,8},{16,20},{20,16},{24,28},{28,24},{1,5},{5... | collective-permute-start | bytes 2359304 | tf_op jit(solution)/shard_map/ppermute | solution.py:754
  (5 other events, 5.1 us)

commit v3 on v2

--- a/solution.py
+++ b/solution.py
@@ -22,6 +22,7 @@
 F32 = jnp.float32
 BF16 = jnp.bfloat16
 MIB = 1024 * 1024
+VMEM_MIB = 30
 NN = (((1,), (0,)), ((), ()))
 NT = (((1,), (1,)), ((), ()))
 TN = (((0,), (0,)), ((), ()))
@@ -86,7 +87,7 @@
 
 
 def weights_kernel(cin, mix, cout, prior, bias, gains, lu, table,
-                   win, wt, mixh, mixth, bias2, wout, woutt, weff, wpt, wp, tablep,
+                   win, wt, mixh, mixth, bias2, wout, woutt, weff, wpt, wp, tablep, net_bias,
                    big, square, strip):
     hidden = mix.shape[0]
     wt[...] = jnp.zeros_like(wt)
@@ -117,6 +118,8 @@
     strip[...] = jnp.zeros_like(strip)
     strip[0:3, 0:12] = gains[...]
     weff[...] = spread_weight(square[...], strip[0:8, :])
+    added = dot(half_map(), strip[...], NT, HIGH)[:, 2:3] + as_f32(iota((16, 1), 0) >= 8) * 2.0
+    net_bias[...] = jnp.broadcast_to(added, (16, 128))
     out_map = prior_out_map()
     flat = dot(prior_in_map(), dot(prior[...].reshape(216, 48), out_map, NN, HIGH), NN, HIGH)
     flat_hi = flat.astype(BF16)
@@ -136,22 +139,38 @@
 
 def hidden_unit(u):
     wide = 1.0 + jnp.tanh(u)
-    act = u * wide
-    return act.astype(BF16), (wide + act * (2.0 - wide)).astype(BF16)
-
-
-def forward_kernel(cols, sub, images, noise, top, bottom, flags, weff, win, mixh, bias2, wout,
-                   act1, sg1, act2, sg2, xa2, xt, xaf, xbf, nn, edge_top, edge_bottom,
-                   xs, taps, acc):
+    act = (u * wide).astype(BF16)
+    wide = wide.astype(BF16)
+    return act, wide + act * (2.0 - wide)
+
+
+def fill_windows(xaf, r2, half, count, taps_hi, taps_lo=None):
+    for w in range(half):
+        lanes = pl.ds(w * count, count)
+        for ty in range(3):
+            for tx in range(3):
+                for dy in range(2):
+                    er, ec = 2 * r2 + 2 * ty + dy, 2 * w + 2 * tx
+                    pair = jnp.concatenate([xaf[er, ec], xaf[er, ec + 1]], axis=0)
+                    high = pair.astype(BF16)
+                    at = pl.ds((ty * 3 + tx) * 32 + dy * 16, 16)
+                    taps_hi[at, lanes] = high
+                    if taps_lo is not None:
+                        taps_lo[at, lanes] = (pair - high.astype(F32)).astype(BF16)
+
+
+def forward_kernel(cols, sub, images, noise, top, bottom, flags, weff, win, mixh, bias2, wout, wp, labels,
+                   act1, sg1, act2, sg2, xa2, xt, xaf, xbf, nn, edge_top, edge_bottom, stats,
+                   xs, taps, acc, taps_hi, taps_lo):
     step = pl.program_id(0)
     rows, width, count = images.shape[1:]
     groups = width // cols
 
     @pl.when(step == 0)
     def _():
-        xs[:, 0:2] = top[...]
+        xs[:, 0:2] = top[...].astype(F32)
         xs[:, 2 : rows + 2] = images[...] + noise[...]
-        xs[:, rows + 2 : rows + 4] = bottom[...]
+        xs[:, rows + 2 : rows + 4] = bottom[...].astype(F32)
         xaf[...] = jnp.zeros_like(xaf)
         xt[...] = jnp.zeros_like(xt)
         acc[...] = jnp.zeros_like(acc)
@@ -164,6 +183,7 @@
             own = (er >= 2) & (er < rows + 2)
             valid = jnp.where(er < 2, flags[0], jnp.where(er >= rows + 2, flags[1], 1.0))
             inner = jnp.clip(er - 2, 0, rows - 1)
+            before = jnp.zeros((8, count), F32)
             for c in range(width):
                 a, b = col_a[12], col_b[12]
                 t0 = jnp.zeros((8, count), F32)
@@ -176,19 +196,30 @@
                         t0 = jnp.where(row8 == ch, x, t0)
                     else:
                         t1 = jnp.where(row8 == ch - 8, x, t1)
-                xaf[er, c + 2] = a * valid
+                a = a * valid
+                xaf[er, c + 2] = a
+                xa2[er, c] = (jnp.concatenate([before, a], axis=0) + ones).astype(BF16)
+                before = a
                 xt[er, c + 1] = jnp.concatenate([t0, t1], axis=0).astype(BF16)
 
                 @pl.when(own)
                 def _():
                     xbf[inner, c] = b
 
-            for c in range(width + 2):
-                pair = jnp.concatenate([xaf[er, c + 1], xaf[er, c + 2]], axis=0)
-                xa2[er, c] = (pair + ones).astype(BF16)
+            last = jnp.concatenate([before, jnp.zeros((8, count), F32)], axis=0)
+            xa2[er, width] = (last + ones).astype(BF16)
+            xa2[er, width + 1] = ones.astype(BF16)
             return carry
 
         lax.fori_loop(0, rows + 4, per_row, 0)
+
+        def per_pair(r2, carry):
+            fill_windows(xaf, r2, width // 2, count, taps_hi, taps_lo)
+            main = dot(wp[:, 0:288], taps_hi[...])
+            stats[r2] = main[0:64] + main[64:128] + dot(wp[0:64, 0:288], taps_lo[...])
+            return carry
+
+        lax.fori_loop(0, rows // 2, per_pair, 0)
 
     row = step // groups
     start = (step % groups) * cols
@@ -210,13 +241,16 @@
         act2[0, :, lanes] = two
         sg2[0, :, lanes] = slope2
         out = dot(wout[...], two)
-        for i in range(sub):
-            for dy in range(3):
+        for dy in range(3):
+            for k in range(sub + 2):
+                value = None
                 for dx in range(3):
-                    r = row + 2 - dy
-                    c = start + s * sub + i + 2 - dx
-                    tap = dy * 3 + dx
-                    acc[r, c] += out[tap * 16 : tap * 16 + 16, i * count : (i + 1) * count]
+                    i = k + dx - 2
+                    if 0 <= i < sub:
+                        at = 16 * (dy * 3 + dx)
+                        part = out[at : at + 16, i * count : (i + 1) * count]
+                        value = part if value is None else value + part
+                acc[row + 2 - dy, start + s * sub + k] += value
 
     @pl.when(step == rows * groups - 1)
     def _():
@@ -225,134 +259,143 @@
         edge_bottom[...] = acc[rows + 1, 1 : width + 1].astype(BF16)
 
 
-def coupling_kernel(nn, edge_top, edge_bottom, xaf, xbf, xt, labels, counts, wp, wpt, tablep, net_bias_ref,
-                    dn, dprior, small, taps_hi, taps_lo, stats, dstats, dtaps, dxa, dxb, total,
-                    loss_acc, gain_acc, table_acc):
+def coupling_kernel(dims, nn, edge_top, edge_bottom, xbf, stats, labels, everyone, tablep, net_bias,
+                    dn, dn_first, dn_last, dstats, dxb, loss_acc, per_image, counts):
     rows, width, _, count = nn.shape
     half = width // 2
-    classes = 10
     hot = as_f32(iota((16, count), 0) == jnp.broadcast_to(labels[...], (16, count)))
-    present = jnp.maximum(counts[...], 1.0)
-    dims = 12.0 * width * width
-    scale16 = 1.0 / (classes * present * (dims * LOG_TWO))
+    seen = jnp.zeros((16, count), F32)
+    for k in range(everyone.shape[0]):
+        same = iota((16, count), 0) == jnp.broadcast_to(everyone[k : k + 1, :], (16, count))
+        seen = seen + as_f32(same)
+    number = jnp.broadcast_to(jnp.sum(seen, axis=1, keepdims=True), (16, 128))
+    counts[...] = number
+    scale16 = 1.0 / (10.0 * jnp.maximum(number, 1.0) * (dims * LOG_TWO))
     coef = jnp.sum(hot * scale16[:, 0:1], axis=0, keepdims=True)
     coef = jnp.broadcast_to(coef, (8, count))
     cls = dot(tablep[...], hot, TN, HIGH)
-    dxa[...] = jnp.zeros_like(dxa)
-    loss_acc[...] = jnp.zeros_like(loss_acc)
-    gain_acc[...] = jnp.zeros_like(gain_acc)
-    table_acc[...] = jnp.zeros_like(table_acc)
-    dprior[...] = jnp.zeros_like(dprior)
-    dstats[...] = jnp.zeros_like(dstats)
-    keep = iota((8, count), 0) < 6
-    net_bias = net_bias_ref[...]
+    per_image[0:128, :] = cls
+    per_image[128:136, :] = coef
+    per_image[136:152, :] = hot
     bias_a = jnp.broadcast_to(net_bias[0:8, 0:1], (8, count))
     bias_b = jnp.broadcast_to(net_bias[8:16, 0:1], (8, count))
-
-    def per_row(r2, carry):
-        for w in range(half):
-            lanes = pl.ds(w * count, count)
-            for ty in range(3):
-                for tx in range(3):
-                    for dy in range(2):
-                        er, ec = 2 * r2 + 2 * ty + dy, 2 * w + 2 * tx
-                        pair = jnp.concatenate([xaf[er, ec], xaf[er, ec + 1]], axis=0)
-                        high = pair.astype(BF16)
-                        at = pl.ds((ty * 3 + tx) * 32 + dy * 16, 16)
-                        taps_hi[at, lanes] = high
-                        taps_lo[at, lanes] = (pair - high.astype(F32)).astype(BF16)
-        main = dot(wp[:, 0:288], taps_hi[...])
-        stats[...] = main[0:64] + main[64:128] + dot(wp[0:64, 0:288], taps_lo[...])
+    loss = jnp.zeros((8, count), F32)
+    for r2 in range(rows // 2):
         for w in range(half):
             lanes = pl.ds(w * count, count)
             for dy in range(2):
+                pair = []
                 for dx in range(2):
                     d = 2 * dy + dx
                     r, c = 2 * r2 + dy, 2 * w + dx
                     tile = nn[r, c]
-                    tile = tile + jnp.where(r == 0, edge_top[c].astype(F32), 0.0)
-                    tile = tile + jnp.where(r == rows - 1, edge_bottom[c].astype(F32), 0.0)
-                    shift = tile[0:8] + bias_a
+                    if r == 0:
+                        tile = tile + edge_top[c].astype(F32)
+                    if r == rows - 1:
+                        tile = tile + edge_bottom[c].astype(F32)
                     raw = tile[8:16] + bias_b
                     sig = jax.nn.sigmoid(raw)
                     log_sig = jnp.minimum(raw, 0.0) - jnp.log(1.0 + jnp.exp(-jnp.abs(raw)))
-                    base = xbf[r, c] + shift
-                    second = base * sig
-                    mean = stats[pl.ds(8 * d, 8), lanes] + cls[8 * d : 8 * d + 8]
-                    logs = stats[pl.ds(32 + 8 * d, 8), lanes] + cls[32 + 8 * d : 40 + 8 * d]
-                    diff = second - mean
+                    base = xbf[r, c] + tile[0:8] + bias_a
+                    logs = stats[r2, pl.ds(32 + 8 * d, 8), lanes] + cls[32 + 8 * d : 40 + 8 * d]
+                    diff = base * sig - (stats[r2, pl.ds(8 * d, 8), lanes] + cls[8 * d : 8 * d + 8])
                     weighted = diff * jnp.exp(-2.0 * logs)
                     quad = diff * weighted
-                    first = xaf[r + 2, c + 2]
-                    mean1 = cls[64 + 8 * d : 72 + 8 * d]
-                    logs1 = cls[96 + 8 * d : 104 + 8 * d]
-                    diff1 = first - mean1
-                    weighted1 = diff1 * jnp.exp(-2.0 * logs1)
-                    quad1 = diff1 * weighted1
-                    value = log_sig - 0.5 * (
-                        2.0 * LOG_TWO_PI + 2.0 * (logs + logs1) + quad + quad1
-                    )
-                    loss_acc[...] += jnp.where(keep, value, 0.0)
+                    loss = loss + (log_sig - 0.5 * (LOG_TWO_PI + 2.0 * logs + quad))
                     dv = coef * weighted
-                    ds_ = coef - coef * quad
-                    dv1 = coef * weighted1
-                    table_acc[pl.ds(8 * d, 8), :] -= dv
-                    table_acc[pl.ds(32 + 8 * d, 8), :] += ds_
-                    table_acc[pl.ds(64 + 8 * d, 8), :] -= dv1
-                    table_acc[pl.ds(96 + 8 * d, 8), :] += coef - coef * quad1
-                    dstats[pl.ds(8 * d, 8), lanes] = -dv
-                    dstats[pl.ds(32 + 8 * d, 8), lanes] = ds_
-                    dxa[r + 2, c + 2] += dv1
+                    dstats[r2, pl.ds(8 * d, 8), lanes] = -dv
+                    dstats[r2, pl.ds(32 + 8 * d, 8), lanes] = coef - coef * quad
                     passed = dv * sig
-                    dxb[r, c] = passed
+                    pair.append(passed)
                     draw = (passed * base - coef) * (1.0 - sig)
-                    net = jnp.concatenate([passed, draw], axis=0).astype(BF16)
-                    dn[r, c] = net
-                    gain_acc[...] += net.astype(F32)
-        grads = dstats[0:64, :]
+                    dn[r, c] = jnp.concatenate([passed, draw], axis=0).astype(BF16)
+                dxb[2 * r2 + dy, w] = jnp.concatenate(pair, axis=0).astype(BF16)
+    loss_acc[...] = loss
+    dn_first[...] = dn[0]
+    dn_last[...] = dn[rows - 1]
+
+
+def prior_kernel(dn, dstats, dxb, loss_part, xaf, xt, per_image, wpt,
+                 dprior, small, taps_hi, dtaps, dxa, table_acc):
+    rows, width, _, count = dn.shape
+    half = width // 2
+    cls = per_image[0:128, :]
+    coef = per_image[128:136, :]
+    hot = per_image[136:152, :]
+    weight_grad = None
+    for r2 in range(rows // 2):
+        fill_windows(xaf, r2, half, count, taps_hi)
+        grads = dstats[r2]
         high = grads.astype(BF16)
         low = (grads - high.astype(F32)).astype(BF16)
-        dprior[:, 0:64] += (
-            dot(taps_hi[...], high, NT) + dot(taps_hi[...], low, NT) + dot(taps_lo[...], high, NT)
-        )
-        stack = jnp.concatenate([high, high, low], axis=0)
-        dtaps[...] = dot(wpt[:, 0:192], stack)
-        for w in range(half):
-            lanes = pl.ds(w * count, count)
-            for ty in range(3):
-                for tx in range(3):
-                    for dy in range(2):
-                        for dx in range(2):
-                            k = (ty * 3 + tx) * 32 + dy * 16 + dx * 8
-                            dxa[2 * r2 + 2 * ty + dy, 2 * w + 2 * tx + dx] += dtaps[pl.ds(k, 8), lanes]
-        return carry
-
-    lax.fori_loop(0, rows // 2, per_row, 0)
-
-    total[...] = jnp.zeros_like(total)
+        part = dot(taps_hi[...], high, NT)
+        weight_grad = part if weight_grad is None else weight_grad + part
+        dtaps[r2] = dot(wpt[:, 0:192], jnp.concatenate([high, high, low], axis=0))
+    dprior[...] = jnp.zeros_like(dprior)
+    dprior[:, 0:64] = weight_grad
+    for k in range(8):
+        rows8 = pl.ds(8 * k, 8)
+        value = jnp.zeros((8, count), F32)
+        for r2 in range(rows // 2):
+            for w in range(half):
+                value = value + dstats[r2, rows8, pl.ds(w * count, count)]
+        table_acc[rows8, :] = value
+    gain = jnp.zeros((16, count), F32)
+    loss = loss_part[...]
+    means = [jnp.zeros((8, count), F32)] * 4
+    scales = [jnp.zeros((8, count), F32)] * 4
+    for er in range(rows + 4):
+        for pair in range(half):
+            both = []
+            for dx in range(2):
+                c = 2 * pair + dx
+                value = None
+                for r2 in range(rows // 2):
+                    ey = er - 2 * r2
+                    for w in range(half):
+                        ex = c + 2 - 2 * w
+                        if 0 <= ey < 6 and 0 <= ex < 6:
+                            at = ((ey // 2) * 3 + ex // 2) * 32 + (ey % 2) * 16 + (ex % 2) * 8
+                            part = dtaps[r2, pl.ds(at, 8), pl.ds(w * count, count)]
+                            value = part if value is None else value + part
+                r = er - 2
+                if 0 <= r < rows:
+                    d = 2 * (r % 2) + dx
+                    gain = gain + dn[r, c].astype(F32)
+                    logs = cls[96 + 8 * d : 104 + 8 * d]
+                    diff = xaf[er, c + 2] - cls[64 + 8 * d : 72 + 8 * d]
+                    weighted = diff * jnp.exp(-2.0 * logs)
+                    quad = diff * weighted
+                    loss = loss - 0.5 * (LOG_TWO_PI + 2.0 * logs + quad)
+                    dv = coef * weighted
+                    means[d] = means[d] - dv
+                    scales[d] = scales[d] + (coef - coef * quad)
+                    value = value + dv
+                both.append(value)
+            dxa[er, pair] = jnp.concatenate(both, axis=0).astype(BF16)
+    for d in range(4):
+        table_acc[pl.ds(64 + 8 * d, 8), :] = means[d]
+        table_acc[pl.ds(96 + 8 * d, 8), :] = scales[d]
+    outer = jnp.zeros((width * 8, width * 16), F32)
+    inner = jnp.zeros((width * 8, width * 16), F32)
     for er in range(rows + 4):
         field = xt[er, 1 : width + 1].reshape(width * 16, count)
-        part_a = dxa[er, 2 : width + 2].reshape(width * 8, count)
+        outer = outer + dot(dxa[er].reshape(width * 8, count), field, NT)
         if 2 <= er < rows + 2:
-            part_b = dxb[er - 2].reshape(width * 8, count)
-            part = jnp.concatenate([part_a, part_b], axis=0)
-        else:
-            part = part_a
-        size = part.shape[0]
-        high = part.astype(BF16)
-        low = (part - high.astype(F32)).astype(BF16)
-        total[0:size, :] += dot(high, field, NT) + dot(low, field, NT)
+            inner = inner + dot(dxb[er - 2].reshape(width * 8, count), field, NT)
+    total = jnp.concatenate([outer, inner], axis=0)
     row, col = iota((256, 256), 0), iota((256, 256), 1)
-    masked = jnp.where(((row & 127) >> 3) == (col >> 4), total[...], 0.0)
-    gather = as_f32((iota((16, 256), 0) == ((iota((16, 256), 1) & 7) + 8 * (iota((16, 256), 1) >> 7))))
+    masked = jnp.where(((row & 127) >> 3) == (col >> 4), total, 0.0)
+    wide = iota((16, 256), 1)
+    gather = as_f32(iota((16, 256), 0) == (wide & 7) + 8 * (wide >> 7))
     fold = as_f32((iota((256, 128), 0) & 15) == iota((256, 128), 1))
     small[...] = jnp.zeros_like(small)
     small[:, 128:256] = dot(dot(gather, masked, NN, HIGH), fold, NN, HIGH)
     small[:, 0:128] = dot(hot, table_acc[...], NT, HIGH)
     lone = jnp.ones((8, count), F32)
-    gain_row = dot(dot(lone, gain_acc[...], NT, HIGH), half_map(), NN, HIGH)
-    small[0:8, 256:384] = gain_row
-    value = jnp.sum(jnp.sum(loss_acc[...], axis=0, keepdims=True) * coef[0:1], axis=1, keepdims=True)
+    small[0:8, 256:384] = dot(dot(lone, gain, NT, HIGH), half_map(), NN, HIGH)
+    value = jnp.where(iota((8, count), 0) < 6, loss * coef, 0.0)
+    value = jnp.sum(jnp.sum(value, axis=0, keepdims=True), axis=1, keepdims=True)
     small[8:16, 256:384] = jnp.broadcast_to(-value, (8, 128))
 
 
@@ -429,7 +472,7 @@
         chunks, each = keep.shape[:2]
         core = place[0]
         for k in range(2 * chunks):
-            block = packed[k * each : (k + 1) * each, :]
+            block = chunk_of(packed, k, each)
             mine = core == k // chunks
 
             @pl.when(mine)
@@ -438,7 +481,36 @@
 
             @pl.when(jnp.logical_not(mine))
             def _():
-                send[k % chunks] = block
+                send[k % chunks] = to_wire(block)
+
+
+def chunk_of(packed, k, each):
+    plain, fine = 2 * each // 3, each // 3
+    return jnp.concatenate(
+        [
+            packed[k * plain : (k + 1) * plain, :],
+            packed[ROW_OUT + k * fine : ROW_OUT + (k + 1) * fine, :],
+        ],
+        axis=0,
+    )
+
+
+def to_wire(block):
+    axis = block.ndim - 2
+    each = block.shape[axis]
+    plain = lax.slice_in_dim(block, 0, 2 * each // 3, axis=axis)
+    fine = lax.slice_in_dim(block, 2 * each // 3, each, axis=axis)
+    high = fine.astype(BF16).astype(F32)
+    return jnp.concatenate([plain, high, fine - high], axis=axis).astype(BF16)
+
+
+def from_wire(wire):
+    axis = wire.ndim - 2
+    part = wire.shape[axis] // 4
+    wide = wire.astype(F32)
+    fine = lax.slice_in_dim(wide, 2 * part, 3 * part, axis=axis)
+    fine = fine + lax.slice_in_dim(wide, 3 * part, 4 * part, axis=axis)
+    return jnp.concatenate([lax.slice_in_dim(wide, 0, 2 * part, axis=axis), fine], axis=axis)
 
 
 def halve_kernel(place, keep, got, mine, *sends):
@@ -446,28 +518,34 @@
     bands = keep.shape[0] // count
     here = place[1]
     for m in range(count):
-        target = mine if m == 0 else sends[m - 1]
-        at = pl.ds((here ^ m) * bands, bands)
-        target[...] = keep[at] + got[at]
+        for b in range(bands):
+            at = (here ^ m) * bands + b
+            value = keep[at] + from_wire(got[at])
+            if m == 0:
+                mine[b] = value
+            else:
+                sends[m - 1][b] = to_wire(value)
 
 
 def spread_kernel(place, bands, first, *refs):
-    gots, mine, sends = refs[: -bands], refs[-bands], refs[1 - bands :]
+    gots, mine, sends = refs[:-bands], refs[-bands], refs[1 - bands :]
     here = place[2]
     for k in range(bands):
-        target = mine if k == 0 else sends[k - 1]
         at = lax.rem(here + k, bands)
         value = first[at]
         for got in gots:
-            value = value + got[at]
-        target[...] = value
-
-
-def sum_kernel(*refs):
-    value = refs[0][...]
-    for ref in refs[1:-1]:
-        value = value + ref[...]
-    refs[-1][...] = value
+            value = value + from_wire(got[at])
+        if k == 0:
+            mine[...] = value
+        else:
+            sends[k - 1][...] = to_wire(value)
+
+
+def sum_kernel(mine, *refs):
+    value = mine[...]
+    for ref in refs[:-1]:
+        value = value + from_wire(ref[...])
+    refs[-1][...] = to_wire(value)
 
 
 def gather_kernel(place, which, xor, mine, *refs):
@@ -498,10 +576,13 @@
     loss, norm = refs[24:26]
     news, new_firsts, new_seconds = refs[26:34], refs[34:42], refs[42:50]
     square, strip, gin, gout, flat, grads = refs[50:]
-    chunks, each = own.shape[:2]
+    chunks = own.shape[0]
+    fine = own.shape[1] // 4
     for k in range(2 * chunks):
         mine = place[0] == k // chunks
-        grads[k * each : (k + 1) * each, :] = jnp.where(mine, own[k % chunks], other[k % chunks])
+        block = from_wire(jnp.where(mine, own[k % chunks], other[k % chunks]))
+        grads[2 * k * fine : 2 * (k + 1) * fine, :] = block[0 : 2 * fine]
+        grads[ROW_OUT + k * fine : ROW_OUT + (k + 1) * fine, :] = block[2 * fine :]
     bias, gains_ref, lu_ref = params[4:7]
     hidden = grads.shape[1]
     square[...] = jnp.zeros_like(square)
@@ -517,7 +598,8 @@
     real = iota((16, 128), 0) & 7
     moved = jnp.where((lane < 12) & (real < 6), field + level * gains[0:1], 0.0)
     level = jnp.where(real < 6, level, 0.0)
-    present = counts[...] / jnp.maximum(counts[...], 1.0)
+    number = counts[...]
+    present = number / jnp.maximum(number, 1.0)
     share = jnp.sum(present[:, 0:1], axis=0, keepdims=True)
     coef = share * (1.0 / (10.0 * dims * LOG_TWO)) * area
     weight = jnp.where(lane < 12, weight, 0.0)
@@ -615,18 +697,16 @@
     whole = pl.BlockSpec(memory_space=pltpu.VMEM)
 
     top, bottom = exchange_rows(
-        images[:, :2] + noise[:, :2], images[:, rows - 2 :] + noise[:, rows - 2 :]
-    )
+        (images[:, :2] + noise[:, :2]).astype(BF16),
+        (images[:, rows - 2 :] + noise[:, rows - 2 :]).astype(BF16),
+    )
+    everyone = jnp.broadcast_to(labels[None, :], (lax.axis_size("dp"), count))
+    everyone = lax.all_to_all(everyone, "dp", 0, 0, tiled=True)
     flags = jnp.stack([band > 0, band < bands - 1]).astype(F32)
     dp = lax.axis_index("dp")
     place = jnp.stack([dp & 1, dp >> 1, band]).astype(jnp.int32)
     smem = pl.BlockSpec(memory_space=pltpu.SMEM)
-    hits = (labels[None, :] == jnp.arange(16, dtype=jnp.int32)[:, None]).astype(F32)
-    groups = lax.axis_size("dp")
-    counts = jnp.broadcast_to(jnp.sum(hits, axis=1)[None, :, None], (groups, 16, 128))
-    counts = jnp.sum(lax.all_to_all(counts, "dp", 0, 0, tiled=True), axis=0)
-
-    win, wt, mixh, mixth, bias2, wout, woutt, weff, wpt, wp, tablep = pl.pallas_call(
+    win, wt, mixh, mixth, bias2, wout, woutt, weff, wpt, wp, tablep, net_bias = pl.pallas_call(
         weights_kernel,
         out_shape=(
             near((hidden, 128), BF16),
@@ -640,26 +720,28 @@
             near((288, 256), BF16),
             near((128, 384), BF16),
             near((16, 128)),
+            near((16, 128)),
         ),
         in_specs=[whole] * 8,
-        out_specs=(whole,) * 11,
+        out_specs=(whole,) * 12,
         scratch_shapes=[
             pltpu.VMEM((512, hidden), F32),
             pltpu.VMEM((128, 128), F32),
             pltpu.VMEM((8, 128), F32),
         ],
-        compiler_params=params_of(26),
+        compiler_params=params_of(VMEM_MIB),
         name="weights",
     )(*[far(p) for p in params])
 
     cols, sub = 4, 4
+    pixels = (width // 2) * count
     groups = width // cols
     steps = rows * groups
     size = cols * count
     chunk = pl.BlockSpec((1, hidden, size), lambda i: (i, 0, 0))
     ext = (rows + 4, width + 2, 16, count)
     exta = (rows + 4, width + 4, 8, count)
-    act1, sg1, act2, sg2, xa2, xt, xaf, xbf, nn, edge_top, edge_bottom = pl.pallas_call(
+    act1, sg1, act2, sg2, xa2, xt, xaf, xbf, nn, edge_top, edge_bottom, stats = pl.pallas_call(
         functools.partial(forward_kernel, cols, sub),
         grid=(steps,),
         out_shape=(pltpu.HBM((steps, hidden, size), BF16),) * 4
@@ -671,58 +753,92 @@
             near((rows, width, 16, count)),
             near((width, 16, count), BF16),
             near((width, 16, count), BF16),
+            near((rows // 2, 64, pixels)),
         ),
-        in_specs=[whole] * 4 + [smem] + [whole] * 5,
-        out_specs=(chunk,) * 4 + (whole,) * 7,
+        in_specs=[whole] * 4 + [smem] + [whole] * 7,
+        out_specs=(chunk,) * 4 + (whole,) * 8,
         scratch_shapes=[
             pltpu.VMEM((chans, rows + 4, width, count), F32),
             pltpu.VMEM((128, size), BF16),
             pltpu.VMEM((rows + 2, width + 2, 16, count), F32),
-        ],
-        compiler_params=params_of(26),
-        name="forward",
-    )(*map(far, (images, noise, top, bottom)), flags, *map(far, (weff, win, mixh, bias2, wout)))
-
-    edge_top, edge_bottom = exchange_rows(edge_top, edge_bottom)
-    gain3 = params[5][2]
-    zero = jnp.zeros((2,), F32)
-    net_bias = jnp.concatenate([gain3[:6], zero, gain3[6:] + 2.0, zero])[:, None]
-    pixels = (width // 2) * count
-    dn, dprior, small = pl.pallas_call(
-        coupling_kernel,
-        out_shape=(
-            near((rows, width, 16, count), BF16),
-            near((288, 128)),
-            near((16, 512)),
-        ),
-        in_specs=[whole] * 12,
-        out_specs=(whole,) * 3,
-        scratch_shapes=[
             pltpu.VMEM((288, pixels), BF16),
             pltpu.VMEM((288, pixels), BF16),
-            pltpu.VMEM((64, pixels), F32),
-            pltpu.VMEM((64, pixels), F32),
-            pltpu.VMEM((288, pixels), F32),
-            pltpu.VMEM(exta, F32),
-            pltpu.VMEM((rows, width, 8, count), F32),
-            pltpu.VMEM((256, 256), F32),
-            pltpu.VMEM((8, count), F32),
-            pltpu.VMEM((16, count), F32),
+        ],
+        compiler_params=params_of(VMEM_MIB),
+        cost_estimate=pl.CostEstimate(
+            flops=2 * rows * width * count * hidden * (hidden + 272),
+            transcendentals=2 * rows * width * count * hidden,
+            bytes_accessed=8 * rows * width * count * hidden,
+        ),
+        name="forward",
+    )(far(images), far(noise), top, bottom, flags, *map(far, (weff, win, mixh, bias2, wout, wp)), everyone)
+
+    got_top, got_bottom = exchange_rows(edge_top, edge_bottom)
+    def local(kernel, name, outs, scratch, *inputs):
+        return pl.pallas_call(
+            kernel,
+            out_shape=outs,
+            in_specs=[whole for _ in inputs],
+            out_specs=tuple(whole for _ in outs),
+            scratch_shapes=scratch,
+            compiler_params=params_of(VMEM_MIB),
+            name=name,
+        )(*[a if a is got_top or a is got_bottom else far(a) for a in inputs])
+
+    dn, dn_first, dn_last, dstats, dxb, loss_part, per_image, counts = local(
+        functools.partial(coupling_kernel, 12.0 * width * width),
+        "coupling",
+        (
+            near((rows, width, 16, count), BF16),
+            near((width, 16, count), BF16),
+            near((width, 16, count), BF16),
+            near((rows // 2, 64, pixels)),
+            near((rows, width // 2, 16, count), BF16),
+            near((8, count)),
+            near((152, count)),
+            near((16, 128)),
+        ),
+        [],
+        nn,
+        got_top,
+        got_bottom,
+        xbf,
+        stats,
+        labels[None, :],
+        everyone,
+        tablep,
+        net_bias,
+    )
+    dprior, small = local(
+        prior_kernel,
+        "prior_grads",
+        (near((288, 128)), near((16, 512))),
+        [
+            pltpu.VMEM((288, pixels), BF16),
+            pltpu.VMEM((rows // 2, 288, pixels), F32),
+            pltpu.VMEM((rows + 4, width // 2, 16, count), BF16),
             pltpu.VMEM((128, count), F32),
         ],
-        compiler_params=params_of(26),
-        name="coupling",
-    )(*map(far, (nn, edge_top, edge_bottom, xaf, xbf, xt, labels[None, :], counts, wp, wpt, tablep, net_bias)))
-
-    dn_top, dn_bottom = exchange_rows(dn[0], dn[rows - 1])
+        dn,
+        dstats,
+        dxb,
+        loss_part,
+        xaf,
+        xt,
+        per_image,
+        wpt,
+    )
+
+    dn_top, dn_bottom = exchange_rows(dn_first, dn_last)
     both = ("dp", "band")
     devices = lax.axis_size(both)
-    each = -(-ROWS // devices)
+    each = ROWS // devices
+    wires = each + each // 3
     half_shape = (devices // 2, each, hidden)
     keep, send = pl.pallas_call(
         functools.partial(backward_kernel, cols, sub),
         grid=(steps,),
-        out_shape=(near(half_shape),) * 2,
+        out_shape=(near(half_shape), near((devices // 2, wires, hidden), BF16)),
         in_specs=[chunk] * 4 + [smem] + [whole] * 10,
         out_specs=(whole,) * 2,
         scratch_shapes=[
@@ -735,9 +851,9 @@
             pltpu.VMEM((144, hidden), F32),
             pltpu.VMEM((96, hidden), F32),
         ],
-        compiler_params=params_of(26),
+        compiler_params=params_of(VMEM_MIB),
         name="backward",
-    )(*map(far, (act1, sg1, act2, sg2)), place, *map(far, (dn, dn_top, dn_bottom, xa2, xt, mixth, woutt, wt, dprior, small)))
+    )(*map(far, (act1, sg1, act2, sg2)), place, far(dn), dn_top, dn_bottom, *map(far, (xa2, xt, mixth, woutt, wt, dprior, small)))
 
     def call(kernel, name, outs, *inputs):
         return pl.pallas_call(
@@ -745,7 +861,7 @@
             out_shape=outs,
             in_specs=[smem if a is place else whole for a in inputs],
             out_specs=jax.tree.map(lambda _: whole, outs),
-            compiler_params=params_of(26),
+            compiler_params=params_of(VMEM_MIB),
             name=name,
         )(*inputs)
 
@@ -759,12 +875,19 @@
     groups_dp = lax.axis_size("dp")
     chips = groups_dp // 2
     got = swap(send, 1)
-    block = shape((bands, each, hidden))
-    tile = shape((each, hidden))
-    mine, *sends = call(halve_kernel, "halve", (block,) * chips, place, keep, got)
+    block = shape((bands, wires, hidden), BF16)
+    tile = shape((wires, hidden), BF16)
+    mine, *sends = call(
+        halve_kernel, "halve", (shape((bands, each, hidden)),) + (block,) * (chips - 1), place, far(keep), got
+    )
     gots = [swap(a, 2 * (m + 1)) for m, a in enumerate(sends)]
     mine, *sends = call(
-        lambda p, *refs: spread_kernel(p, bands, *refs), "spread", (tile,) * bands, place, mine, *gots
+        lambda p, *refs: spread_kernel(p, bands, *refs),
+        "spread",
+        (shape((each, hidden)),) + (tile,) * (bands - 1),
+        place,
+        mine,
+        *gots,
     )
     gots = [turn(a, k + 1) for k, a in enumerate(sends)]
     mine = call(sum_kernel, "total", tile, mine, *gots)
@@ -776,12 +899,12 @@
     mine = call(
         lambda p, *refs: gather_kernel(p, 1, True, *refs),
         "gather_chips",
-        shape((chips,) + block.shape),
+        shape((chips,) + block.shape, BF16),
         place,
         mine,
         *gots,
     )
-    mine = mine.reshape(half_shape)
+    mine = mine.reshape((devices // 2, wires, hidden))
     other = swap(mine, 1)
 
     area = float(width * width)
@@ -798,7 +921,7 @@
             pltpu.VMEM((288, 128), F32),
             pltpu.VMEM((devices * each, hidden), F32),
         ],
-        compiler_params=params_of(26),
+        compiler_params=params_of(VMEM_MIB),
         name="update",
     )(place, mine, other, counts, *params, *firsts, *seconds)
     outs = [results[0][0, 0], results[1][0, 0]]

time: 188 us -> 174 us (0.926)
  waiting for transfers between devices: 36.5 us -> 28.2 us
  local copies, waits for them, and re-layouts: 5.75 us -> 1.44 us
  other arithmetic: 3.98 us -> 1.65 us
  starting transfers between devices: 35.3 us -> 37.2 us
    ppermute x3, waiting for transfers between devices: 9.8 us -> 4.13 us  [exchange_rows(): after = lax.ppermute(up, 'band', [(i + 1, i) for i in range(count - 1)])]
    ppermute x8, waiting for transfers between devices: 19.5 us -> 14.2 us  [swap(): return lax.ppermute(array, 'dp', pairs)]
    unnamed x64 -> x53, local copies, waits for them, and re-layouts: 3.37 us -> 0.15 us
    pallas_call x1 -> x2, Pallas kernels: 9.85 us -> 9.41 us  [local(): pl.pallas_call(kernel, out_shape=outs, in_specs=[whole for _ in inputs],...]
  transfers between devices with their start and end apart: 21 -> 21, of which waited for: 15 -> 16; matrix products, arithmetic and copies ran while one was open for 2% -> 1% of each run, Pallas kernels for 23% -> 5%
where the time goes in v3:
time: 174 us; the launch traced here: 173 us
  Pallas kernels  104 us (60%)
  starting transfers between devices  37.2 us (21%)
  waiting for transfers between devices  28.2 us (16%)
    pallas_call x1, Pallas kernels, body(): pl.pallas_call(functools.partial(backward_kernel, cols, sub), grid=(steps...  42.1 us
    pallas_call x1, Pallas kernels, body(): pl.pallas_call(functools.partial(forward_kernel, cols, sub), grid=(steps,...  38 us
    ppermute x8, waiting for transfers between devices, swap(): return lax.ppermute(array, 'dp', pairs)  14.2 us
    ppermute x3, starting transfers between devices, exchange_rows(): before = lax.ppermute(down, 'band', [(i, i + 1) for i in range(count - 1)])  12.5 us
    ppermute x6, starting transfers between devices, turn(): lax.ppermute(array, 'band', [(i, (i + k) % bands) for i in range(bands)])  9.5 us
    pallas_call x2, Pallas kernels, local(): pl.pallas_call(kernel, out_shape=outs, in_specs=[whole for _ in inputs],...  9.41 us
    ppermute x6, waiting for transfers between devices, turn(): lax.ppermute(array, 'band', [(i, (i + k) % bands) for i in range(bands)])  7.31 us
    pallas_call x1, Pallas kernels, body(): pl.pallas_call(functools.partial(update_kernel, area, 12.0 * width * widt...  7.27 us
  transfers between devices with their start and end apart: 21, of which 16 were waited for; matrix products, arithmetic and copies ran while one was open for 1% of the time, Pallas kernels for 5%

profile of v3, /device:TPU:0, one launch (start us, length us, event | category | flops | bytes accessed | tf_op | source)
XLA Modules:
  0.0 173.5 jit_solution(15680408182704042021)
XLA Ops:
  0.7 1.5 add_convert_fusion
  2.2 1.3 collective-permute-start.1
  3.5 5.6 %collective-permute-start = (bf16[12,2,16,256]{3,2,1,0:T(8,128)(2,1)S(1)}, bf16[12,2,16,256]{3,2,1,0:T(8,128)(2,1)S(1)}, u32[]{:S(2)}, u32[]{:S(2)}) collective-permute-start(bf16[12,2,16,256]{3,2,1,0:T(8,128)(2,1)S(1)} %get-tuple-element.167), channel_id=1, source_target_pairs={{0,1},{1,2},{2,3},{4,5},{5,6},{6,7},{8,9},{9,10},{10,11},{12,13},{... | collective-permute-start | bytes 589832 | tf_op jit(solution)/shard_map/ppermute | solution.py:683
  9.0 1.3 broadcast_in_dim.4
  10.3 4.2 %all-to-all-start = ((s32[8,1,256]{2,1,0:T(1,128)}), s32[8,1,256]{2,1,0:T(1,128)S(1)}, u32[]{:S(2)}, u32[]{:S(2)}) async-start(s32[8,1,256]{2,1,0:T(1,128)} %broadcast_in_dim.4), calls=%async_computation | async-start | bytes 16384 | tf_op jit(solution)/shard_map/all_to_all | solution.py:704
  14.5 0.1 add_convert_fusion.2.flags
  14.6 3.7 %weights.1 = (bf16[512,128]{1,0:T(8,128)(2,1)}, f32[128,512]{1,0:T(8,128)}, bf16[512,512]{1,0:T(8,128)(2,1)}, bf16[512,512]{1,0:T(8,128)(2,1)}, f32[512,128]{1,0...) custom-call(f32[9,6,512]{2,1,0:T(8,128)} %bitcast.26, ...), custom_call_target="tpu_custom_call" | custom-call | tf_op jit(solution)/shard_map/weights/pallas_call | solution.py:709
  18.3 0.9 all-to-all-done
  19.2 38.0 %forward.1 = (bf16[16,512,1024]{2,1,0:T(8,128)(2,1)}, bf16[16,512,1024]{2,1,0:T(8,128)(2,1)}, bf16[16,512,1024]{2,1,0:T(8,128)(2,1)}, bf16[16,512,1024]{2,1,0:T(...) custom-call(f32[12,4,16,256]{3,2,1,0:T(8,128)} %images.1, ...), custom_call_target="tpu_custom_call" | custom-call | flops 13153337344 | bytes 67108864 | tf_op jit(solution)/shard_map/forward/pallas_call | solution.py:744
  57.2 3.5 %collective-permute-start.2 = (bf16[16,16,256]{2,1,0:T(8,128)(2,1)}, bf16[16,16,256]{2,1,0:T(8,128)(2,1)S(1)}, u32[]{:S(2)}, u32[]{:S(2)}) collective-permute-start(bf16[16,16,256]{2,1,0:T(8,128)(2,1)} %get-tuple-element.107), channel_id=1, source_target_pairs={{0,1},{1,2},{2,3},{4,5},{5,6},{6,7},{8,9},{9,10},{10,11},{12,13},{... | collective-permute-start | bytes 393224 | tf_op jit(solution)/shard_map/ppermute | solution.py:683
  60.7 1.3 collective-permute-start.3
  62.0 1.7 collective-permute-done.2.edge_top
  63.7 4.1 %collective-permute-done.3.edge_bottom = bf16[16,16,256]{2,1,0:T(8,128)(2,1)S(1)} collective-permute-done((bf16[16,16,256]{2,1,0:T(8,128)(2,1)}, bf16[16,16,256]{2,1,0:T(8,128)(2,1)S(1)}, u32[]{:S(2)}, u32[]{:S(2)}) %collective-permute-start.3) | collective-permute-done | bytes 131104 | tf_op jit(solution)/shard_map/ppermute | solution.py:684
  67.8 3.8 %coupling.1 = (bf16[4,16,16,256]{3,2,1,0:T(8,128)(2,1)}, bf16[16,16,256]{2,1,0:T(8,128)(2,1)}, bf16[16,16,256]{2,1,0:T(8,128)(2,1)}, f32[2,64,2048]{2,1,0:T(8,12...) custom-call(f32[4,16,16,256]{3,2,1,0:T(8,128)} %get-tuple-element.106.nn, ...), custom_call_target="tpu_custom_call" | custom-call | tf_op jit(solution)/shard_map/coupling/pallas_call | solution.py:778
  71.6 3.5 %collective-permute-start.4 = (bf16[16,16,256]{2,1,0:T(8,128)(2,1)}, bf16[16,16,256]{2,1,0:T(8,128)(2,1)S(1)}, u32[]{:S(2)}, u32[]{:S(2)}) collective-permute-start(bf16[16,16,256]{2,1,0:T(8,128)(2,1)} %get-tuple-element.114), channel_id=1, source_target_pairs={{0,1},{1,2},{2,3},{4,5},{5,6},{6,7},{8,9},{9,10},{10,11},{12,13},{... | collective-permute-start | bytes 393224 | tf_op jit(solution)/shard_map/ppermute | solution.py:683
  75.1 1.3 collective-permute-start.5
  76.4 0.1 pad_add_fusion.place.p.refs_0_
  76.5 5.6 %prior_grads.1 = (f32[288,128]{1,0:T(8,128)}, f32[16,512]{1,0:T(8,128)}) custom-call(bf16[4,16,16,256]{3,2,1,0:T(8,128)(2,1)} %get-tuple-element.113.dn, f32[2,64,2048]{2,1,0:T(8,128)} %get-tuple-element.121.dstats, bf16[4,8,16,256]{3,2,1,0:T(8,128)(2,1)} %get-tuple-element.122.dxb, f32[8,256]{1,0:T(8,128)} %get-tuple-element.123.loss_part, ...), custom_call_target="tpu_custom_call" | custom-call | tf_op jit(solution)/shard_map/prior_grads/pallas_call | solution.py:778
  82.1 0.1 collective-permute-done.5.dn_bottom
  82.4 42.1 %backward.1 = (f32[16,24,512]{2,1,0:T(8,128)}, bf16[16,32,512]{2,1,0:T(8,128)(2,1)}) custom-call(bf16[16,512,1024]{2,1,0:T(8,128)(2,1)} %get-tuple-element.102.act1, bf16[16,512,1024]{2,1,0:T(8,128)(2,1)} %get-tuple-element.103.sg1, bf16[16,512,1024]{2,1,0:T(8,128)(2,1)} %get-tuple-element.104.act2, bf16[16,512,1024]{2,1,0:T(8,128)(2,1)} %get-tuple-element.105.sg2, ...), custom_call_target="tpu_custom_call" | custom-call | tf_op jit(solution)/shard_map/backward/pallas_call | solution.py:838
  124.5 2.1 %collective-permute-done.6.got = bf16[16,32,512]{2,1,0:T(8,128)(2,1)S(1)} collective-permute-done((bf16[16,32,512]{2,1,0:T(8,128)(2,1)}, bf16[16,32,512]{2,1,0:T(8,128)(2,1)S(1)}, u32[]{:S(2)}, u32[]{:S(2)}) %collective-permute-start.6) | collective-permute-done | bytes 524320 | tf_op jit(solution)/shard_map/ppermute | solution.py:870
  126.7 1.3 halve.1
  127.9 1.6 collective-permute-start.7
  129.5 1.5 collective-permute-start.8
  130.9 0.5 collective-permute-start.9
  131.5 2.4 %collective-permute-done.7.refs_1_ = bf16[4,32,512]{2,1,0:T(8,128)(2,1)S(1)} collective-permute-done((bf16[4,32,512]{2,1,0:T(8,128)(2,1)S(1)}, bf16[4,32,512]{2,1,0:T(8,128)(2,1)S(1)}, u32[]{:S(2)}, u32[]{:S(2)}) %collective-permute-start.7) | collective-permute-done | bytes 131104 | tf_op jit(solution)/shard_map/ppermute | solution.py:870
  133.9 3.7 %collective-permute-done.8.refs_2_ = bf16[4,32,512]{2,1,0:T(8,128)(2,1)S(1)} collective-permute-done((bf16[4,32,512]{2,1,0:T(8,128)(2,1)S(1)}, bf16[4,32,512]{2,1,0:T(8,128)(2,1)S(1)}, u32[]{:S(2)}, u32[]{:S(2)}) %collective-permute-start.8) | collective-permute-done | bytes 131104 | tf_op jit(solution)/shard_map/ppermute | solution.py:870
  137.5 0.6 spread.1
  138.2 2.7 %collective-permute-start.10 = (bf16[32,512]{1,0:T(8,128)(2,1)S(1)}, bf16[32,512]{1,0:T(8,128)(2,1)S(1)}, u32[]{:S(2)}, u32[]{:S(2)}) collective-permute-start(bf16[32,512]{1,0:T(8,128)(2,1)S(1)} %get-tuple-element.136), channel_id=1, source_target_pairs={{0,1},{1,2},{2,3},{3,0},{4,5},{5,6},{6,7},{7,4},{8,9},{9,10},{10,1... | collective-permute-start | bytes 98312 | tf_op jit(solution)/shard_map/ppermute | solution.py:873
  140.8 2.6 %collective-permute-start.12 = (bf16[32,512]{1,0:T(8,128)(2,1)S(1)}, bf16[32,512]{1,0:T(8,128)(2,1)S(1)}, u32[]{:S(2)}, u32[]{:S(2)}) collective-permute-start(bf16[32,512]{1,0:T(8,128)(2,1)S(1)} %get-tuple-element.138), channel_id=1, source_target_pairs={{0,3},{1,0},{2,1},{3,2},{4,7},{5,4},{6,5},{7,6},{8,11},{9,8},{10,9... | collective-permute-start | bytes 98312 | tf_op jit(solution)/shard_map/ppermute | solution.py:873
  143.5 0.5 collective-permute-done.10.refs_0_
  144.0 1.7 collective-permute-done.11.refs_1_
  145.8 3.5 %collective-permute-start.15 = (bf16[32,512]{1,0:T(8,128)(2,1)S(1)}, bf16[32,512]{1,0:T(8,128)(2,1)S(1)}, u32[]{:S(2)}, u32[]{:S(2)}) collective-permute-start(bf16[32,512]{1,0:T(8,128)(2,1)S(1)} %total.1.refs_0_), channel_id=1, source_target_pairs={{0,3},{1,0},{2,1},{3,2},{4,7},{5,4},{6,5},{7,6},{8,11},{9,8},{10,9... | collective-permute-start | bytes 98312 | tf_op jit(solution)/shard_map/ppermute | solution.py:873
  149.3 0.6 collective-permute-start.13
  149.9 1.0 collective-permute-done.15.refs_3_
  150.9 3.2 %collective-permute-done.14.refs_2_ = bf16[32,512]{1,0:T(8,128)(2,1)S(1)} collective-permute-done((bf16[32,512]{1,0:T(8,128)(2,1)S(1)}, bf16[32,512]{1,0:T(8,128)(2,1)S(1)}, u32[]{:S(2)}, u32[]{:S(2)}) %collective-permute-start.14) | collective-permute-done | bytes 32800 | tf_op jit(solution)/shard_map/ppermute | solution.py:873
  154.1 0.9 collective-permute-done.13.refs_1_
  155.0 0.6 gather_band.1.refs_0_
  155.6 1.5 collective-permute-start.18
  157.1 1.2 collective-permute-start.17
  158.3 0.8 collective-permute-start.16
  159.1 2.5 %collective-permute-done.18.refs_3_ = bf16[4,32,512]{2,1,0:T(8,128)(2,1)S(1)} collective-permute-done((bf16[4,32,512]{2,1,0:T(8,128)(2,1)S(1)}, bf16[4,32,512]{2,1,0:T(8,128)(2,1)S(1)}, u32[]{:S(2)}, u32[]{:S(2)}) %collective-permute-start.18) | collective-permute-done | bytes 131104 | tf_op jit(solution)/shard_map/ppermute | solution.py:870
  161.6 1.3 collective-permute-done.17.refs_2_
  162.9 0.3 collective-permute-done.16.refs_1_
  163.2 0.6 gather_chips.1
  163.8 0.1 collective-permute-start.19
  163.9 1.9 %collective-permute-done.19.refs_2_ = bf16[16,32,512]{2,1,0:T(8,128)(2,1)S(1)} collective-permute-done((bf16[16,32,512]{2,1,0:T(8,128)(2,1)S(1)}, bf16[16,32,512]{2,1,0:T(8,128)(2,1)S(1)}, u32[]{:S(2)}, u32[]{:S(2)}) %collective-permute-start.19) | collective-permute-done | bytes 524320 | tf_op jit(solution)/shard_map/ppermute | solution.py:870
  166.0 7.3 %update.1 = (f32[1,1]{1,0:T(1,128)}, f32[1,1]{1,0:T(1,128)}, f32[9,6,512]{2,1,0:T(8,128)}, f32[512,512]{1,0:T(8,128)}, f32[9,12,512]{2,1,0:T(8,128)}, /*index=5*...) custom-call(s32[3]{0:T(128)S(1)} %pad_add_fusion.place.p.refs_0_, ...), custom_call_target="tpu_custom_call" | custom-call | tf_op jit(solution)/shard_map/update/pallas_call | solution.py:911
  (62 shorter events, 0.2 us)
Async XLA Ops:
  2.2 17.0 %collective-permute-start.1 = (bf16[12,2,16,256]{3,2,1,0:T(8,128)(2,1)S(1)}, bf16[12,2,16,256]{3,2,1,0:T(8,128)(2,1)S(1)}, u32[]{:S(2)}, u32[]{:S(2)}) collective-permute-start(bf16[12,2,16,256]{3,2,1,0:T(8,128)(2,1)S(1)} %get-tuple-element.166), channel_id=1, source_target_pairs={{1,0},{2,1},{3,2},{5,4},{6,5},{7,6},{9,8},{10,9},{11,10},{13,12},{... | collective-permute-start | bytes 589832 | tf_op jit(solution)/shard_map/ppermute | solution.py:684
  3.5 15.7 %collective-permute-start = (bf16[12,2,16,256]{3,2,1,0:T(8,128)(2,1)S(1)}, bf16[12,2,16,256]{3,2,1,0:T(8,128)(2,1)S(1)}, u32[]{:S(2)}, u32[]{:S(2)}) collective-permute-start(bf16[12,2,16,256]{3,2,1,0:T(8,128)(2,1)S(1)} %get-tuple-element.167), channel_id=1, source_target_pairs={{0,1},{1,2},{2,3},{4,5},{5,6},{6,7},{8,9},{9,10},{10,11},{12,13},{... | collective-permute-start | bytes 589832 | tf_op jit(solution)/shard_map/ppermute | solution.py:683
  10.3 8.9 %all-to-all-start = ((s32[8,1,256]{2,1,0:T(1,128)}), s32[8,1,256]{2,1,0:T(1,128)S(1)}, u32[]{:S(2)}, u32[]{:S(2)}) async-start(s32[8,1,256]{2,1,0:T(1,128)} %broadcast_in_dim.4), calls=%async_computation | async-start | bytes 16384 | tf_op jit(solution)/shard_map/all_to_all | solution.py:704
  19.2 38.0 %copy-start.14 = (s32[8,1,256]{2,0,1:T(8,128)}, s32[8,1,256]{2,0,1:T(8,128)S(1)}, u32[]{:S(2)}) copy-start(s32[8,1,256]{2,0,1:T(8,128)S(1)} %copy.55) | copy-start | bytes 24580
  57.2 6.5 %collective-permute-start.2 = (bf16[16,16,256]{2,1,0:T(8,128)(2,1)}, bf16[16,16,256]{2,1,0:T(8,128)(2,1)S(1)}, u32[]{:S(2)}, u32[]{:S(2)}) collective-permute-start(bf16[16,16,256]{2,1,0:T(8,128)(2,1)} %get-tuple-element.107), channel_id=1, source_target_pairs={{0,1},{1,2},{2,3},{4,5},{5,6},{6,7},{8,9},{9,10},{10,11},{12,13},{... | collective-permute-start | bytes 393224 | tf_op jit(solution)/shard_map/ppermute | solution.py:683
  60.7 7.1 %collective-permute-start.3 = (bf16[16,16,256]{2,1,0:T(8,128)(2,1)}, bf16[16,16,256]{2,1,0:T(8,128)(2,1)S(1)}, u32[]{:S(2)}, u32[]{:S(2)}) collective-permute-start(bf16[16,16,256]{2,1,0:T(8,128)(2,1)} %get-tuple-element.108), channel_id=1, source_target_pairs={{1,0},{2,1},{3,2},{5,4},{6,5},{7,6},{9,8},{10,9},{11,10},{13,12},{... | collective-permute-start | bytes 393224 | tf_op jit(solution)/shard_map/ppermute | solution.py:684
  71.6 10.5 %collective-permute-start.4 = (bf16[16,16,256]{2,1,0:T(8,128)(2,1)}, bf16[16,16,256]{2,1,0:T(8,128)(2,1)S(1)}, u32[]{:S(2)}, u32[]{:S(2)}) collective-permute-start(bf16[16,16,256]{2,1,0:T(8,128)(2,1)} %get-tuple-element.114), channel_id=1, source_target_pairs={{0,1},{1,2},{2,3},{4,5},{5,6},{6,7},{8,9},{9,10},{10,11},{12,13},{... | collective-permute-start | bytes 393224 | tf_op jit(solution)/shard_map/ppermute | solution.py:683
  75.1 7.1 %collective-permute-start.5 = (bf16[16,16,256]{2,1,0:T(8,128)(2,1)}, bf16[16,16,256]{2,1,0:T(8,128)(2,1)S(1)}, u32[]{:S(2)}, u32[]{:S(2)}) collective-permute-start(bf16[16,16,256]{2,1,0:T(8,128)(2,1)} %get-tuple-element.115), channel_id=1, source_target_pairs={{1,0},{2,1},{3,2},{5,4},{6,5},{7,6},{9,8},{10,9},{11,10},{13,12},{... | collective-permute-start | bytes 393224 | tf_op jit(solution)/shard_map/ppermute | solution.py:684
  82.1 83.7 %copy-start = (f32[512,512]{1,0:T(8,128)S(1)}, f32[512,512]{1,0:T(8,128)}, u32[]{:S(2)}) copy-start(f32[512,512]{1,0:T(8,128)} %refs_5_.1) | copy-start | bytes 3145732
  82.1 83.7 %copy-start.1 = (f32[9,12,512]{2,1,0:T(8,128)S(1)}, f32[9,12,512]{2,1,0:T(8,128)}, u32[]{:S(2)}) copy-start(f32[9,12,512]{2,1,0:T(8,128)} %refs_6_.1) | copy-start | bytes 663556
  82.1 83.7 %copy-start.2 = (f32[512,512]{1,0:T(8,128)S(1)}, f32[512,512]{1,0:T(8,128)}, u32[]{:S(2)}) copy-start(f32[512,512]{1,0:T(8,128)} %refs_13_.1) | copy-start | bytes 3145732
  82.2 83.7 %copy-start.3 = (f32[512,512]{1,0:T(8,128)S(1)}, f32[512,512]{1,0:T(8,128)}, u32[]{:S(2)}) copy-start(f32[512,512]{1,0:T(8,128)} %refs_21_.1) | copy-start | bytes 3145732
  82.2 83.7 %copy-start.4 = (f32[9,512,6]{1,2,0:T(8,128)S(1)}, f32[9,512,6]{1,2,0:T(8,128)}, u32[]{:S(2)}) copy-start(f32[9,512,6]{1,2,0:T(8,128)} %param.30) | copy-start | bytes 331780
  82.2 83.7 %copy-start.5 = (f32[9,48,24]{1,2,0:T(8,128)S(1)}, f32[9,48,24]{1,2,0:T(8,128)}, u32[]{:S(2)}) copy-start(f32[9,48,24]{1,2,0:T(8,128)} %param.33) | copy-start | bytes 124420
  82.2 83.7 %copy-start.6 = (f32[9,12,512]{2,1,0:T(8,128)S(1)}, f32[9,12,512]{2,1,0:T(8,128)}, u32[]{:S(2)}) copy-start(f32[9,12,512]{2,1,0:T(8,128)} %refs_14_.1) | copy-start | bytes 663556
  82.2 83.7 %copy-start.7 = (f32[9,12,512]{2,1,0:T(8,128)S(1)}, f32[9,12,512]{2,1,0:T(8,128)}, u32[]{:S(2)}) copy-start(f32[9,12,512]{2,1,0:T(8,128)} %refs_22_.1) | copy-start | bytes 663556
  82.2 83.7 %copy-start.8 = (f32[9,512,6]{1,2,0:T(8,128)S(1)}, f32[9,512,6]{1,2,0:T(8,128)}, u32[]{:S(2)}) copy-start(f32[9,512,6]{1,2,0:T(8,128)} %param.38) | copy-start | bytes 331780
  82.2 83.7 %copy-start.9 = (f32[9,512,6]{1,2,0:T(8,128)S(1)}, f32[9,512,6]{1,2,0:T(8,128)}, u32[]{:S(2)}) copy-start(f32[9,512,6]{1,2,0:T(8,128)} %param.46) | copy-start | bytes 331780
  82.2 83.7 %copy-start.10 = (f32[9,48,24]{1,2,0:T(8,128)S(1)}, f32[9,48,24]{1,2,0:T(8,128)}, u32[]{:S(2)}) copy-start(f32[9,48,24]{1,2,0:T(8,128)} %param.41) | copy-start | bytes 124420
  82.2 83.7 %copy-start.11 = (f32[9,48,24]{1,2,0:T(8,128)S(1)}, f32[9,48,24]{1,2,0:T(8,128)}, u32[]{:S(2)}) copy-start(f32[9,48,24]{1,2,0:T(8,128)} %param.49) | copy-start | bytes 124420
  82.3 83.7 %copy-start.12 = (f32[12,12]{1,0:T(8,128)S(1)}, f32[12,12]{1,0:T(8,128)}, u32[]{:S(2)}) copy-start(f32[12,12]{1,0:T(8,128)} %refs_10_.1) | copy-start | bytes 1732
  82.3 83.7 %copy-start.13 = (f32[10,96]{1,0:T(8,128)S(1)}, f32[10,96]{1,0:T(8,128)}, u32[]{:S(2)}) copy-start(f32[10,96]{1,0:T(8,128)} %refs_11_.1) | copy-start | bytes 11524
  82.3 83.7 %copy-start.15 = (f32[2,512]{1,0:T(2,128)S(1)}, f32[2,512]{1,0:T(2,128)}, u32[]{:S(2)}) copy-start(f32[2,512]{1,0:T(2,128)} %refs_8_.1) | copy-start | bytes 12292
  82.3 83.7 %copy-start.16 = (f32[3,12]{1,0:T(4,128)S(1)}, f32[3,12]{1,0:T(4,128)}, u32[]{:S(2)}) copy-start(f32[3,12]{1,0:T(4,128)} %refs_9_.1) | copy-start | bytes 436
  82.3 83.7 %copy-start.17 = (f32[12,12]{1,0:T(8,128)S(1)}, f32[12,12]{1,0:T(8,128)}, u32[]{:S(2)}) copy-start(f32[12,12]{1,0:T(8,128)} %refs_18_.1) | copy-start | bytes 1732
  82.3 83.6 %copy-start.18 = (f32[10,96]{1,0:T(8,128)S(1)}, f32[10,96]{1,0:T(8,128)}, u32[]{:S(2)}) copy-start(f32[10,96]{1,0:T(8,128)} %refs_19_.1) | copy-start | bytes 11524
  82.3 83.6 %copy-start.19 = (f32[12,12]{1,0:T(8,128)S(1)}, f32[12,12]{1,0:T(8,128)}, u32[]{:S(2)}) copy-start(f32[12,12]{1,0:T(8,128)} %refs_26_.1) | copy-start | bytes 1732
  82.3 83.6 %copy-start.20 = (f32[10,96]{1,0:T(8,128)S(1)}, f32[10,96]{1,0:T(8,128)}, u32[]{:S(2)}) copy-start(f32[10,96]{1,0:T(8,128)} %refs_27_.1) | copy-start | bytes 11524
  82.3 83.6 %copy-start.21 = (f32[16,128]{1,0:T(8,128)S(1)}, f32[16,128]{1,0:T(8,128)}, u32[]{:S(2)}) copy-start(f32[16,128]{1,0:T(8,128)} %get-tuple-element.139.refs_3_) | copy-start | bytes 24580
  82.4 83.6 %copy-start.22 = (f32[2,512]{1,0:T(2,128)S(1)}, f32[2,512]{1,0:T(2,128)}, u32[]{:S(2)}) copy-start(f32[2,512]{1,0:T(2,128)} %refs_16_.1) | copy-start | bytes 12292
  82.4 83.6 %copy-start.23 = (f32[2,512]{1,0:T(2,128)S(1)}, f32[2,512]{1,0:T(2,128)}, u32[]{:S(2)}) copy-start(f32[2,512]{1,0:T(2,128)} %refs_24_.1) | copy-start | bytes 12292
  82.4 83.6 %copy-start.24 = (f32[3,12]{1,0:T(4,128)S(1)}, f32[3,12]{1,0:T(4,128)}, u32[]{:S(2)}) copy-start(f32[3,12]{1,0:T(4,128)} %refs_17_.1) | copy-start | bytes 436
  82.4 83.6 %copy-start.25 = (f32[3,12]{1,0:T(4,128)S(1)}, f32[3,12]{1,0:T(4,128)}, u32[]{:S(2)}) copy-start(f32[3,12]{1,0:T(4,128)} %refs_25_.1) | copy-start | bytes 436
  124.5 2.1 %collective-permute-start.6 = (bf16[16,32,512]{2,1,0:T(8,128)(2,1)}, bf16[16,32,512]{2,1,0:T(8,128)(2,1)S(1)}, u32[]{:S(2)}, u32[]{:S(2)}) collective-permute-start(bf16[16,32,512]{2,1,0:T(8,128)(2,1)} %get-tuple-element.130), channel_id=1, source_target_pairs={{0,4},{4,0},{8,12},{12,8},{16,20},{20,16},{24,28},{28,24},{1,5},{5... | collective-permute-start | bytes 1572872 | tf_op jit(solution)/shard_map/ppermute | solution.py:870
  127.9 5.9 %collective-permute-start.7 = (bf16[4,32,512]{2,1,0:T(8,128)(2,1)S(1)}, bf16[4,32,512]{2,1,0:T(8,128)(2,1)S(1)}, u32[]{:S(2)}, u32[]{:S(2)}) collective-permute-start(bf16[4,32,512]{2,1,0:T(8,128)(2,1)S(1)} %get-tuple-element.132), channel_id=1, source_target_pairs={{0,8},{4,12},{8,0},{12,4},{16,24},{20,28},{24,16},{28,20},{1,9},{5... | collective-permute-start | bytes 393224 | tf_op jit(solution)/shard_map/ppermute | solution.py:870
  129.5 8.1 %collective-permute-start.8 = (bf16[4,32,512]{2,1,0:T(8,128)(2,1)S(1)}, bf16[4,32,512]{2,1,0:T(8,128)(2,1)S(1)}, u32[]{:S(2)}, u32[]{:S(2)}) collective-permute-start(bf16[4,32,512]{2,1,0:T(8,128)(2,1)S(1)} %get-tuple-element.133), channel_id=1, source_target_pairs={{0,16},{4,20},{8,24},{12,28},{16,0},{20,4},{24,8},{28,12},{1,17},{... | collective-permute-start | bytes 393224 | tf_op jit(solution)/shard_map/ppermute | solution.py:870
  130.9 6.6 %collective-permute-start.9 = (bf16[4,32,512]{2,1,0:T(8,128)(2,1)S(1)}, bf16[4,32,512]{2,1,0:T(8,128)(2,1)S(1)}, u32[]{:S(2)}, u32[]{:S(2)}) collective-permute-start(bf16[4,32,512]{2,1,0:T(8,128)(2,1)S(1)} %get-tuple-element.134), channel_id=1, source_target_pairs={{0,24},{4,28},{8,16},{12,20},{16,8},{20,12},{24,0},{28,4},{1,25},{... | collective-permute-start | bytes 393224 | tf_op jit(solution)/shard_map/ppermute | solution.py:870
  138.2 5.9 %collective-permute-start.10 = (bf16[32,512]{1,0:T(8,128)(2,1)S(1)}, bf16[32,512]{1,0:T(8,128)(2,1)S(1)}, u32[]{:S(2)}, u32[]{:S(2)}) collective-permute-start(bf16[32,512]{1,0:T(8,128)(2,1)S(1)} %get-tuple-element.136), channel_id=1, source_target_pairs={{0,1},{1,2},{2,3},{3,0},{4,5},{5,6},{6,7},{7,4},{8,9},{9,10},{10,1... | collective-permute-start | bytes 98312 | tf_op jit(solution)/shard_map/ppermute | solution.py:873
  140.8 4.9 %collective-permute-start.11 = (bf16[32,512]{1,0:T(8,128)(2,1)S(1)}, bf16[32,512]{1,0:T(8,128)(2,1)S(1)}, u32[]{:S(2)}, u32[]{:S(2)}) collective-permute-start(bf16[32,512]{1,0:T(8,128)(2,1)S(1)} %get-tuple-element.137), channel_id=1, source_target_pairs={{0,2},{1,3},{2,0},{3,1},{4,6},{5,7},{6,4},{7,5},{8,10},{9,11},{10,... | collective-permute-start | bytes 98312 | tf_op jit(solution)/shard_map/ppermute | solution.py:873
  140.8 4.9 %collective-permute-start.12 = (bf16[32,512]{1,0:T(8,128)(2,1)S(1)}, bf16[32,512]{1,0:T(8,128)(2,1)S(1)}, u32[]{:S(2)}, u32[]{:S(2)}) collective-permute-start(bf16[32,512]{1,0:T(8,128)(2,1)S(1)} %get-tuple-element.138), channel_id=1, source_target_pairs={{0,3},{1,0},{2,1},{3,2},{4,7},{5,4},{6,5},{7,6},{8,11},{9,8},{10,9... | collective-permute-start | bytes 98312 | tf_op jit(solution)/shard_map/ppermute | solution.py:873
  145.8 5.1 %collective-permute-start.15 = (bf16[32,512]{1,0:T(8,128)(2,1)S(1)}, bf16[32,512]{1,0:T(8,128)(2,1)S(1)}, u32[]{:S(2)}, u32[]{:S(2)}) collective-permute-start(bf16[32,512]{1,0:T(8,128)(2,1)S(1)} %total.1.refs_0_), channel_id=1, source_target_pairs={{0,3},{1,0},{2,1},{3,2},{4,7},{5,4},{6,5},{7,6},{8,11},{9,8},{10,9... | collective-permute-start | bytes 98312 | tf_op jit(solution)/shard_map/ppermute | solution.py:873
  149.3 4.8 %collective-permute-start.14 = (bf16[32,512]{1,0:T(8,128)(2,1)S(1)}, bf16[32,512]{1,0:T(8,128)(2,1)S(1)}, u32[]{:S(2)}, u32[]{:S(2)}) collective-permute-start(bf16[32,512]{1,0:T(8,128)(2,1)S(1)} %total.1.refs_0_), channel_id=1, source_target_pairs={{0,2},{1,3},{2,0},{3,1},{4,6},{5,7},{6,4},{7,5},{8,10},{9,11},{10,... | collective-permute-start | bytes 98312 | tf_op jit(solution)/shard_map/ppermute | solution.py:873
  149.3 5.7 %collective-permute-start.13 = (bf16[32,512]{1,0:T(8,128)(2,1)S(1)}, bf16[32,512]{1,0:T(8,128)(2,1)S(1)}, u32[]{:S(2)}, u32[]{:S(2)}) collective-permute-start(bf16[32,512]{1,0:T(8,128)(2,1)S(1)} %total.1.refs_0_), channel_id=1, source_target_pairs={{0,1},{1,2},{2,3},{3,0},{4,5},{5,6},{6,7},{7,4},{8,9},{9,10},{10,1... | collective-permute-start | bytes 98312 | tf_op jit(solution)/shard_map/ppermute | solution.py:873
  155.6 6.0 %collective-permute-start.18 = (bf16[4,32,512]{2,1,0:T(8,128)(2,1)S(1)}, bf16[4,32,512]{2,1,0:T(8,128)(2,1)S(1)}, u32[]{:S(2)}, u32[]{:S(2)}) collective-permute-start(bf16[4,32,512]{2,1,0:T(8,128)(2,1)S(1)} %gather_band.1.refs_0_), channel_id=1, source_target_pairs={{0,24},{4,28},{8,16},{12,20},{16,8},{20,12},{24,0},{28,4},{1,25},{... | collective-permute-start | bytes 393224 | tf_op jit(solution)/shard_map/ppermute | solution.py:870
  157.1 5.8 %collective-permute-start.17 = (bf16[4,32,512]{2,1,0:T(8,128)(2,1)S(1)}, bf16[4,32,512]{2,1,0:T(8,128)(2,1)S(1)}, u32[]{:S(2)}, u32[]{:S(2)}) collective-permute-start(bf16[4,32,512]{2,1,0:T(8,128)(2,1)S(1)} %gather_band.1.refs_0_), channel_id=1, source_target_pairs={{0,16},{4,20},{8,24},{12,28},{16,0},{20,4},{24,8},{28,12},{1,17},{... | collective-permute-start | bytes 393224 | tf_op jit(solution)/shard_map/ppermute | solution.py:870
  158.3 5.0 %collective-permute-start.16 = (bf16[4,32,512]{2,1,0:T(8,128)(2,1)S(1)}, bf16[4,32,512]{2,1,0:T(8,128)(2,1)S(1)}, u32[]{:S(2)}, u32[]{:S(2)}) collective-permute-start(bf16[4,32,512]{2,1,0:T(8,128)(2,1)S(1)} %gather_band.1.refs_0_), channel_id=1, source_target_pairs={{0,8},{4,12},{8,0},{12,4},{16,24},{20,28},{24,16},{28,20},{1,9},{5... | collective-permute-start | bytes 393224 | tf_op jit(solution)/shard_map/ppermute | solution.py:870
  163.8 2.0 %collective-permute-start.19 = (bf16[16,32,512]{2,1,0:T(8,128)(2,1)S(1)}, bf16[16,32,512]{2,1,0:T(8,128)(2,1)S(1)}, u32[]{:S(2)}, u32[]{:S(2)}) collective-permute-start(bf16[16,32,512]{2,1,0:T(8,128)(2,1)S(1)} %bitcast.24), channel_id=1, source_target_pairs={{0,4},{4,0},{8,12},{12,8},{16,20},{20,16},{24,28},{28,24},{1,5},{5... | collective-permute-start | bytes 1572872 | tf_op jit(solution)/shard_map/ppermute | solution.py:870

commit v4 on v3

--- a/solution.py
+++ b/solution.py
@@ -22,7 +22,7 @@
 F32 = jnp.float32
 BF16 = jnp.bfloat16
 MIB = 1024 * 1024
-VMEM_MIB = 30
+VMEM_MIB = 46
 NN = (((1,), (0,)), ((), ()))
 NT = (((1,), (1,)), ((), ()))
 TN = (((0,), (0,)), ((), ()))
@@ -40,6 +40,25 @@
     return lax.dot_general(left, right, dims, precision=precision, preferred_element_type=F32)
 
 
+def thirds(value):
+    high = value.astype(BF16)
+    rest = value - high.astype(F32)
+    middle = rest.astype(BF16)
+    return high, middle, (rest - middle.astype(F32)).astype(BF16)
+
+
+def select(left, right, dims=NN):
+    left = left.astype(BF16)
+    high, middle, low = (dot(left, part, dims) for part in thirds(right))
+    return high + (middle + low)
+
+
+def selected(left, right, dims=NN):
+    right = right.astype(BF16)
+    high, middle, low = (dot(part, right, dims) for part in thirds(left))
+    return high + (middle + low)
+
+
 def iota(shape, dim):
     return lax.broadcasted_iota(jnp.int32, shape, dim)
 
@@ -80,7 +99,7 @@
 
 def spread_weight(lu, gains):
     lower, upper, _ = lu_factors(lu)
-    weight = dot(channel_map(), dot(lower, upper, NN, HIGH), NN, HIGH)
+    weight = select(channel_map(), dot(lower, upper, NN, HIGH))
     scaled = weight * jnp.exp(gains[1:2])
     shift = jnp.sum(scaled * gains[0:1], axis=1, keepdims=True)
     return jnp.where(iota((16, 128), 1) == 12, shift, scaled)
@@ -118,10 +137,10 @@
     strip[...] = jnp.zeros_like(strip)
     strip[0:3, 0:12] = gains[...]
     weff[...] = spread_weight(square[...], strip[0:8, :])
-    added = dot(half_map(), strip[...], NT, HIGH)[:, 2:3] + as_f32(iota((16, 1), 0) >= 8) * 2.0
+    added = select(half_map(), strip[...], NT)[:, 2:3] + as_f32(iota((16, 1), 0) >= 8) * 2.0
     net_bias[...] = jnp.broadcast_to(added, (16, 128))
     out_map = prior_out_map()
-    flat = dot(prior_in_map(), dot(prior[...].reshape(216, 48), out_map, NN, HIGH), NN, HIGH)
+    flat = select(prior_in_map(), selected(prior[...].reshape(216, 48), out_map))
     flat_hi = flat.astype(BF16)
     flat_lo = (flat - flat_hi.astype(F32)).astype(BF16)
     wpt[...] = jnp.zeros_like(wpt)
@@ -133,8 +152,8 @@
     big[0:288, 64:128] = flat_lo.astype(F32)
     wp[...] = big[0:384, 0:128].T.astype(BF16)
     tablep[...] = jnp.zeros_like(tablep)
-    tablep[0:10, 0:64] = dot(table[:, 0:48], out_map, NN, HIGH)
-    tablep[0:10, 64:128] = dot(table[:, 48:96], out_map, NN, HIGH)
+    tablep[0:10, 0:64] = selected(table[:, 0:48], out_map)
+    tablep[0:10, 64:128] = selected(table[:, 48:96], out_map)
 
 
 def hidden_unit(u):
@@ -159,8 +178,8 @@
                         taps_lo[at, lanes] = (pair - high.astype(F32)).astype(BF16)
 
 
-def forward_kernel(cols, sub, images, noise, top, bottom, flags, weff, win, mixh, bias2, wout, wp, labels,
-                   act1, sg1, act2, sg2, xa2, xt, xaf, xbf, nn, edge_top, edge_bottom, stats,
+def forward_kernel(cols, sub, images, noise, top, bottom, flags, weff, win, mixh, bias2, wout, wp, labels, others,
+                   act1, sg1, act2, sg2, xa2, xt, xaf, xbf, nn, edge_top, edge_bottom, stats, hits,
                    xs, taps, acc, taps_hi, taps_lo):
     step = pl.program_id(0)
     rows, width, count = images.shape[1:]
@@ -168,6 +187,10 @@
 
     @pl.when(step == 0)
     def _():
+        seen = iota((16, count), 0) == jnp.broadcast_to(labels[...], (16, count))
+        same = iota((16, count), 0) == jnp.broadcast_to(others[...], (16, count))
+        seen = jnp.sum(as_f32(seen) + as_f32(same), axis=1, keepdims=True)
+        hits[...] = jnp.broadcast_to(seen, (16, 128))
         xs[:, 0:2] = top[...].astype(F32)
         xs[:, 2 : rows + 2] = images[...] + noise[...]
         xs[:, rows + 2 : rows + 4] = bottom[...].astype(F32)
@@ -179,10 +202,8 @@
         col_a = [jnp.broadcast_to(weff[0:8, c : c + 1], (8, count)) for c in range(13)]
         col_b = [jnp.broadcast_to(weff[8:16, c : c + 1], (8, count)) for c in range(13)]
 
-        def per_row(er, carry):
-            own = (er >= 2) & (er < rows + 2)
+        def per_row(own, er):
             valid = jnp.where(er < 2, flags[0], jnp.where(er >= rows + 2, flags[1], 1.0))
-            inner = jnp.clip(er - 2, 0, rows - 1)
             before = jnp.zeros((8, count), F32)
             for c in range(width):
                 a, b = col_a[12], col_b[12]
@@ -191,7 +212,8 @@
                 for ch in range(12):
                     x = jnp.broadcast_to(xs[ch, er, c : c + 1, :], (8, count))
                     a = a + col_a[ch] * x
-                    b = b + col_b[ch] * x
+                    if own:
+                        b = b + col_b[ch] * x
                     if ch < 8:
                         t0 = jnp.where(row8 == ch, x, t0)
                     else:
@@ -202,16 +224,23 @@
                 before = a
                 xt[er, c + 1] = jnp.concatenate([t0, t1], axis=0).astype(BF16)
 
-                @pl.when(own)
-                def _():
-                    xbf[inner, c] = b
+                if own:
+                    xbf[er - 2, c] = b
 
             last = jnp.concatenate([before, jnp.zeros((8, count), F32)], axis=0)
             xa2[er, width] = (last + ones).astype(BF16)
             xa2[er, width + 1] = ones.astype(BF16)
+
+        def own_row(i, carry):
+            per_row(True, i + 2)
             return carry
 
-        lax.fori_loop(0, rows + 4, per_row, 0)
+        def other_row(i, carry):
+            per_row(False, jnp.where(i < 2, i, i + rows))
+            return carry
+
+        lax.fori_loop(0, rows, own_row, 0)
+        lax.fori_loop(0, 4, other_row, 0)
 
         def per_pair(r2, carry):
             fill_windows(xaf, r2, width // 2, count, taps_hi, taps_lo)
@@ -259,21 +288,19 @@
         edge_bottom[...] = acc[rows + 1, 1 : width + 1].astype(BF16)
 
 
-def coupling_kernel(dims, nn, edge_top, edge_bottom, xbf, stats, labels, everyone, tablep, net_bias,
-                    dn, dn_first, dn_last, dstats, dxb, loss_acc, per_image, counts):
+def coupling_kernel(dims, nn, edge_top, edge_bottom, xbf, stats, labels, tablep, net_bias, *refs):
+    dn, dn_first, dn_last, dstats, dxb, loss_acc, per_image, counts = refs[-8:]
     rows, width, _, count = nn.shape
     half = width // 2
     hot = as_f32(iota((16, count), 0) == jnp.broadcast_to(labels[...], (16, count)))
-    seen = jnp.zeros((16, count), F32)
-    for k in range(everyone.shape[0]):
-        same = iota((16, count), 0) == jnp.broadcast_to(everyone[k : k + 1, :], (16, count))
-        seen = seen + as_f32(same)
-    number = jnp.broadcast_to(jnp.sum(seen, axis=1, keepdims=True), (16, 128))
+    number = refs[0][...]
+    for ref in refs[1:-8]:
+        number = number + ref[...]
     counts[...] = number
     scale16 = 1.0 / (10.0 * jnp.maximum(number, 1.0) * (dims * LOG_TWO))
     coef = jnp.sum(hot * scale16[:, 0:1], axis=0, keepdims=True)
     coef = jnp.broadcast_to(coef, (8, count))
-    cls = dot(tablep[...], hot, TN, HIGH)
+    cls = selected(tablep[...], hot, TN)
     per_image[0:128, :] = cls
     per_image[128:136, :] = coef
     per_image[136:152, :] = hot
@@ -294,7 +321,7 @@
                     if r == rows - 1:
                         tile = tile + edge_bottom[c].astype(F32)
                     raw = tile[8:16] + bias_b
-                    sig = jax.nn.sigmoid(raw)
+                    sig = 0.5 + 0.5 * jnp.tanh(0.5 * raw)
                     log_sig = jnp.minimum(raw, 0.0) - jnp.log(1.0 + jnp.exp(-jnp.abs(raw)))
                     base = xbf[r, c] + tile[0:8] + bias_a
                     logs = stats[r2, pl.ds(32 + 8 * d, 8), lanes] + cls[32 + 8 * d : 40 + 8 * d]
@@ -386,14 +413,18 @@
     total = jnp.concatenate([outer, inner], axis=0)
     row, col = iota((256, 256), 0), iota((256, 256), 1)
     masked = jnp.where(((row & 127) >> 3) == (col >> 4), total, 0.0)
-    wide = iota((16, 256), 1)
-    gather = as_f32(iota((16, 256), 0) == (wide & 7) + 8 * (wide >> 7))
+    halves = []
+    for h in range(2):
+        value = masked[128 * h : 128 * h + 8]
+        for k in range(1, 16):
+            value = value + masked[128 * h + 8 * k : 128 * h + 8 * k + 8]
+        halves.append(value)
     fold = as_f32((iota((256, 128), 0) & 15) == iota((256, 128), 1))
     small[...] = jnp.zeros_like(small)
-    small[:, 128:256] = dot(dot(gather, masked, NN, HIGH), fold, NN, HIGH)
-    small[:, 0:128] = dot(hot, table_acc[...], NT, HIGH)
-    lone = jnp.ones((8, count), F32)
-    small[0:8, 256:384] = dot(dot(lone, gain, NT, HIGH), half_map(), NN, HIGH)
+    small[:, 128:256] = selected(jnp.concatenate(halves, axis=0), fold)
+    small[:, 0:128] = select(hot, table_acc[...], NT)
+    spread = half_map() * jnp.sum(gain, axis=1, keepdims=True)
+    small[0:8, 256:384] = jnp.broadcast_to(jnp.sum(spread, axis=0, keepdims=True), (8, 128))
     value = jnp.where(iota((8, count), 0) < 6, loss * coef, 0.0)
     value = jnp.sum(jnp.sum(value, axis=0, keepdims=True), axis=1, keepdims=True)
     small[8:16, 256:384] = jnp.broadcast_to(-value, (8, 128))
@@ -457,17 +488,20 @@
             packed[at : at + 6, :] = gin[from_row : from_row + 6, :]
         packed[ROW_BIAS : ROW_BIAS + 1, :] = gin[46:47, :]
         lone = jnp.ones((8, 128), F32)
-        packed[ROW_BIAS + 1 : ROW_BIAS + 2, :] = dot(lone, bias_acc[...], NT, HIGH)[0:1]
+        packed[ROW_BIAS + 1 : ROW_BIAS + 2, :] = select(lone, bias_acc[...], NT)[0:1]
         for k in range(4):
             packed[ROW_PRIOR:ROW_SMALL, 128 * k : 128 * k + 128] = dprior[72 * k : 72 * k + 72, :]
         packed[ROW_SMALL:ROWS, :] = small[...]
-        cross = dot(wt[0:96, :], wfield[...], NT, HIGH)
+        cross = select(wt[0:96, :], wfield[...], NT)
         row, col = iota((96, 144), 0), iota((96, 144), 1)
         slot = (row >> 3) & 3
         same = (slot < 3) & ((row >> 5) * 3 + slot == col >> 4) & ((row & 7) < 6)
-        gather = as_f32(iota((8, 96), 0) == (iota((8, 96), 1) & 7))
         fold = as_f32((iota((144, 128), 0) & 15) == iota((144, 128), 1))
-        field_terms = dot(dot(gather, jnp.where(same, cross, 0.0), NN, HIGH), fold, NN, HIGH)
+        cross = jnp.where(same, cross, 0.0)
+        value = cross[0:8]
+        for k in range(1, 12):
+            value = value + cross[8 * k : 8 * k + 8]
+        field_terms = selected(value, fold)
         packed[ROW_SMALL : ROW_SMALL + 8, 128:256] += 2.0 * field_terms
         chunks, each = keep.shape[:2]
         core = place[0]
@@ -560,8 +594,8 @@
 def adamw(weight, first, second, grad, out, out_first, out_second, at=Ellipsis):
     first_new = BETA_ONE * first[at] + (1.0 - BETA_ONE) * grad
     second_new = BETA_TWO * second[at] + (1.0 - BETA_TWO) * grad * grad
-    first_hat = first_new / (1.0 - BETA_ONE**STEP)
-    second_hat = second_new / (1.0 - BETA_TWO**STEP)
+    first_hat = first_new * (1.0 / (1.0 - BETA_ONE**STEP))
+    second_hat = second_new * (1.0 / (1.0 - BETA_TWO**STEP))
     out[at] = weight[at] - RATE * (
         first_hat / (jnp.sqrt(second_hat) + EPSILON) + DECAY * weight[at]
     )
@@ -575,7 +609,7 @@
     params, firsts, seconds = refs[:8], refs[8:16], refs[16:24]
     loss, norm = refs[24:26]
     news, new_firsts, new_seconds = refs[26:34], refs[34:42], refs[42:50]
-    square, strip, gin, gout, flat, grads = refs[50:]
+    square, strip, gin, gout, flat, kept, grads = refs[50:]
     chunks = own.shape[0]
     fine = own.shape[1] // 4
     for k in range(2 * chunks):
@@ -605,7 +639,7 @@
     weight = jnp.where(lane < 12, weight, 0.0)
     d_shift = jnp.sum(weight * level, axis=0, keepdims=True)
     d_scale = jnp.sum(weight * moved, axis=0, keepdims=True) - coef
-    d_product = dot(channel_map(), moved * jnp.exp(gains[1:2]), TN, HIGH)
+    d_product = select(channel_map(), moved * jnp.exp(gains[1:2]), TN)
     d_lower = dot(d_product, upper, NT, HIGH)
     d_upper = dot(lower, d_product, TN, HIGH)
     row, col = iota((128, 128), 0), iota((128, 128), 1)
@@ -624,9 +658,11 @@
     for k in range(4):
         flat[72 * k : 72 * k + 72, :] = grads[ROW_PRIOR:ROW_SMALL, 128 * k : 128 * k + 128]
     out_map = prior_out_map()
-    d_prior = dot(dot(prior_in_map(), flat[...], TN, HIGH)[:, 0:64], out_map, NT, HIGH)
+    for k in range(36):
+        kept[pl.ds((k >> 2) * 24 + (k & 3), 6, stride=4), :] = flat[8 * k : 8 * k + 6, :]
+    d_prior = selected(kept[:, 0:64], out_map, NT)
     d_table = grads[ROW_SMALL:ROWS, 0:128]
-    d_table = [dot(d_table[:, 0:64], out_map, NT, HIGH), dot(d_table[:, 64:128], out_map, NT, HIGH)]
+    d_table = [selected(d_table[:, 0:64], out_map, NT), selected(d_table[:, 64:128], out_map, NT)]
     d_table = [part[0:10] for part in d_table]
     d_bias = [grads[ROW_BIAS : ROW_BIAS + 1, :], grads[ROW_BIAS + 1 : ROW_BIAS + 2, :]]
     d_mix = grads[0:ROW_OUT, :]
@@ -700,8 +736,15 @@
         (images[:, :2] + noise[:, :2]).astype(BF16),
         (images[:, rows - 2 :] + noise[:, rows - 2 :]).astype(BF16),
     )
-    everyone = jnp.broadcast_to(labels[None, :], (lax.axis_size("dp"), count))
-    everyone = lax.all_to_all(everyone, "dp", 0, 0, tiled=True)
+    groups_dp = lax.axis_size("dp")
+    chips = groups_dp // 2
+
+    def swap(array, mask):
+        pairs = [(i, i ^ mask) for i in range(groups_dp)]
+        return lax.ppermute(array, "dp", pairs)
+
+    labels = labels[None, :]
+    others = swap(labels, 1)
     flags = jnp.stack([band > 0, band < bands - 1]).astype(F32)
     dp = lax.axis_index("dp")
     place = jnp.stack([dp & 1, dp >> 1, band]).astype(jnp.int32)
@@ -733,7 +776,7 @@
         name="weights",
     )(*[far(p) for p in params])
 
-    cols, sub = 4, 4
+    cols, sub = 8, 4
     pixels = (width // 2) * count
     groups = width // cols
     steps = rows * groups
@@ -741,7 +784,7 @@
     chunk = pl.BlockSpec((1, hidden, size), lambda i: (i, 0, 0))
     ext = (rows + 4, width + 2, 16, count)
     exta = (rows + 4, width + 4, 8, count)
-    act1, sg1, act2, sg2, xa2, xt, xaf, xbf, nn, edge_top, edge_bottom, stats = pl.pallas_call(
+    act1, sg1, act2, sg2, xa2, xt, xaf, xbf, nn, edge_top, edge_bottom, stats, hits = pl.pallas_call(
         functools.partial(forward_kernel, cols, sub),
         grid=(steps,),
         out_shape=(pltpu.HBM((steps, hidden, size), BF16),) * 4
@@ -754,9 +797,10 @@
             near((width, 16, count), BF16),
             near((width, 16, count), BF16),
             near((rows // 2, 64, pixels)),
+            shape((16, 128)),
         ),
-        in_specs=[whole] * 4 + [smem] + [whole] * 7,
-        out_specs=(chunk,) * 4 + (whole,) * 8,
+        in_specs=[whole] * 4 + [smem] + [whole] * 8,
+        out_specs=(chunk,) * 4 + (whole,) * 9,
         scratch_shapes=[
             pltpu.VMEM((chans, rows + 4, width, count), F32),
             pltpu.VMEM((128, size), BF16),
@@ -771,9 +815,11 @@
             bytes_accessed=8 * rows * width * count * hidden,
         ),
         name="forward",
-    )(far(images), far(noise), top, bottom, flags, *map(far, (weff, win, mixh, bias2, wout, wp)), everyone)
+    )(far(images), far(noise), top, bottom, flags, *map(far, (weff, win, mixh, bias2, wout, wp, labels)), others)
 
     got_top, got_bottom = exchange_rows(edge_top, edge_bottom)
+    plain = (got_top.shape, hits.shape)
+
     def local(kernel, name, outs, scratch, *inputs):
         return pl.pallas_call(
             kernel,
@@ -783,7 +829,7 @@
             scratch_shapes=scratch,
             compiler_params=params_of(VMEM_MIB),
             name=name,
-        )(*[a if a is got_top or a is got_bottom else far(a) for a in inputs])
+        )(*[a if a.shape in plain else far(a) for a in inputs])
 
     dn, dn_first, dn_last, dstats, dxb, loss_part, per_image, counts = local(
         functools.partial(coupling_kernel, 12.0 * width * width),
@@ -804,10 +850,11 @@
         got_bottom,
         xbf,
         stats,
-        labels[None, :],
-        everyone,
+        labels,
         tablep,
         net_bias,
+        hits,
+        *[swap(hits, 2 * m) for m in range(1, chips)],
     )
     dprior, small = local(
         prior_kernel,
@@ -865,15 +912,9 @@
             name=name,
         )(*inputs)
 
-    def swap(array, mask):
-        pairs = [(i, i ^ mask) for i in range(groups_dp)]
-        return lax.ppermute(array, "dp", pairs)
-
     def turn(array, k):
         return lax.ppermute(array, "band", [(i, (i + k) % bands) for i in range(bands)])
 
-    groups_dp = lax.axis_size("dp")
-    chips = groups_dp // 2
     got = swap(send, 1)
     block = shape((bands, wires, hidden), BF16)
     tile = shape((wires, hidden), BF16)
@@ -919,6 +960,7 @@
             pltpu.VMEM((9, 6, hidden), F32),
             pltpu.VMEM((9, 12, hidden), F32),
             pltpu.VMEM((288, 128), F32),
+            pltpu.VMEM((216, 128), F32),
             pltpu.VMEM((devices * each, hidden), F32),
         ],
         compiler_params=params_of(VMEM_MIB),

time: 174 us -> 166 us (0.954)
  Pallas kernels: 104 us -> 97 us
  waiting for transfers between devices: 28.2 us -> 25.5 us
  starting transfers between devices: 37.2 us -> 39.4 us
    all_to_all x1 -> x0, starting transfers between devices: 4.16 us -> none  [body(): everyone = lax.all_to_all(everyone, 'dp', 0, 0, tiled=True)]
    ppermute x3, waiting for transfers between devices: 4.13 us -> 0.45 us  [exchange_rows(): after = lax.ppermute(up, 'band', [(i + 1, i) for i in range(count - 1)])]
    ppermute x8 -> x12, starting transfers between devices: 7.18 us -> 10.8 us  [swap(): return lax.ppermute(array, 'dp', pairs)]
    pallas_call x1, Pallas kernels: 38 us -> 34.4 us  [body(): pl.pallas_call(functools.partial(forward_kernel, cols, sub), grid=(steps,...]
    ppermute x8 -> x12, waiting for transfers between devices: 14.2 us -> 16.9 us  [swap(): return lax.ppermute(array, 'dp', pairs)]
    ppermute x3, starting transfers between devices: 12.5 us -> 14.5 us  [exchange_rows(): before = lax.ppermute(down, 'band', [(i, i + 1) for i in range(count - 1)])]
  transfers between devices with their start and end apart: 21 -> 24, of which waited for: 16 -> 18; matrix products, arithmetic and copies ran while one was open for 1% -> 0% of each run, Pallas kernels for 5% -> 5%
where the time goes in v4:
time: 166 us; the launch traced here: 165 us
  Pallas kernels  97 us (58%)
  starting transfers between devices  39.4 us (24%)
  waiting for transfers between devices  25.5 us (15%)
    pallas_call x1, Pallas kernels, body(): pl.pallas_call(functools.partial(backward_kernel, cols, sub), grid=(steps...  41.2 us
    pallas_call x1, Pallas kernels, body(): pl.pallas_call(functools.partial(forward_kernel, cols, sub), grid=(steps,...  34.4 us
    ppermute x12, waiting for transfers between devices, swap(): return lax.ppermute(array, 'dp', pairs)  16.9 us
    ppermute x3, starting transfers between devices, exchange_rows(): before = lax.ppermute(down, 'band', [(i, i + 1) for i in range(count - 1)])  14.5 us
    ppermute x12, starting transfers between devices, swap(): return lax.ppermute(array, 'dp', pairs)  10.8 us
    ppermute x6, starting transfers between devices, turn(): lax.ppermute(array, 'band', [(i, (i + k) % bands) for i in range(bands)])  10.1 us
    pallas_call x2, Pallas kernels, local(): pl.pallas_call(kernel, out_shape=outs, in_specs=[whole for _ in inputs],...  8.74 us
    ppermute x6, waiting for transfers between devices, turn(): lax.ppermute(array, 'band', [(i, (i + k) % bands) for i in range(bands)])  7.65 us
  transfers between devices with their start and end apart: 24, of which 18 were waited for; matrix products, arithmetic and copies ran while one was open for 0% of the time, Pallas kernels for 5%

profile of v4, /device:TPU:0, one launch (start us, length us, event | category | flops | bytes accessed | tf_op | source)
XLA Modules:
  0.0 165.1 jit_solution(236862831827997263)
XLA Ops:
  0.7 1.5 add_convert_fusion
  2.2 1.3 collective-permute-start.1
  3.5 5.6 %collective-permute-start = (bf16[12,2,16,256]{3,2,1,0:T(8,128)(2,1)S(1)}, bf16[12,2,16,256]{3,2,1,0:T(8,128)(2,1)S(1)}, u32[]{:S(2)}, u32[]{:S(2)}) collective-permute-start(bf16[12,2,16,256]{3,2,1,0:T(8,128)(2,1)S(1)} %get-tuple-element.169), channel_id=1, source_target_pairs={{0,1},{1,2},{2,3},{4,5},{5,6},{6,7},{8,9},{9,10},{10,11},{12,13},{... | collective-permute-start | bytes 589832 | tf_op jit(solution)/shard_map/ppermute | solution.py:719
  9.2 3.4 %weights.1 = (bf16[512,128]{1,0:T(8,128)(2,1)}, f32[128,512]{1,0:T(8,128)}, bf16[512,512]{1,0:T(8,128)(2,1)}, bf16[512,512]{1,0:T(8,128)(2,1)}, f32[512,128]{1,0...) custom-call(f32[9,6,512]{2,1,0:T(8,128)} %bitcast.23, ...), custom_call_target="tpu_custom_call" | custom-call | tf_op jit(solution)/shard_map/weights/pallas_call | solution.py:752
  12.6 0.6 collective-permute-done.top
  13.2 34.4 %forward.1 = (bf16[8,512,2048]{2,1,0:T(8,128)(2,1)}, bf16[8,512,2048]{2,1,0:T(8,128)(2,1)}, bf16[8,512,2048]{2,1,0:T(8,128)(2,1)}, bf16[8,512,2048]{2,1,0:T(8,12...) custom-call(f32[12,4,16,256]{3,2,1,0:T(8,128)} %images.1, ...), custom_call_target="tpu_custom_call" | custom-call | flops 13153337344 | bytes 67108864 | tf_op jit(solution)/shard_map/forward/pallas_call | solution.py:787
  47.6 4.4 %collective-permute-start.3 = (bf16[16,16,256]{2,1,0:T(8,128)(2,1)}, bf16[16,16,256]{2,1,0:T(8,128)(2,1)S(1)}, u32[]{:S(2)}, u32[]{:S(2)}) collective-permute-start(bf16[16,16,256]{2,1,0:T(8,128)(2,1)} %get-tuple-element.108), channel_id=1, source_target_pairs={{0,1},{1,2},{2,3},{4,5},{5,6},{6,7},{8,9},{9,10},{10,11},{12,13},{... | collective-permute-start | bytes 393224 | tf_op jit(solution)/shard_map/ppermute | solution.py:719
  52.0 1.3 collective-permute-start.4
  53.3 2.7 %collective-permute-start.7 = (f32[16,128]{1,0:T(8,128)S(1)}, f32[16,128]{1,0:T(8,128)S(1)}, u32[]{:S(2)}, u32[]{:S(2)}) collective-permute-start(f32[16,128]{1,0:T(8,128)S(1)} %get-tuple-element.114.refs_0_), channel_id=1, source_target_pairs={{0,24},{4,28},{8,16},{12,20},{16,8},{20,12},{24,0},{28,4},{1,25},{... | collective-permute-start | bytes 24584 | tf_op jit(solution)/shard_map/ppermute | solution.py:744
  56.0 0.5 collective-permute-start.6
  56.9 1.1 collective-permute-done.7.refs_3_
  57.9 1.7 %collective-permute-done.6.refs_2_ = f32[16,128]{1,0:T(8,128)S(1)} collective-permute-done((f32[16,128]{1,0:T(8,128)S(1)}, f32[16,128]{1,0:T(8,128)S(1)}, u32[]{:S(2)}, u32[]{:S(2)}) %collective-permute-start.6) | collective-permute-done | bytes 8224 | tf_op jit(solution)/shard_map/ppermute | solution.py:744
  59.6 0.5 collective-permute-done.5.refs_1_
  60.2 3.7 %coupling.1 = (bf16[4,16,16,256]{3,2,1,0:T(8,128)(2,1)}, bf16[16,16,256]{2,1,0:T(8,128)(2,1)}, bf16[16,16,256]{2,1,0:T(8,128)(2,1)}, f32[2,64,2048]{2,1,0:T(8,12...) custom-call(f32[4,16,16,256]{3,2,1,0:T(8,128)} %get-tuple-element.107.nn, ...), custom_call_target="tpu_custom_call" | custom-call | tf_op jit(solution)/shard_map/coupling/pallas_call | solution.py:824
  63.9 4.5 %collective-permute-start.8 = (bf16[16,16,256]{2,1,0:T(8,128)(2,1)}, bf16[16,16,256]{2,1,0:T(8,128)(2,1)S(1)}, u32[]{:S(2)}, u32[]{:S(2)}) collective-permute-start(bf16[16,16,256]{2,1,0:T(8,128)(2,1)} %get-tuple-element.116), channel_id=1, source_target_pairs={{0,1},{1,2},{2,3},{4,5},{5,6},{6,7},{8,9},{9,10},{10,11},{12,13},{... | collective-permute-start | bytes 393224 | tf_op jit(solution)/shard_map/ppermute | solution.py:719
  68.4 1.5 collective-permute-start.9
  70.0 5.1 %prior_grads.1 = (f32[288,128]{1,0:T(8,128)}, f32[16,512]{1,0:T(8,128)}) custom-call(bf16[4,16,16,256]{3,2,1,0:T(8,128)(2,1)} %get-tuple-element.115.dn, f32[2,64,2048]{2,1,0:T(8,128)} %get-tuple-element.123.dstats, bf16[4,8,16,256]{3,2,1,0:T(8,128)(2,1)} %get-tuple-element.124.dxb, f32[8,256]{1,0:T(8,128)} %get-tuple-element.125.loss_part, ...), custom_call_target="tpu_custom_call" | custom-call | tf_op jit(solution)/shard_map/prior_grads/pallas_call | solution.py:824
  75.0 0.4 collective-permute-done.9.dn_bottom
  75.7 41.2 %backward.1 = (f32[16,24,512]{2,1,0:T(8,128)}, bf16[16,32,512]{2,1,0:T(8,128)(2,1)}) custom-call(bf16[8,512,2048]{2,1,0:T(8,128)(2,1)} %get-tuple-element.103.act1, bf16[8,512,2048]{2,1,0:T(8,128)(2,1)} %get-tuple-element.104.sg1, bf16[8,512,2048]{2,1,0:T(8,128)(2,1)} %get-tuple-element.105.act2, bf16[8,512,2048]{2,1,0:T(8,128)(2,1)} %get-tuple-element.106.sg2, ...), custom_call_target="tpu_custom_call" | custom-call | tf_op jit(solution)/shard_map/backward/pallas_call | solution.py:885
  117.0 2.1 %collective-permute-done.10.got = bf16[16,32,512]{2,1,0:T(8,128)(2,1)S(1)} collective-permute-done((bf16[16,32,512]{2,1,0:T(8,128)(2,1)}, bf16[16,32,512]{2,1,0:T(8,128)(2,1)S(1)}, u32[]{:S(2)}, u32[]{:S(2)}) %collective-permute-start.10) | collective-permute-done | bytes 524320 | tf_op jit(solution)/shard_map/ppermute | solution.py:744
  119.1 1.3 halve.1
  120.4 0.4 collective-permute-start.11
  120.8 1.7 %collective-permute-start.12 = (bf16[4,32,512]{2,1,0:T(8,128)(2,1)S(1)}, bf16[4,32,512]{2,1,0:T(8,128)(2,1)S(1)}, u32[]{:S(2)}, u32[]{:S(2)}) collective-permute-start(bf16[4,32,512]{2,1,0:T(8,128)(2,1)S(1)} %get-tuple-element.135), channel_id=1, source_target_pairs={{0,16},{4,20},{8,24},{12,28},{16,0},{20,4},{24,8},{28,12},{1,17},{... | collective-permute-start | bytes 393224 | tf_op jit(solution)/shard_map/ppermute | solution.py:744
  122.5 1.4 collective-permute-start.13
  123.9 2.9 %collective-permute-done.11.refs_1_ = bf16[4,32,512]{2,1,0:T(8,128)(2,1)S(1)} collective-permute-done((bf16[4,32,512]{2,1,0:T(8,128)(2,1)S(1)}, bf16[4,32,512]{2,1,0:T(8,128)(2,1)S(1)}, u32[]{:S(2)}, u32[]{:S(2)}) %collective-permute-start.11) | collective-permute-done | bytes 131104 | tf_op jit(solution)/shard_map/ppermute | solution.py:744
  126.8 1.3 collective-permute-done.12.refs_2_
  128.1 1.6 collective-permute-done.13.refs_3_
  129.7 0.6 spread.1
  130.3 2.3 %collective-permute-start.14 = (bf16[32,512]{1,0:T(8,128)(2,1)S(1)}, bf16[32,512]{1,0:T(8,128)(2,1)S(1)}, u32[]{:S(2)}, u32[]{:S(2)}) collective-permute-start(bf16[32,512]{1,0:T(8,128)(2,1)S(1)} %get-tuple-element.138), channel_id=1, source_target_pairs={{0,1},{1,2},{2,3},{3,0},{4,5},{5,6},{6,7},{7,4},{8,9},{9,10},{10,1... | collective-permute-start | bytes 98312 | tf_op jit(solution)/shard_map/ppermute | solution.py:916
  132.6 2.6 %collective-permute-start.15 = (bf16[32,512]{1,0:T(8,128)(2,1)S(1)}, bf16[32,512]{1,0:T(8,128)(2,1)S(1)}, u32[]{:S(2)}, u32[]{:S(2)}) collective-permute-start(bf16[32,512]{1,0:T(8,128)(2,1)S(1)} %get-tuple-element.139), channel_id=1, source_target_pairs={{0,2},{1,3},{2,0},{3,1},{4,6},{5,7},{6,4},{7,5},{8,10},{9,11},{10,... | collective-permute-start | bytes 98312 | tf_op jit(solution)/shard_map/ppermute | solution.py:916
  135.2 1.3 collective-permute-start.16
  136.6 0.4 collective-permute-done.14.refs_0_
  137.0 0.6 collective-permute-done.15.refs_1_
  137.6 1.6 collective-permute-done.16.refs_2_
  139.2 3.2 %collective-permute-start.19 = (bf16[32,512]{1,0:T(8,128)(2,1)S(1)}, bf16[32,512]{1,0:T(8,128)(2,1)S(1)}, u32[]{:S(2)}, u32[]{:S(2)}) collective-permute-start(bf16[32,512]{1,0:T(8,128)(2,1)S(1)} %total.1.refs_0_), channel_id=1, source_target_pairs={{0,3},{1,0},{2,1},{3,2},{4,7},{5,4},{6,5},{7,6},{8,11},{9,8},{10,9... | collective-permute-start | bytes 98312 | tf_op jit(solution)/shard_map/ppermute | solution.py:916
  142.4 0.6 collective-permute-start.17
  143.0 1.0 collective-permute-done.19.refs_3_
  144.0 3.2 %collective-permute-done.18.refs_2_ = bf16[32,512]{1,0:T(8,128)(2,1)S(1)} collective-permute-done((bf16[32,512]{1,0:T(8,128)(2,1)S(1)}, bf16[32,512]{1,0:T(8,128)(2,1)S(1)}, u32[]{:S(2)}, u32[]{:S(2)}) %collective-permute-start.18) | collective-permute-done | bytes 32800 | tf_op jit(solution)/shard_map/ppermute | solution.py:916
  147.2 0.9 collective-permute-done.17.refs_1_
  148.1 0.6 gather_band.1.refs_0_
  148.6 1.8 %collective-permute-start.22 = (bf16[4,32,512]{2,1,0:T(8,128)(2,1)S(1)}, bf16[4,32,512]{2,1,0:T(8,128)(2,1)S(1)}, u32[]{:S(2)}, u32[]{:S(2)}) collective-permute-start(bf16[4,32,512]{2,1,0:T(8,128)(2,1)S(1)} %gather_band.1.refs_0_), channel_id=1, source_target_pairs={{0,24},{4,28},{8,16},{12,20},{16,8},{20,12},{24,0},{28,4},{1,25},{... | collective-permute-start | bytes 393224 | tf_op jit(solution)/shard_map/ppermute | solution.py:744
  150.5 0.5 collective-permute-start.21
  151.0 1.2 collective-permute-start.20
  152.2 2.4 %collective-permute-done.22.refs_3_ = bf16[4,32,512]{2,1,0:T(8,128)(2,1)S(1)} collective-permute-done((bf16[4,32,512]{2,1,0:T(8,128)(2,1)S(1)}, bf16[4,32,512]{2,1,0:T(8,128)(2,1)S(1)}, u32[]{:S(2)}, u32[]{:S(2)}) %collective-permute-start.22) | collective-permute-done | bytes 131104 | tf_op jit(solution)/shard_map/ppermute | solution.py:744
  154.6 1.3 collective-permute-done.21.refs_2_
  156.0 0.6 gather_chips.1
  156.7 1.9 %collective-permute-done.23.refs_2_ = bf16[16,32,512]{2,1,0:T(8,128)(2,1)S(1)} collective-permute-done((bf16[16,32,512]{2,1,0:T(8,128)(2,1)S(1)}, bf16[16,32,512]{2,1,0:T(8,128)(2,1)S(1)}, u32[]{:S(2)}, u32[]{:S(2)}) %collective-permute-start.23) | collective-permute-done | bytes 524320 | tf_op jit(solution)/shard_map/ppermute | solution.py:744
  158.8 6.2 %update.1 = (f32[1,1]{1,0:T(1,128)}, f32[1,1]{1,0:T(1,128)}, f32[9,6,512]{2,1,0:T(8,128)}, f32[512,512]{1,0:T(8,128)}, f32[9,12,512]{2,1,0:T(8,128)}, /*index=5*...) custom-call(s32[3]{0:T(128)S(1)} %pad_add_fusion.place.p.refs_0_, ...), custom_call_target="tpu_custom_call" | custom-call | tf_op jit(solution)/shard_map/update/pallas_call | solution.py:952
  (68 shorter events, 0.9 us)
Async XLA Ops:
  2.2 10.4 %collective-permute-start.1 = (bf16[12,2,16,256]{3,2,1,0:T(8,128)(2,1)S(1)}, bf16[12,2,16,256]{3,2,1,0:T(8,128)(2,1)S(1)}, u32[]{:S(2)}, u32[]{:S(2)}) collective-permute-start(bf16[12,2,16,256]{3,2,1,0:T(8,128)(2,1)S(1)} %get-tuple-element.168), channel_id=1, source_target_pairs={{1,0},{2,1},{3,2},{5,4},{6,5},{7,6},{9,8},{10,9},{11,10},{13,12},{... | collective-permute-start | bytes 589832 | tf_op jit(solution)/shard_map/ppermute | solution.py:720
  3.5 9.7 %collective-permute-start = (bf16[12,2,16,256]{3,2,1,0:T(8,128)(2,1)S(1)}, bf16[12,2,16,256]{3,2,1,0:T(8,128)(2,1)S(1)}, u32[]{:S(2)}, u32[]{:S(2)}) collective-permute-start(bf16[12,2,16,256]{3,2,1,0:T(8,128)(2,1)S(1)} %get-tuple-element.169), channel_id=1, source_target_pairs={{0,1},{1,2},{2,3},{4,5},{5,6},{6,7},{8,9},{9,10},{10,11},{12,13},{... | collective-permute-start | bytes 589832 | tf_op jit(solution)/shard_map/ppermute | solution.py:719
  9.0 3.5 %collective-permute-start.2 = (s32[1,256]{1,0:T(1,128)}, s32[1,256]{1,0:T(1,128)S(1)}, u32[]{:S(2)}, u32[]{:S(2)}) collective-permute-start(s32[1,256]{1,0:T(1,128)} %bitcast.31), channel_id=1, source_target_pairs={{0,4},{4,0},{8,12},{12,8},{16,20},{20,16},{24,28},{28,24},{1,5},{5... | collective-permute-start | bytes 3080 | tf_op jit(solution)/shard_map/ppermute | solution.py:744
  47.6 12.5 %collective-permute-start.3 = (bf16[16,16,256]{2,1,0:T(8,128)(2,1)}, bf16[16,16,256]{2,1,0:T(8,128)(2,1)S(1)}, u32[]{:S(2)}, u32[]{:S(2)}) collective-permute-start(bf16[16,16,256]{2,1,0:T(8,128)(2,1)} %get-tuple-element.108), channel_id=1, source_target_pairs={{0,1},{1,2},{2,3},{4,5},{5,6},{6,7},{8,9},{9,10},{10,11},{12,13},{... | collective-permute-start | bytes 393224 | tf_op jit(solution)/shard_map/ppermute | solution.py:719
  52.0 8.1 %collective-permute-start.4 = (bf16[16,16,256]{2,1,0:T(8,128)(2,1)}, bf16[16,16,256]{2,1,0:T(8,128)(2,1)S(1)}, u32[]{:S(2)}, u32[]{:S(2)}) collective-permute-start(bf16[16,16,256]{2,1,0:T(8,128)(2,1)} %get-tuple-element.109), channel_id=1, source_target_pairs={{1,0},{2,1},{3,2},{5,4},{6,5},{7,6},{9,8},{10,9},{11,10},{13,12},{... | collective-permute-start | bytes 393224 | tf_op jit(solution)/shard_map/ppermute | solution.py:720
  53.3 4.6 %collective-permute-start.7 = (f32[16,128]{1,0:T(8,128)S(1)}, f32[16,128]{1,0:T(8,128)S(1)}, u32[]{:S(2)}, u32[]{:S(2)}) collective-permute-start(f32[16,128]{1,0:T(8,128)S(1)} %get-tuple-element.114.refs_0_), channel_id=1, source_target_pairs={{0,24},{4,28},{8,16},{12,20},{16,8},{20,12},{24,0},{28,4},{1,25},{... | collective-permute-start | bytes 24584 | tf_op jit(solution)/shard_map/ppermute | solution.py:744
  56.0 3.7 %collective-permute-start.6 = (f32[16,128]{1,0:T(8,128)S(1)}, f32[16,128]{1,0:T(8,128)S(1)}, u32[]{:S(2)}, u32[]{:S(2)}) collective-permute-start(f32[16,128]{1,0:T(8,128)S(1)} %get-tuple-element.114.refs_0_), channel_id=1, source_target_pairs={{0,16},{4,20},{8,24},{12,28},{16,0},{20,4},{24,8},{28,12},{1,17},{... | collective-permute-start | bytes 24584 | tf_op jit(solution)/shard_map/ppermute | solution.py:744
  56.5 3.7 %collective-permute-start.5 = (f32[16,128]{1,0:T(8,128)S(1)}, f32[16,128]{1,0:T(8,128)S(1)}, u32[]{:S(2)}, u32[]{:S(2)}) collective-permute-start(f32[16,128]{1,0:T(8,128)S(1)} %get-tuple-element.114.refs_0_), channel_id=1, source_target_pairs={{0,8},{4,12},{8,0},{12,4},{16,24},{20,28},{24,16},{28,20},{1,9},{5... | collective-permute-start | bytes 24584 | tf_op jit(solution)/shard_map/ppermute | solution.py:744
  63.9 11.2 %collective-permute-start.8 = (bf16[16,16,256]{2,1,0:T(8,128)(2,1)}, bf16[16,16,256]{2,1,0:T(8,128)(2,1)S(1)}, u32[]{:S(2)}, u32[]{:S(2)}) collective-permute-start(bf16[16,16,256]{2,1,0:T(8,128)(2,1)} %get-tuple-element.116), channel_id=1, source_target_pairs={{0,1},{1,2},{2,3},{4,5},{5,6},{6,7},{8,9},{9,10},{10,11},{12,13},{... | collective-permute-start | bytes 393224 | tf_op jit(solution)/shard_map/ppermute | solution.py:719
  68.4 7.1 %collective-permute-start.9 = (bf16[16,16,256]{2,1,0:T(8,128)(2,1)}, bf16[16,16,256]{2,1,0:T(8,128)(2,1)S(1)}, u32[]{:S(2)}, u32[]{:S(2)}) collective-permute-start(bf16[16,16,256]{2,1,0:T(8,128)(2,1)} %get-tuple-element.117), channel_id=1, source_target_pairs={{1,0},{2,1},{3,2},{5,4},{6,5},{7,6},{9,8},{10,9},{11,10},{13,12},{... | collective-permute-start | bytes 393224 | tf_op jit(solution)/shard_map/ppermute | solution.py:720
  75.5 83.1 %copy-start = (f32[512,512]{1,0:T(8,128)S(1)}, f32[512,512]{1,0:T(8,128)}, u32[]{:S(2)}) copy-start(f32[512,512]{1,0:T(8,128)} %refs_5_.1) | copy-start | bytes 3145732
  75.5 83.1 %copy-start.1 = (f32[9,12,512]{2,1,0:T(8,128)S(1)}, f32[9,12,512]{2,1,0:T(8,128)}, u32[]{:S(2)}) copy-start(f32[9,12,512]{2,1,0:T(8,128)} %refs_6_.1) | copy-start | bytes 663556
  75.5 83.1 %copy-start.2 = (f32[512,512]{1,0:T(8,128)S(1)}, f32[512,512]{1,0:T(8,128)}, u32[]{:S(2)}) copy-start(f32[512,512]{1,0:T(8,128)} %refs_13_.1) | copy-start | bytes 3145732
  75.5 83.1 %copy-start.3 = (f32[512,512]{1,0:T(8,128)S(1)}, f32[512,512]{1,0:T(8,128)}, u32[]{:S(2)}) copy-start(f32[512,512]{1,0:T(8,128)} %refs_21_.1) | copy-start | bytes 3145732
  75.5 83.1 %copy-start.4 = (f32[9,512,6]{1,2,0:T(8,128)S(1)}, f32[9,512,6]{1,2,0:T(8,128)}, u32[]{:S(2)}) copy-start(f32[9,512,6]{1,2,0:T(8,128)} %param.30) | copy-start | bytes 331780
  75.5 83.1 %copy-start.5 = (f32[9,48,24]{1,2,0:T(8,128)S(1)}, f32[9,48,24]{1,2,0:T(8,128)}, u32[]{:S(2)}) copy-start(f32[9,48,24]{1,2,0:T(8,128)} %param.33) | copy-start | bytes 124420
  75.5 83.1 %copy-start.6 = (f32[9,12,512]{2,1,0:T(8,128)S(1)}, f32[9,12,512]{2,1,0:T(8,128)}, u32[]{:S(2)}) copy-start(f32[9,12,512]{2,1,0:T(8,128)} %refs_14_.1) | copy-start | bytes 663556
  75.5 83.1 %copy-start.7 = (f32[9,12,512]{2,1,0:T(8,128)S(1)}, f32[9,12,512]{2,1,0:T(8,128)}, u32[]{:S(2)}) copy-start(f32[9,12,512]{2,1,0:T(8,128)} %refs_22_.1) | copy-start | bytes 663556
  75.5 83.1 %copy-start.8 = (f32[9,512,6]{1,2,0:T(8,128)S(1)}, f32[9,512,6]{1,2,0:T(8,128)}, u32[]{:S(2)}) copy-start(f32[9,512,6]{1,2,0:T(8,128)} %param.38) | copy-start | bytes 331780
  75.5 83.1 %copy-start.9 = (f32[9,512,6]{1,2,0:T(8,128)S(1)}, f32[9,512,6]{1,2,0:T(8,128)}, u32[]{:S(2)}) copy-start(f32[9,512,6]{1,2,0:T(8,128)} %param.46) | copy-start | bytes 331780
  75.6 83.1 %copy-start.10 = (f32[9,48,24]{1,2,0:T(8,128)S(1)}, f32[9,48,24]{1,2,0:T(8,128)}, u32[]{:S(2)}) copy-start(f32[9,48,24]{1,2,0:T(8,128)} %param.41) | copy-start | bytes 124420
  75.6 83.1 %copy-start.11 = (f32[9,48,24]{1,2,0:T(8,128)S(1)}, f32[9,48,24]{1,2,0:T(8,128)}, u32[]{:S(2)}) copy-start(f32[9,48,24]{1,2,0:T(8,128)} %param.49) | copy-start | bytes 124420
  75.6 83.1 %copy-start.12 = (f32[12,12]{1,0:T(8,128)S(1)}, f32[12,12]{1,0:T(8,128)}, u32[]{:S(2)}) copy-start(f32[12,12]{1,0:T(8,128)} %refs_10_.1) | copy-start | bytes 1732
  75.6 83.1 %copy-start.13 = (f32[10,96]{1,0:T(8,128)S(1)}, f32[10,96]{1,0:T(8,128)}, u32[]{:S(2)}) copy-start(f32[10,96]{1,0:T(8,128)} %refs_11_.1) | copy-start | bytes 11524
  75.6 83.1 %copy-start.14 = (f32[2,512]{1,0:T(2,128)S(1)}, f32[2,512]{1,0:T(2,128)}, u32[]{:S(2)}) copy-start(f32[2,512]{1,0:T(2,128)} %refs_8_.1) | copy-start | bytes 12292
  75.6 83.1 %copy-start.15 = (f32[3,12]{1,0:T(4,128)S(1)}, f32[3,12]{1,0:T(4,128)}, u32[]{:S(2)}) copy-start(f32[3,12]{1,0:T(4,128)} %refs_9_.1) | copy-start | bytes 436
  75.6 83.1 %copy-start.16 = (f32[12,12]{1,0:T(8,128)S(1)}, f32[12,12]{1,0:T(8,128)}, u32[]{:S(2)}) copy-start(f32[12,12]{1,0:T(8,128)} %refs_18_.1) | copy-start | bytes 1732
  75.6 83.1 %copy-start.17 = (f32[10,96]{1,0:T(8,128)S(1)}, f32[10,96]{1,0:T(8,128)}, u32[]{:S(2)}) copy-start(f32[10,96]{1,0:T(8,128)} %refs_19_.1) | copy-start | bytes 11524
  75.7 83.1 %copy-start.18 = (f32[12,12]{1,0:T(8,128)S(1)}, f32[12,12]{1,0:T(8,128)}, u32[]{:S(2)}) copy-start(f32[12,12]{1,0:T(8,128)} %refs_26_.1) | copy-start | bytes 1732
  75.7 83.1 %copy-start.19 = (f32[10,96]{1,0:T(8,128)S(1)}, f32[10,96]{1,0:T(8,128)}, u32[]{:S(2)}) copy-start(f32[10,96]{1,0:T(8,128)} %refs_27_.1) | copy-start | bytes 11524
  75.7 83.1 %copy-start.20 = (f32[16,128]{1,0:T(8,128)S(1)}, f32[16,128]{1,0:T(8,128)}, u32[]{:S(2)}) copy-start(f32[16,128]{1,0:T(8,128)} %get-tuple-element.141.refs_3_) | copy-start | bytes 24580
  75.7 83.0 %copy-start.23 = (f32[2,512]{1,0:T(2,128)S(1)}, f32[2,512]{1,0:T(2,128)}, u32[]{:S(2)}) copy-start(f32[2,512]{1,0:T(2,128)} %refs_16_.1) | copy-start | bytes 12292
  75.7 83.0 %copy-start.24 = (f32[2,512]{1,0:T(2,128)S(1)}, f32[2,512]{1,0:T(2,128)}, u32[]{:S(2)}) copy-start(f32[2,512]{1,0:T(2,128)} %refs_24_.1) | copy-start | bytes 12292
  75.7 83.0 %copy-start.25 = (f32[3,12]{1,0:T(4,128)S(1)}, f32[3,12]{1,0:T(4,128)}, u32[]{:S(2)}) copy-start(f32[3,12]{1,0:T(4,128)} %refs_17_.1) | copy-start | bytes 436
  117.0 2.1 %collective-permute-start.10 = (bf16[16,32,512]{2,1,0:T(8,128)(2,1)}, bf16[16,32,512]{2,1,0:T(8,128)(2,1)S(1)}, u32[]{:S(2)}, u32[]{:S(2)}) collective-permute-start(bf16[16,32,512]{2,1,0:T(8,128)(2,1)} %get-tuple-element.132), channel_id=1, source_target_pairs={{0,4},{4,0},{8,12},{12,8},{16,20},{20,16},{24,28},{28,24},{1,5},{5... | collective-permute-start | bytes 1572872 | tf_op jit(solution)/shard_map/ppermute | solution.py:744
  120.4 6.4 %collective-permute-start.11 = (bf16[4,32,512]{2,1,0:T(8,128)(2,1)S(1)}, bf16[4,32,512]{2,1,0:T(8,128)(2,1)S(1)}, u32[]{:S(2)}, u32[]{:S(2)}) collective-permute-start(bf16[4,32,512]{2,1,0:T(8,128)(2,1)S(1)} %get-tuple-element.134), channel_id=1, source_target_pairs={{0,8},{4,12},{8,0},{12,4},{16,24},{20,28},{24,16},{28,20},{1,9},{5... | collective-permute-start | bytes 393224 | tf_op jit(solution)/shard_map/ppermute | solution.py:744
  120.8 7.3 %collective-permute-start.12 = (bf16[4,32,512]{2,1,0:T(8,128)(2,1)S(1)}, bf16[4,32,512]{2,1,0:T(8,128)(2,1)S(1)}, u32[]{:S(2)}, u32[]{:S(2)}) collective-permute-start(bf16[4,32,512]{2,1,0:T(8,128)(2,1)S(1)} %get-tuple-element.135), channel_id=1, source_target_pairs={{0,16},{4,20},{8,24},{12,28},{16,0},{20,4},{24,8},{28,12},{1,17},{... | collective-permute-start | bytes 393224 | tf_op jit(solution)/shard_map/ppermute | solution.py:744
  122.5 7.3 %collective-permute-start.13 = (bf16[4,32,512]{2,1,0:T(8,128)(2,1)S(1)}, bf16[4,32,512]{2,1,0:T(8,128)(2,1)S(1)}, u32[]{:S(2)}, u32[]{:S(2)}) collective-permute-start(bf16[4,32,512]{2,1,0:T(8,128)(2,1)S(1)} %get-tuple-element.136), channel_id=1, source_target_pairs={{0,24},{4,28},{8,16},{12,20},{16,8},{20,12},{24,0},{28,4},{1,25},{... | collective-permute-start | bytes 393224 | tf_op jit(solution)/shard_map/ppermute | solution.py:744
  130.3 6.7 %collective-permute-start.14 = (bf16[32,512]{1,0:T(8,128)(2,1)S(1)}, bf16[32,512]{1,0:T(8,128)(2,1)S(1)}, u32[]{:S(2)}, u32[]{:S(2)}) collective-permute-start(bf16[32,512]{1,0:T(8,128)(2,1)S(1)} %get-tuple-element.138), channel_id=1, source_target_pairs={{0,1},{1,2},{2,3},{3,0},{4,5},{5,6},{6,7},{7,4},{8,9},{9,10},{10,1... | collective-permute-start | bytes 98312 | tf_op jit(solution)/shard_map/ppermute | solution.py:916
  132.6 4.9 %collective-permute-start.15 = (bf16[32,512]{1,0:T(8,128)(2,1)S(1)}, bf16[32,512]{1,0:T(8,128)(2,1)S(1)}, u32[]{:S(2)}, u32[]{:S(2)}) collective-permute-start(bf16[32,512]{1,0:T(8,128)(2,1)S(1)} %get-tuple-element.139), channel_id=1, source_target_pairs={{0,2},{1,3},{2,0},{3,1},{4,6},{5,7},{6,4},{7,5},{8,10},{9,11},{10,... | collective-permute-start | bytes 98312 | tf_op jit(solution)/shard_map/ppermute | solution.py:916
  135.2 3.9 %collective-permute-start.16 = (bf16[32,512]{1,0:T(8,128)(2,1)S(1)}, bf16[32,512]{1,0:T(8,128)(2,1)S(1)}, u32[]{:S(2)}, u32[]{:S(2)}) collective-permute-start(bf16[32,512]{1,0:T(8,128)(2,1)S(1)} %get-tuple-element.140), channel_id=1, source_target_pairs={{0,3},{1,0},{2,1},{3,2},{4,7},{5,4},{6,5},{7,6},{8,11},{9,8},{10,9... | collective-permute-start | bytes 98312 | tf_op jit(solution)/shard_map/ppermute | solution.py:916
  139.2 4.8 %collective-permute-start.19 = (bf16[32,512]{1,0:T(8,128)(2,1)S(1)}, bf16[32,512]{1,0:T(8,128)(2,1)S(1)}, u32[]{:S(2)}, u32[]{:S(2)}) collective-permute-start(bf16[32,512]{1,0:T(8,128)(2,1)S(1)} %total.1.refs_0_), channel_id=1, source_target_pairs={{0,3},{1,0},{2,1},{3,2},{4,7},{5,4},{6,5},{7,6},{8,11},{9,8},{10,9... | collective-permute-start | bytes 98312 | tf_op jit(solution)/shard_map/ppermute | solution.py:916
  142.4 4.8 %collective-permute-start.18 = (bf16[32,512]{1,0:T(8,128)(2,1)S(1)}, bf16[32,512]{1,0:T(8,128)(2,1)S(1)}, u32[]{:S(2)}, u32[]{:S(2)}) collective-permute-start(bf16[32,512]{1,0:T(8,128)(2,1)S(1)} %total.1.refs_0_), channel_id=1, source_target_pairs={{0,2},{1,3},{2,0},{3,1},{4,6},{5,7},{6,4},{7,5},{8,10},{9,11},{10,... | collective-permute-start | bytes 98312 | tf_op jit(solution)/shard_map/ppermute | solution.py:916
  142.4 5.7 %collective-permute-start.17 = (bf16[32,512]{1,0:T(8,128)(2,1)S(1)}, bf16[32,512]{1,0:T(8,128)(2,1)S(1)}, u32[]{:S(2)}, u32[]{:S(2)}) collective-permute-start(bf16[32,512]{1,0:T(8,128)(2,1)S(1)} %total.1.refs_0_), channel_id=1, source_target_pairs={{0,1},{1,2},{2,3},{3,0},{4,5},{5,6},{6,7},{7,4},{8,9},{9,10},{10,1... | collective-permute-start | bytes 98312 | tf_op jit(solution)/shard_map/ppermute | solution.py:916
  148.6 6.0 %collective-permute-start.22 = (bf16[4,32,512]{2,1,0:T(8,128)(2,1)S(1)}, bf16[4,32,512]{2,1,0:T(8,128)(2,1)S(1)}, u32[]{:S(2)}, u32[]{:S(2)}) collective-permute-start(bf16[4,32,512]{2,1,0:T(8,128)(2,1)S(1)} %gather_band.1.refs_0_), channel_id=1, source_target_pairs={{0,24},{4,28},{8,16},{12,20},{16,8},{20,12},{24,0},{28,4},{1,25},{... | collective-permute-start | bytes 393224 | tf_op jit(solution)/shard_map/ppermute | solution.py:744
  150.5 5.5 %collective-permute-start.21 = (bf16[4,32,512]{2,1,0:T(8,128)(2,1)S(1)}, bf16[4,32,512]{2,1,0:T(8,128)(2,1)S(1)}, u32[]{:S(2)}, u32[]{:S(2)}) collective-permute-start(bf16[4,32,512]{2,1,0:T(8,128)(2,1)S(1)} %gather_band.1.refs_0_), channel_id=1, source_target_pairs={{0,16},{4,20},{8,24},{12,28},{16,0},{20,4},{24,8},{28,12},{1,17},{... | collective-permute-start | bytes 393224 | tf_op jit(solution)/shard_map/ppermute | solution.py:744
  151.0 5.0 %collective-permute-start.20 = (bf16[4,32,512]{2,1,0:T(8,128)(2,1)S(1)}, bf16[4,32,512]{2,1,0:T(8,128)(2,1)S(1)}, u32[]{:S(2)}, u32[]{:S(2)}) collective-permute-start(bf16[4,32,512]{2,1,0:T(8,128)(2,1)S(1)} %gather_band.1.refs_0_), channel_id=1, source_target_pairs={{0,8},{4,12},{8,0},{12,4},{16,24},{20,28},{24,16},{28,20},{1,9},{5... | collective-permute-start | bytes 393224 | tf_op jit(solution)/shard_map/ppermute | solution.py:744
  156.6 2.0 %collective-permute-start.23 = (bf16[16,32,512]{2,1,0:T(8,128)(2,1)S(1)}, bf16[16,32,512]{2,1,0:T(8,128)(2,1)S(1)}, u32[]{:S(2)}, u32[]{:S(2)}) collective-permute-start(bf16[16,32,512]{2,1,0:T(8,128)(2,1)S(1)} %bitcast.21), channel_id=1, source_target_pairs={{0,4},{4,0},{8,12},{12,8},{16,20},{20,16},{24,28},{28,24},{1,5},{5... | collective-permute-start | bytes 1572872 | tf_op jit(solution)/shard_map/ppermute | solution.py:744
  (3 other events, 177.0 us)

commit v5 on v4

--- a/solution.py
+++ b/solution.py
@@ -431,24 +431,23 @@
 
 
 def backward_kernel(cols, sub, act1, sg1, act2, sg2, place, dn, dn_top, dn_bottom, xa2, xt, mixth, woutt, wt,
-                    dprior, small, keep, send, packed, dnp, taps, gtaps, bias_acc, wfield, gout, gin):
+                    dprior, small, keep, send, packed, dnp, taps, gtaps, bias_acc, wfield, gout, gin, turned, turned2):
     step = pl.program_id(0)
     rows, width, _, count = dn.shape
     groups = width // cols
+    hidden = mixth.shape[0]
 
     @pl.when(step == 0)
     def _():
         packed[...] = jnp.zeros_like(packed)
-        gout[...] = jnp.zeros_like(gout)
-        gin[...] = jnp.zeros_like(gin)
+        turned2[...] = jnp.zeros_like(turned2)
         bias_acc[...] = jnp.zeros_like(bias_acc)
-        wfield[...] = jnp.zeros_like(wfield)
+        turned[...] = jnp.zeros_like(turned)
         dnp[...] = jnp.zeros_like(dnp)
         dnp[0, 1 : width + 1] = dn_top[...]
         dnp[1 : rows + 1, 1 : width + 1] = dn[...]
         dnp[rows + 1, 1 : width + 1] = dn_bottom[...]
         taps[240:256, :] = jnp.zeros_like(taps[240:256, :])
-        gtaps[144:256, :] = jnp.zeros_like(gtaps[144:256, :])
 
     row = step // groups
     start = (step % groups) * cols
@@ -464,21 +463,23 @@
     size = sub * count
     for s in range(cols // sub):
         lanes = pl.ds(s * size, size)
-        grad2 = (dot(woutt[...], gtaps[:, lanes]) * sg2[0, :, lanes].astype(F32)).astype(BF16)
+        grad2 = (dot(woutt[:, 0:144], gtaps[0:144, lanes]) * sg2[0, :, lanes].astype(F32)).astype(BF16)
         grad1 = (dot(mixth[...], grad2) * sg1[0, :, lanes].astype(F32)).astype(BF16)
         wide = grad2.astype(F32)
         bias = wide[:, 0:128]
         for k in range(1, size // 128):
             bias = bias + wide[:, k * 128 : (k + 1) * 128]
         bias_acc[...] += bias
-        gout[...] += dot(gtaps[0:144, lanes], act2[0, :, lanes], NT)
+        turned2[...] += dot(act2[0, :, lanes], gtaps[0:144, lanes], NT)
         packed[ROW_MIX:ROW_OUT, :] += dot(grad2, act1[0, :, lanes], NT)
-        gathered = dot(taps[0:240, lanes], grad1, NT)
-        gin[...] += gathered[0:96]
-        wfield[...] += gathered[96:240]
+        turned[...] += dot(grad1, taps[:, lanes], NT)
 
     @pl.when(step == rows * groups - 1)
     def _():
+        gathered = turned[...].T
+        gin[...] = gathered[0:96]
+        gout[...] = jnp.concatenate([turned2[...], jnp.zeros((hidden, 112), F32)], axis=1).T[0:144]
+        wfield[...] = gathered[96:240]
         for tap in range(9):
             at = ROW_OUT + 12 * tap
             packed[at : at + 6, :] = gout[16 * tap : 16 * tap + 6, :]
@@ -892,11 +893,13 @@
             pltpu.VMEM((devices * each, hidden), F32),
             pltpu.VMEM((rows + 2, width + 2, 16, count), BF16),
             pltpu.VMEM((256, size), BF16),
-            pltpu.VMEM((256, size), BF16),
+            pltpu.VMEM((144, size), BF16),
             pltpu.VMEM((hidden, 128), F32),
             pltpu.VMEM((144, hidden), F32),
             pltpu.VMEM((144, hidden), F32),
             pltpu.VMEM((96, hidden), F32),
+            pltpu.VMEM((hidden, 256), F32),
+            pltpu.VMEM((hidden, 144), F32),
         ],
         compiler_params=params_of(VMEM_MIB),
         name="backward",

time: 166 us -> 164 us (0.988)
  no operation moved by 1% of the time
where the time goes in v5:
time: 164 us
  Pallas kernels  95.9 us (58%)
  starting transfers between devices  39.4 us (24%)
  waiting for transfers between devices  25.5 us (16%)
  other arithmetic  1.65 us (1%)
    pallas_call x1, Pallas kernels, body(): pl.pallas_call(functools.partial(backward_kernel, cols, sub), grid=(steps...  40.1 us
    pallas_call x1, Pallas kernels, body(): pl.pallas_call(functools.partial(forward_kernel, cols, sub), grid=(steps,...  34.4 us
    ppermute x12, waiting for transfers between devices, swap(): return lax.ppermute(array, 'dp', pairs)  16.9 us
    ppermute x3, starting transfers between devices, exchange_rows(): before = lax.ppermute(down, 'band', [(i, i + 1) for i in range(count - 1)])  14.5 us
    ppermute x12, starting transfers between devices, swap(): return lax.ppermute(array, 'dp', pairs)  10.8 us
    ppermute x6, starting transfers between devices, turn(): lax.ppermute(array, 'band', [(i, (i + k) % bands) for i in range(bands)])  10.1 us
    pallas_call x2, Pallas kernels, local(): pl.pallas_call(kernel, out_shape=outs, in_specs=[whole for _ in inputs],...  8.74 us
    ppermute x6, waiting for transfers between devices, turn(): lax.ppermute(array, 'band', [(i, (i + k) % bands) for i in range(bands)])  7.64 us
  transfers between devices with their start and end apart: 24, of which 18 were waited for; matrix products, arithmetic and copies ran while one was open for 0% of the time, Pallas kernels for 5%

profile of v5, /device:TPU:0, one launch (start us, length us, event | category | flops | bytes accessed | tf_op | source)
XLA Modules:
  0.0 164.0 jit_solution(4995890912954676400)
XLA Ops:
  0.7 1.5 add_convert_fusion
  2.2 1.3 collective-permute-start.1
  3.5 5.6 %collective-permute-start = (bf16[12,2,16,256]{3,2,1,0:T(8,128)(2,1)S(1)}, bf16[12,2,16,256]{3,2,1,0:T(8,128)(2,1)S(1)}, u32[]{:S(2)}, u32[]{:S(2)}) collective-permute-start(bf16[12,2,16,256]{3,2,1,0:T(8,128)(2,1)S(1)} %get-tuple-element.169), channel_id=1, source_target_pairs={{0,1},{1,2},{2,3},{4,5},{5,6},{6,7},{8,9},{9,10},{10,11},{12,13},{... | collective-permute-start | bytes 589832 | tf_op jit(solution)/shard_map/ppermute | solution.py:720
  9.2 3.4 %weights.1 = (bf16[512,128]{1,0:T(8,128)(2,1)}, f32[128,512]{1,0:T(8,128)}, bf16[512,512]{1,0:T(8,128)(2,1)}, bf16[512,512]{1,0:T(8,128)(2,1)}, f32[512,128]{1,0...) custom-call(f32[9,6,512]{2,1,0:T(8,128)} %bitcast.23, ...), custom_call_target="tpu_custom_call" | custom-call | tf_op jit(solution)/shard_map/weights/pallas_call | solution.py:753
  12.6 0.6 collective-permute-done.top
  13.2 34.4 %forward.1 = (bf16[8,512,2048]{2,1,0:T(8,128)(2,1)}, bf16[8,512,2048]{2,1,0:T(8,128)(2,1)}, bf16[8,512,2048]{2,1,0:T(8,128)(2,1)}, bf16[8,512,2048]{2,1,0:T(8,12...) custom-call(f32[12,4,16,256]{3,2,1,0:T(8,128)} %images.1, ...), custom_call_target="tpu_custom_call" | custom-call | flops 13153337344 | bytes 67108864 | tf_op jit(solution)/shard_map/forward/pallas_call | solution.py:788
  47.6 4.4 %collective-permute-start.3 = (bf16[16,16,256]{2,1,0:T(8,128)(2,1)}, bf16[16,16,256]{2,1,0:T(8,128)(2,1)S(1)}, u32[]{:S(2)}, u32[]{:S(2)}) collective-permute-start(bf16[16,16,256]{2,1,0:T(8,128)(2,1)} %get-tuple-element.108), channel_id=1, source_target_pairs={{0,1},{1,2},{2,3},{4,5},{5,6},{6,7},{8,9},{9,10},{10,11},{12,13},{... | collective-permute-start | bytes 393224 | tf_op jit(solution)/shard_map/ppermute | solution.py:720
  52.0 1.3 collective-permute-start.4
  53.3 2.7 %collective-permute-start.7 = (f32[16,128]{1,0:T(8,128)S(1)}, f32[16,128]{1,0:T(8,128)S(1)}, u32[]{:S(2)}, u32[]{:S(2)}) collective-permute-start(f32[16,128]{1,0:T(8,128)S(1)} %get-tuple-element.114.refs_0_), channel_id=1, source_target_pairs={{0,24},{4,28},{8,16},{12,20},{16,8},{20,12},{24,0},{28,4},{1,25},{... | collective-permute-start | bytes 24584 | tf_op jit(solution)/shard_map/ppermute | solution.py:745
  56.0 0.5 collective-permute-start.6
  56.9 1.1 collective-permute-done.7.refs_3_
  57.9 1.7 %collective-permute-done.6.refs_2_ = f32[16,128]{1,0:T(8,128)S(1)} collective-permute-done((f32[16,128]{1,0:T(8,128)S(1)}, f32[16,128]{1,0:T(8,128)S(1)}, u32[]{:S(2)}, u32[]{:S(2)}) %collective-permute-start.6) | collective-permute-done | bytes 8224 | tf_op jit(solution)/shard_map/ppermute | solution.py:745
  59.6 0.5 collective-permute-done.5.refs_1_
  60.2 3.7 %coupling.1 = (bf16[4,16,16,256]{3,2,1,0:T(8,128)(2,1)}, bf16[16,16,256]{2,1,0:T(8,128)(2,1)}, bf16[16,16,256]{2,1,0:T(8,128)(2,1)}, f32[2,64,2048]{2,1,0:T(8,12...) custom-call(f32[4,16,16,256]{3,2,1,0:T(8,128)} %get-tuple-element.107.nn, ...), custom_call_target="tpu_custom_call" | custom-call | tf_op jit(solution)/shard_map/coupling/pallas_call | solution.py:825
  63.9 4.5 %collective-permute-start.8 = (bf16[16,16,256]{2,1,0:T(8,128)(2,1)}, bf16[16,16,256]{2,1,0:T(8,128)(2,1)S(1)}, u32[]{:S(2)}, u32[]{:S(2)}) collective-permute-start(bf16[16,16,256]{2,1,0:T(8,128)(2,1)} %get-tuple-element.116), channel_id=1, source_target_pairs={{0,1},{1,2},{2,3},{4,5},{5,6},{6,7},{8,9},{9,10},{10,11},{12,13},{... | collective-permute-start | bytes 393224 | tf_op jit(solution)/shard_map/ppermute | solution.py:720
  68.4 1.5 collective-permute-start.9
  70.0 5.1 %prior_grads.1 = (f32[288,128]{1,0:T(8,128)}, f32[16,512]{1,0:T(8,128)}) custom-call(bf16[4,16,16,256]{3,2,1,0:T(8,128)(2,1)} %get-tuple-element.115.dn, f32[2,64,2048]{2,1,0:T(8,128)} %get-tuple-element.123.dstats, bf16[4,8,16,256]{3,2,1,0:T(8,128)(2,1)} %get-tuple-element.124.dxb, f32[8,256]{1,0:T(8,128)} %get-tuple-element.125.loss_part, ...), custom_call_target="tpu_custom_call" | custom-call | tf_op jit(solution)/shard_map/prior_grads/pallas_call | solution.py:825
  75.0 0.4 collective-permute-done.9.dn_bottom
  75.7 40.1 %backward.1 = (f32[16,24,512]{2,1,0:T(8,128)}, bf16[16,32,512]{2,1,0:T(8,128)(2,1)}) custom-call(bf16[8,512,2048]{2,1,0:T(8,128)(2,1)} %get-tuple-element.103.act1, bf16[8,512,2048]{2,1,0:T(8,128)(2,1)} %get-tuple-element.104.sg1, bf16[8,512,2048]{2,1,0:T(8,128)(2,1)} %get-tuple-element.105.act2, bf16[8,512,2048]{2,1,0:T(8,128)(2,1)} %get-tuple-element.106.sg2, ...), custom_call_target="tpu_custom_call" | custom-call | tf_op jit(solution)/shard_map/backward/pallas_call | solution.py:886
  115.8 2.1 %collective-permute-done.10.got = bf16[16,32,512]{2,1,0:T(8,128)(2,1)S(1)} collective-permute-done((bf16[16,32,512]{2,1,0:T(8,128)(2,1)}, bf16[16,32,512]{2,1,0:T(8,128)(2,1)S(1)}, u32[]{:S(2)}, u32[]{:S(2)}) %collective-permute-start.10) | collective-permute-done | bytes 524320 | tf_op jit(solution)/shard_map/ppermute | solution.py:745
  118.0 1.3 halve.1
  119.2 0.4 collective-permute-start.11
  119.7 1.7 %collective-permute-start.12 = (bf16[4,32,512]{2,1,0:T(8,128)(2,1)S(1)}, bf16[4,32,512]{2,1,0:T(8,128)(2,1)S(1)}, u32[]{:S(2)}, u32[]{:S(2)}) collective-permute-start(bf16[4,32,512]{2,1,0:T(8,128)(2,1)S(1)} %get-tuple-element.135), channel_id=1, source_target_pairs={{0,16},{4,20},{8,24},{12,28},{16,0},{20,4},{24,8},{28,12},{1,17},{... | collective-permute-start | bytes 393224 | tf_op jit(solution)/shard_map/ppermute | solution.py:745
  121.3 1.4 collective-permute-start.13
  122.8 2.9 %collective-permute-done.11.refs_1_ = bf16[4,32,512]{2,1,0:T(8,128)(2,1)S(1)} collective-permute-done((bf16[4,32,512]{2,1,0:T(8,128)(2,1)S(1)}, bf16[4,32,512]{2,1,0:T(8,128)(2,1)S(1)}, u32[]{:S(2)}, u32[]{:S(2)}) %collective-permute-start.11) | collective-permute-done | bytes 131104 | tf_op jit(solution)/shard_map/ppermute | solution.py:745
  125.6 1.3 collective-permute-done.12.refs_2_
  126.9 1.6 collective-permute-done.13.refs_3_
  128.6 0.6 spread.1
  129.2 2.3 %collective-permute-start.14 = (bf16[32,512]{1,0:T(8,128)(2,1)S(1)}, bf16[32,512]{1,0:T(8,128)(2,1)S(1)}, u32[]{:S(2)}, u32[]{:S(2)}) collective-permute-start(bf16[32,512]{1,0:T(8,128)(2,1)S(1)} %get-tuple-element.138), channel_id=1, source_target_pairs={{0,1},{1,2},{2,3},{3,0},{4,5},{5,6},{6,7},{7,4},{8,9},{9,10},{10,1... | collective-permute-start | bytes 98312 | tf_op jit(solution)/shard_map/ppermute | solution.py:919
  131.5 2.6 %collective-permute-start.15 = (bf16[32,512]{1,0:T(8,128)(2,1)S(1)}, bf16[32,512]{1,0:T(8,128)(2,1)S(1)}, u32[]{:S(2)}, u32[]{:S(2)}) collective-permute-start(bf16[32,512]{1,0:T(8,128)(2,1)S(1)} %get-tuple-element.139), channel_id=1, source_target_pairs={{0,2},{1,3},{2,0},{3,1},{4,6},{5,7},{6,4},{7,5},{8,10},{9,11},{10,... | collective-permute-start | bytes 98312 | tf_op jit(solution)/shard_map/ppermute | solution.py:919
  134.1 1.3 collective-permute-start.16
  135.4 0.4 collective-permute-done.14.refs_0_
  135.9 0.6 collective-permute-done.15.refs_1_
  136.4 1.6 collective-permute-done.16.refs_2_
  138.0 3.2 %collective-permute-start.19 = (bf16[32,512]{1,0:T(8,128)(2,1)S(1)}, bf16[32,512]{1,0:T(8,128)(2,1)S(1)}, u32[]{:S(2)}, u32[]{:S(2)}) collective-permute-start(bf16[32,512]{1,0:T(8,128)(2,1)S(1)} %total.1.refs_0_), channel_id=1, source_target_pairs={{0,3},{1,0},{2,1},{3,2},{4,7},{5,4},{6,5},{7,6},{8,11},{9,8},{10,9... | collective-permute-start | bytes 98312 | tf_op jit(solution)/shard_map/ppermute | solution.py:919
  141.2 0.6 collective-permute-start.17
  141.9 1.0 collective-permute-done.19.refs_3_
  142.8 3.2 %collective-permute-done.18.refs_2_ = bf16[32,512]{1,0:T(8,128)(2,1)S(1)} collective-permute-done((bf16[32,512]{1,0:T(8,128)(2,1)S(1)}, bf16[32,512]{1,0:T(8,128)(2,1)S(1)}, u32[]{:S(2)}, u32[]{:S(2)}) %collective-permute-start.18) | collective-permute-done | bytes 32800 | tf_op jit(solution)/shard_map/ppermute | solution.py:919
  146.0 0.9 collective-permute-done.17.refs_1_
  146.9 0.6 gather_band.1.refs_0_
  147.5 1.8 %collective-permute-start.22 = (bf16[4,32,512]{2,1,0:T(8,128)(2,1)S(1)}, bf16[4,32,512]{2,1,0:T(8,128)(2,1)S(1)}, u32[]{:S(2)}, u32[]{:S(2)}) collective-permute-start(bf16[4,32,512]{2,1,0:T(8,128)(2,1)S(1)} %gather_band.1.refs_0_), channel_id=1, source_target_pairs={{0,24},{4,28},{8,16},{12,20},{16,8},{20,12},{24,0},{28,4},{1,25},{... | collective-permute-start | bytes 393224 | tf_op jit(solution)/shard_map/ppermute | solution.py:745
  149.3 0.5 collective-permute-start.21
  149.8 1.2 collective-permute-start.20
  151.1 2.4 %collective-permute-done.22.refs_3_ = bf16[4,32,512]{2,1,0:T(8,128)(2,1)S(1)} collective-permute-done((bf16[4,32,512]{2,1,0:T(8,128)(2,1)S(1)}, bf16[4,32,512]{2,1,0:T(8,128)(2,1)S(1)}, u32[]{:S(2)}, u32[]{:S(2)}) %collective-permute-start.22) | collective-permute-done | bytes 131104 | tf_op jit(solution)/shard_map/ppermute | solution.py:745
  153.5 1.3 collective-permute-done.21.refs_2_
  154.8 0.6 gather_chips.1
  155.5 1.9 %collective-permute-done.23.refs_2_ = bf16[16,32,512]{2,1,0:T(8,128)(2,1)S(1)} collective-permute-done((bf16[16,32,512]{2,1,0:T(8,128)(2,1)S(1)}, bf16[16,32,512]{2,1,0:T(8,128)(2,1)S(1)}, u32[]{:S(2)}, u32[]{:S(2)}) %collective-permute-start.23) | collective-permute-done | bytes 524320 | tf_op jit(solution)/shard_map/ppermute | solution.py:745
  157.6 6.2 %update.1 = (f32[1,1]{1,0:T(1,128)}, f32[1,1]{1,0:T(1,128)}, f32[9,6,512]{2,1,0:T(8,128)}, f32[512,512]{1,0:T(8,128)}, f32[9,12,512]{2,1,0:T(8,128)}, /*index=5*...) custom-call(s32[3]{0:T(128)S(1)} %pad_add_fusion.place.p.refs_0_, ...), custom_call_target="tpu_custom_call" | custom-call | tf_op jit(solution)/shard_map/update/pallas_call | solution.py:955
  (68 shorter events, 0.9 us)
Async XLA Ops:
  2.2 10.4 %collective-permute-start.1 = (bf16[12,2,16,256]{3,2,1,0:T(8,128)(2,1)S(1)}, bf16[12,2,16,256]{3,2,1,0:T(8,128)(2,1)S(1)}, u32[]{:S(2)}, u32[]{:S(2)}) collective-permute-start(bf16[12,2,16,256]{3,2,1,0:T(8,128)(2,1)S(1)} %get-tuple-element.168), channel_id=1, source_target_pairs={{1,0},{2,1},{3,2},{5,4},{6,5},{7,6},{9,8},{10,9},{11,10},{13,12},{... | collective-permute-start | bytes 589832 | tf_op jit(solution)/shard_map/ppermute | solution.py:721
  3.5 9.7 %collective-permute-start = (bf16[12,2,16,256]{3,2,1,0:T(8,128)(2,1)S(1)}, bf16[12,2,16,256]{3,2,1,0:T(8,128)(2,1)S(1)}, u32[]{:S(2)}, u32[]{:S(2)}) collective-permute-start(bf16[12,2,16,256]{3,2,1,0:T(8,128)(2,1)S(1)} %get-tuple-element.169), channel_id=1, source_target_pairs={{0,1},{1,2},{2,3},{4,5},{5,6},{6,7},{8,9},{9,10},{10,11},{12,13},{... | collective-permute-start | bytes 589832 | tf_op jit(solution)/shard_map/ppermute | solution.py:720
  9.0 3.5 %collective-permute-start.2 = (s32[1,256]{1,0:T(1,128)}, s32[1,256]{1,0:T(1,128)S(1)}, u32[]{:S(2)}, u32[]{:S(2)}) collective-permute-start(s32[1,256]{1,0:T(1,128)} %bitcast.31), channel_id=1, source_target_pairs={{0,4},{4,0},{8,12},{12,8},{16,20},{20,16},{24,28},{28,24},{1,5},{5... | collective-permute-start | bytes 3080 | tf_op jit(solution)/shard_map/ppermute | solution.py:745
  47.6 12.5 %collective-permute-start.3 = (bf16[16,16,256]{2,1,0:T(8,128)(2,1)}, bf16[16,16,256]{2,1,0:T(8,128)(2,1)S(1)}, u32[]{:S(2)}, u32[]{:S(2)}) collective-permute-start(bf16[16,16,256]{2,1,0:T(8,128)(2,1)} %get-tuple-element.108), channel_id=1, source_target_pairs={{0,1},{1,2},{2,3},{4,5},{5,6},{6,7},{8,9},{9,10},{10,11},{12,13},{... | collective-permute-start | bytes 393224 | tf_op jit(solution)/shard_map/ppermute | solution.py:720
  52.0 8.1 %collective-permute-start.4 = (bf16[16,16,256]{2,1,0:T(8,128)(2,1)}, bf16[16,16,256]{2,1,0:T(8,128)(2,1)S(1)}, u32[]{:S(2)}, u32[]{:S(2)}) collective-permute-start(bf16[16,16,256]{2,1,0:T(8,128)(2,1)} %get-tuple-element.109), channel_id=1, source_target_pairs={{1,0},{2,1},{3,2},{5,4},{6,5},{7,6},{9,8},{10,9},{11,10},{13,12},{... | collective-permute-start | bytes 393224 | tf_op jit(solution)/shard_map/ppermute | solution.py:721
  53.3 4.6 %collective-permute-start.7 = (f32[16,128]{1,0:T(8,128)S(1)}, f32[16,128]{1,0:T(8,128)S(1)}, u32[]{:S(2)}, u32[]{:S(2)}) collective-permute-start(f32[16,128]{1,0:T(8,128)S(1)} %get-tuple-element.114.refs_0_), channel_id=1, source_target_pairs={{0,24},{4,28},{8,16},{12,20},{16,8},{20,12},{24,0},{28,4},{1,25},{... | collective-permute-start | bytes 24584 | tf_op jit(solution)/shard_map/ppermute | solution.py:745
  56.0 3.7 %collective-permute-start.6 = (f32[16,128]{1,0:T(8,128)S(1)}, f32[16,128]{1,0:T(8,128)S(1)}, u32[]{:S(2)}, u32[]{:S(2)}) collective-permute-start(f32[16,128]{1,0:T(8,128)S(1)} %get-tuple-element.114.refs_0_), channel_id=1, source_target_pairs={{0,16},{4,20},{8,24},{12,28},{16,0},{20,4},{24,8},{28,12},{1,17},{... | collective-permute-start | bytes 24584 | tf_op jit(solution)/shard_map/ppermute | solution.py:745
  56.5 3.7 %collective-permute-start.5 = (f32[16,128]{1,0:T(8,128)S(1)}, f32[16,128]{1,0:T(8,128)S(1)}, u32[]{:S(2)}, u32[]{:S(2)}) collective-permute-start(f32[16,128]{1,0:T(8,128)S(1)} %get-tuple-element.114.refs_0_), channel_id=1, source_target_pairs={{0,8},{4,12},{8,0},{12,4},{16,24},{20,28},{24,16},{28,20},{1,9},{5... | collective-permute-start | bytes 24584 | tf_op jit(solution)/shard_map/ppermute | solution.py:745
  63.9 11.2 %collective-permute-start.8 = (bf16[16,16,256]{2,1,0:T(8,128)(2,1)}, bf16[16,16,256]{2,1,0:T(8,128)(2,1)S(1)}, u32[]{:S(2)}, u32[]{:S(2)}) collective-permute-start(bf16[16,16,256]{2,1,0:T(8,128)(2,1)} %get-tuple-element.116), channel_id=1, source_target_pairs={{0,1},{1,2},{2,3},{4,5},{5,6},{6,7},{8,9},{9,10},{10,11},{12,13},{... | collective-permute-start | bytes 393224 | tf_op jit(solution)/shard_map/ppermute | solution.py:720
  68.4 7.1 %collective-permute-start.9 = (bf16[16,16,256]{2,1,0:T(8,128)(2,1)}, bf16[16,16,256]{2,1,0:T(8,128)(2,1)S(1)}, u32[]{:S(2)}, u32[]{:S(2)}) collective-permute-start(bf16[16,16,256]{2,1,0:T(8,128)(2,1)} %get-tuple-element.117), channel_id=1, source_target_pairs={{1,0},{2,1},{3,2},{5,4},{6,5},{7,6},{9,8},{10,9},{11,10},{13,12},{... | collective-permute-start | bytes 393224 | tf_op jit(solution)/shard_map/ppermute | solution.py:721
  75.5 81.9 %copy-start = (f32[512,512]{1,0:T(8,128)S(1)}, f32[512,512]{1,0:T(8,128)}, u32[]{:S(2)}) copy-start(f32[512,512]{1,0:T(8,128)} %refs_5_.1) | copy-start | bytes 3145732
  75.5 81.9 %copy-start.1 = (f32[9,12,512]{2,1,0:T(8,128)S(1)}, f32[9,12,512]{2,1,0:T(8,128)}, u32[]{:S(2)}) copy-start(f32[9,12,512]{2,1,0:T(8,128)} %refs_6_.1) | copy-start | bytes 663556
  75.5 81.9 %copy-start.2 = (f32[512,512]{1,0:T(8,128)S(1)}, f32[512,512]{1,0:T(8,128)}, u32[]{:S(2)}) copy-start(f32[512,512]{1,0:T(8,128)} %refs_13_.1) | copy-start | bytes 3145732
  75.5 81.9 %copy-start.3 = (f32[512,512]{1,0:T(8,128)S(1)}, f32[512,512]{1,0:T(8,128)}, u32[]{:S(2)}) copy-start(f32[512,512]{1,0:T(8,128)} %refs_21_.1) | copy-start | bytes 3145732
  75.5 81.9 %copy-start.4 = (f32[9,512,6]{1,2,0:T(8,128)S(1)}, f32[9,512,6]{1,2,0:T(8,128)}, u32[]{:S(2)}) copy-start(f32[9,512,6]{1,2,0:T(8,128)} %param.30) | copy-start | bytes 331780
  75.5 81.9 %copy-start.5 = (f32[9,48,24]{1,2,0:T(8,128)S(1)}, f32[9,48,24]{1,2,0:T(8,128)}, u32[]{:S(2)}) copy-start(f32[9,48,24]{1,2,0:T(8,128)} %param.33) | copy-start | bytes 124420
  75.5 81.9 %copy-start.6 = (f32[9,12,512]{2,1,0:T(8,128)S(1)}, f32[9,12,512]{2,1,0:T(8,128)}, u32[]{:S(2)}) copy-start(f32[9,12,512]{2,1,0:T(8,128)} %refs_14_.1) | copy-start | bytes 663556
  75.5 81.9 %copy-start.7 = (f32[9,12,512]{2,1,0:T(8,128)S(1)}, f32[9,12,512]{2,1,0:T(8,128)}, u32[]{:S(2)}) copy-start(f32[9,12,512]{2,1,0:T(8,128)} %refs_22_.1) | copy-start | bytes 663556
  75.5 81.9 %copy-start.8 = (f32[9,512,6]{1,2,0:T(8,128)S(1)}, f32[9,512,6]{1,2,0:T(8,128)}, u32[]{:S(2)}) copy-start(f32[9,512,6]{1,2,0:T(8,128)} %param.38) | copy-start | bytes 331780
  75.5 81.9 %copy-start.9 = (f32[9,512,6]{1,2,0:T(8,128)S(1)}, f32[9,512,6]{1,2,0:T(8,128)}, u32[]{:S(2)}) copy-start(f32[9,512,6]{1,2,0:T(8,128)} %param.46) | copy-start | bytes 331780
  75.6 81.9 %copy-start.10 = (f32[9,48,24]{1,2,0:T(8,128)S(1)}, f32[9,48,24]{1,2,0:T(8,128)}, u32[]{:S(2)}) copy-start(f32[9,48,24]{1,2,0:T(8,128)} %param.41) | copy-start | bytes 124420
  75.6 81.9 %copy-start.11 = (f32[9,48,24]{1,2,0:T(8,128)S(1)}, f32[9,48,24]{1,2,0:T(8,128)}, u32[]{:S(2)}) copy-start(f32[9,48,24]{1,2,0:T(8,128)} %param.49) | copy-start | bytes 124420
  75.6 81.9 %copy-start.12 = (f32[12,12]{1,0:T(8,128)S(1)}, f32[12,12]{1,0:T(8,128)}, u32[]{:S(2)}) copy-start(f32[12,12]{1,0:T(8,128)} %refs_10_.1) | copy-start | bytes 1732
  75.6 81.9 %copy-start.13 = (f32[10,96]{1,0:T(8,128)S(1)}, f32[10,96]{1,0:T(8,128)}, u32[]{:S(2)}) copy-start(f32[10,96]{1,0:T(8,128)} %refs_11_.1) | copy-start | bytes 11524
  75.6 81.9 %copy-start.14 = (f32[2,512]{1,0:T(2,128)S(1)}, f32[2,512]{1,0:T(2,128)}, u32[]{:S(2)}) copy-start(f32[2,512]{1,0:T(2,128)} %refs_8_.1) | copy-start | bytes 12292
  75.6 81.9 %copy-start.15 = (f32[3,12]{1,0:T(4,128)S(1)}, f32[3,12]{1,0:T(4,128)}, u32[]{:S(2)}) copy-start(f32[3,12]{1,0:T(4,128)} %refs_9_.1) | copy-start | bytes 436
  75.6 81.9 %copy-start.16 = (f32[12,12]{1,0:T(8,128)S(1)}, f32[12,12]{1,0:T(8,128)}, u32[]{:S(2)}) copy-start(f32[12,12]{1,0:T(8,128)} %refs_18_.1) | copy-start | bytes 1732
  75.6 81.9 %copy-start.17 = (f32[10,96]{1,0:T(8,128)S(1)}, f32[10,96]{1,0:T(8,128)}, u32[]{:S(2)}) copy-start(f32[10,96]{1,0:T(8,128)} %refs_19_.1) | copy-start | bytes 11524
  75.7 81.9 %copy-start.18 = (f32[12,12]{1,0:T(8,128)S(1)}, f32[12,12]{1,0:T(8,128)}, u32[]{:S(2)}) copy-start(f32[12,12]{1,0:T(8,128)} %refs_26_.1) | copy-start | bytes 1732
  75.7 81.9 %copy-start.19 = (f32[10,96]{1,0:T(8,128)S(1)}, f32[10,96]{1,0:T(8,128)}, u32[]{:S(2)}) copy-start(f32[10,96]{1,0:T(8,128)} %refs_27_.1) | copy-start | bytes 11524
  75.7 81.9 %copy-start.20 = (f32[16,128]{1,0:T(8,128)S(1)}, f32[16,128]{1,0:T(8,128)}, u32[]{:S(2)}) copy-start(f32[16,128]{1,0:T(8,128)} %get-tuple-element.141.refs_3_) | copy-start | bytes 24580
  75.7 81.9 %copy-start.23 = (f32[2,512]{1,0:T(2,128)S(1)}, f32[2,512]{1,0:T(2,128)}, u32[]{:S(2)}) copy-start(f32[2,512]{1,0:T(2,128)} %refs_16_.1) | copy-start | bytes 12292
  75.7 81.9 %copy-start.24 = (f32[2,512]{1,0:T(2,128)S(1)}, f32[2,512]{1,0:T(2,128)}, u32[]{:S(2)}) copy-start(f32[2,512]{1,0:T(2,128)} %refs_24_.1) | copy-start | bytes 12292
  75.7 81.9 %copy-start.25 = (f32[3,12]{1,0:T(4,128)S(1)}, f32[3,12]{1,0:T(4,128)}, u32[]{:S(2)}) copy-start(f32[3,12]{1,0:T(4,128)} %refs_17_.1) | copy-start | bytes 436
  115.8 2.1 %collective-permute-start.10 = (bf16[16,32,512]{2,1,0:T(8,128)(2,1)}, bf16[16,32,512]{2,1,0:T(8,128)(2,1)S(1)}, u32[]{:S(2)}, u32[]{:S(2)}) collective-permute-start(bf16[16,32,512]{2,1,0:T(8,128)(2,1)} %get-tuple-element.132), channel_id=1, source_target_pairs={{0,4},{4,0},{8,12},{12,8},{16,20},{20,16},{24,28},{28,24},{1,5},{5... | collective-permute-start | bytes 1572872 | tf_op jit(solution)/shard_map/ppermute | solution.py:745
  119.2 6.4 %collective-permute-start.11 = (bf16[4,32,512]{2,1,0:T(8,128)(2,1)S(1)}, bf16[4,32,512]{2,1,0:T(8,128)(2,1)S(1)}, u32[]{:S(2)}, u32[]{:S(2)}) collective-permute-start(bf16[4,32,512]{2,1,0:T(8,128)(2,1)S(1)} %get-tuple-element.134), channel_id=1, source_target_pairs={{0,8},{4,12},{8,0},{12,4},{16,24},{20,28},{24,16},{28,20},{1,9},{5... | collective-permute-start | bytes 393224 | tf_op jit(solution)/shard_map/ppermute | solution.py:745
  119.7 7.3 %collective-permute-start.12 = (bf16[4,32,512]{2,1,0:T(8,128)(2,1)S(1)}, bf16[4,32,512]{2,1,0:T(8,128)(2,1)S(1)}, u32[]{:S(2)}, u32[]{:S(2)}) collective-permute-start(bf16[4,32,512]{2,1,0:T(8,128)(2,1)S(1)} %get-tuple-element.135), channel_id=1, source_target_pairs={{0,16},{4,20},{8,24},{12,28},{16,0},{20,4},{24,8},{28,12},{1,17},{... | collective-permute-start | bytes 393224 | tf_op jit(solution)/shard_map/ppermute | solution.py:745
  121.3 7.3 %collective-permute-start.13 = (bf16[4,32,512]{2,1,0:T(8,128)(2,1)S(1)}, bf16[4,32,512]{2,1,0:T(8,128)(2,1)S(1)}, u32[]{:S(2)}, u32[]{:S(2)}) collective-permute-start(bf16[4,32,512]{2,1,0:T(8,128)(2,1)S(1)} %get-tuple-element.136), channel_id=1, source_target_pairs={{0,24},{4,28},{8,16},{12,20},{16,8},{20,12},{24,0},{28,4},{1,25},{... | collective-permute-start | bytes 393224 | tf_op jit(solution)/shard_map/ppermute | solution.py:745
  129.2 6.7 %collective-permute-start.14 = (bf16[32,512]{1,0:T(8,128)(2,1)S(1)}, bf16[32,512]{1,0:T(8,128)(2,1)S(1)}, u32[]{:S(2)}, u32[]{:S(2)}) collective-permute-start(bf16[32,512]{1,0:T(8,128)(2,1)S(1)} %get-tuple-element.138), channel_id=1, source_target_pairs={{0,1},{1,2},{2,3},{3,0},{4,5},{5,6},{6,7},{7,4},{8,9},{9,10},{10,1... | collective-permute-start | bytes 98312 | tf_op jit(solution)/shard_map/ppermute | solution.py:919
  131.5 4.9 %collective-permute-start.15 = (bf16[32,512]{1,0:T(8,128)(2,1)S(1)}, bf16[32,512]{1,0:T(8,128)(2,1)S(1)}, u32[]{:S(2)}, u32[]{:S(2)}) collective-permute-start(bf16[32,512]{1,0:T(8,128)(2,1)S(1)} %get-tuple-element.139), channel_id=1, source_target_pairs={{0,2},{1,3},{2,0},{3,1},{4,6},{5,7},{6,4},{7,5},{8,10},{9,11},{10,... | collective-permute-start | bytes 98312 | tf_op jit(solution)/shard_map/ppermute | solution.py:919
  134.1 3.9 %collective-permute-start.16 = (bf16[32,512]{1,0:T(8,128)(2,1)S(1)}, bf16[32,512]{1,0:T(8,128)(2,1)S(1)}, u32[]{:S(2)}, u32[]{:S(2)}) collective-permute-start(bf16[32,512]{1,0:T(8,128)(2,1)S(1)} %get-tuple-element.140), channel_id=1, source_target_pairs={{0,3},{1,0},{2,1},{3,2},{4,7},{5,4},{6,5},{7,6},{8,11},{9,8},{10,9... | collective-permute-start | bytes 98312 | tf_op jit(solution)/shard_map/ppermute | solution.py:919
  138.0 4.8 %collective-permute-start.19 = (bf16[32,512]{1,0:T(8,128)(2,1)S(1)}, bf16[32,512]{1,0:T(8,128)(2,1)S(1)}, u32[]{:S(2)}, u32[]{:S(2)}) collective-permute-start(bf16[32,512]{1,0:T(8,128)(2,1)S(1)} %total.1.refs_0_), channel_id=1, source_target_pairs={{0,3},{1,0},{2,1},{3,2},{4,7},{5,4},{6,5},{7,6},{8,11},{9,8},{10,9... | collective-permute-start | bytes 98312 | tf_op jit(solution)/shard_map/ppermute | solution.py:919
  141.2 4.8 %collective-permute-start.18 = (bf16[32,512]{1,0:T(8,128)(2,1)S(1)}, bf16[32,512]{1,0:T(8,128)(2,1)S(1)}, u32[]{:S(2)}, u32[]{:S(2)}) collective-permute-start(bf16[32,512]{1,0:T(8,128)(2,1)S(1)} %total.1.refs_0_), channel_id=1, source_target_pairs={{0,2},{1,3},{2,0},{3,1},{4,6},{5,7},{6,4},{7,5},{8,10},{9,11},{10,... | collective-permute-start | bytes 98312 | tf_op jit(solution)/shard_map/ppermute | solution.py:919
  141.2 5.7 %collective-permute-start.17 = (bf16[32,512]{1,0:T(8,128)(2,1)S(1)}, bf16[32,512]{1,0:T(8,128)(2,1)S(1)}, u32[]{:S(2)}, u32[]{:S(2)}) collective-permute-start(bf16[32,512]{1,0:T(8,128)(2,1)S(1)} %total.1.refs_0_), channel_id=1, source_target_pairs={{0,1},{1,2},{2,3},{3,0},{4,5},{5,6},{6,7},{7,4},{8,9},{9,10},{10,1... | collective-permute-start | bytes 98312 | tf_op jit(solution)/shard_map/ppermute | solution.py:919
  147.5 6.0 %collective-permute-start.22 = (bf16[4,32,512]{2,1,0:T(8,128)(2,1)S(1)}, bf16[4,32,512]{2,1,0:T(8,128)(2,1)S(1)}, u32[]{:S(2)}, u32[]{:S(2)}) collective-permute-start(bf16[4,32,512]{2,1,0:T(8,128)(2,1)S(1)} %gather_band.1.refs_0_), channel_id=1, source_target_pairs={{0,24},{4,28},{8,16},{12,20},{16,8},{20,12},{24,0},{28,4},{1,25},{... | collective-permute-start | bytes 393224 | tf_op jit(solution)/shard_map/ppermute | solution.py:745
  149.3 5.5 %collective-permute-start.21 = (bf16[4,32,512]{2,1,0:T(8,128)(2,1)S(1)}, bf16[4,32,512]{2,1,0:T(8,128)(2,1)S(1)}, u32[]{:S(2)}, u32[]{:S(2)}) collective-permute-start(bf16[4,32,512]{2,1,0:T(8,128)(2,1)S(1)} %gather_band.1.refs_0_), channel_id=1, source_target_pairs={{0,16},{4,20},{8,24},{12,28},{16,0},{20,4},{24,8},{28,12},{1,17},{... | collective-permute-start | bytes 393224 | tf_op jit(solution)/shard_map/ppermute | solution.py:745
  149.8 5.0 %collective-permute-start.20 = (bf16[4,32,512]{2,1,0:T(8,128)(2,1)S(1)}, bf16[4,32,512]{2,1,0:T(8,128)(2,1)S(1)}, u32[]{:S(2)}, u32[]{:S(2)}) collective-permute-start(bf16[4,32,512]{2,1,0:T(8,128)(2,1)S(1)} %gather_band.1.refs_0_), channel_id=1, source_target_pairs={{0,8},{4,12},{8,0},{12,4},{16,24},{20,28},{24,16},{28,20},{1,9},{5... | collective-permute-start | bytes 393224 | tf_op jit(solution)/shard_map/ppermute | solution.py:745
  155.4 2.0 %collective-permute-start.23 = (bf16[16,32,512]{2,1,0:T(8,128)(2,1)S(1)}, bf16[16,32,512]{2,1,0:T(8,128)(2,1)S(1)}, u32[]{:S(2)}, u32[]{:S(2)}) collective-permute-start(bf16[16,32,512]{2,1,0:T(8,128)(2,1)S(1)} %bitcast.21), channel_id=1, source_target_pairs={{0,4},{4,0},{8,12},{12,8},{16,20},{20,16},{24,28},{28,24},{1,5},{5... | collective-permute-start | bytes 1572872 | tf_op jit(solution)/shard_map/ppermute | solution.py:745
  (3 other events, 175.9 us)

commit v6 on v5

--- a/solution.py
+++ b/solution.py
@@ -886,7 +886,7 @@
     keep, send = pl.pallas_call(
         functools.partial(backward_kernel, cols, sub),
         grid=(steps,),
-        out_shape=(near(half_shape), near((devices // 2, wires, hidden), BF16)),
+        out_shape=(pltpu.VMEM(half_shape, F32), pltpu.VMEM((devices // 2, wires, hidden), BF16)),
         in_specs=[chunk] * 4 + [smem] + [whole] * 10,
         out_specs=(whole,) * 2,
         scratch_shapes=[
@@ -922,7 +922,7 @@
     block = shape((bands, wires, hidden), BF16)
     tile = shape((wires, hidden), BF16)
     mine, *sends = call(
-        halve_kernel, "halve", (shape((bands, each, hidden)),) + (block,) * (chips - 1), place, far(keep), got
+        halve_kernel, "halve", (shape((bands, each, hidden)),) + (block,) * (chips - 1), place, keep, got
     )
     gots = [swap(a, 2 * (m + 1)) for m, a in enumerate(sends)]
     mine, *sends = call(

time: 164 us -> 163 us (level)
  Pallas kernels: 95.9 us -> 94.2 us
where the time goes in v6:
time: 163 us; the launch traced here: 162 us
  Pallas kernels  94.2 us (58%)
  starting transfers between devices  39.5 us (24%)
  waiting for transfers between devices  25.3 us (16%)
  other arithmetic  1.65 us (1%)
    pallas_call x1, Pallas kernels, body(): pl.pallas_call(functools.partial(backward_kernel, cols, sub), grid=(steps...  39 us
    pallas_call x1, Pallas kernels, body(): pl.pallas_call(functools.partial(forward_kernel, cols, sub), grid=(steps,...  34.4 us
    ppermute x12, waiting for transfers between devices, swap(): return lax.ppermute(array, 'dp', pairs)  16.7 us
    ppermute x3, starting transfers between devices, exchange_rows(): before = lax.ppermute(down, 'band', [(i, i + 1) for i in range(count - 1)])  14.5 us
    ppermute x12, starting transfers between devices, swap(): return lax.ppermute(array, 'dp', pairs)  10.9 us
    ppermute x6, starting transfers between devices, turn(): lax.ppermute(array, 'band', [(i, (i + k) % bands) for i in range(bands)])  10.1 us
    pallas_call x2, Pallas kernels, local(): pl.pallas_call(kernel, out_shape=outs, in_specs=[whole for _ in inputs],...  8.74 us
    ppermute x6, waiting for transfers between devices, turn(): lax.ppermute(array, 'band', [(i, (i + k) % bands) for i in range(bands)])  7.64 us
  transfers between devices with their start and end apart: 24, of which 18 were waited for; matrix products, arithmetic and copies ran while one was open for 0% of the time, Pallas kernels for 5%

profile of v6, /device:TPU:0, one launch (start us, length us, event | category | flops | bytes accessed | tf_op | source)
XLA Modules:
  0.0 162.2 jit_solution(5449106849986908068)
XLA Ops:
  0.7 1.5 add_convert_fusion
  2.2 1.3 collective-permute-start.1
  3.5 5.6 %collective-permute-start = (bf16[12,2,16,256]{3,2,1,0:T(8,128)(2,1)S(1)}, bf16[12,2,16,256]{3,2,1,0:T(8,128)(2,1)S(1)}, u32[]{:S(2)}, u32[]{:S(2)}) collective-permute-start(bf16[12,2,16,256]{3,2,1,0:T(8,128)(2,1)S(1)} %get-tuple-element.169), channel_id=1, source_target_pairs={{0,1},{1,2},{2,3},{4,5},{5,6},{6,7},{8,9},{9,10},{10,11},{12,13},{... | collective-permute-start | bytes 589832 | tf_op jit(solution)/shard_map/ppermute | solution.py:720
  9.2 3.4 %weights.1 = (bf16[512,128]{1,0:T(8,128)(2,1)}, f32[128,512]{1,0:T(8,128)}, bf16[512,512]{1,0:T(8,128)(2,1)}, bf16[512,512]{1,0:T(8,128)(2,1)}, f32[512,128]{1,0...) custom-call(f32[9,6,512]{2,1,0:T(8,128)} %bitcast.23, ...), custom_call_target="tpu_custom_call" | custom-call | tf_op jit(solution)/shard_map/weights/pallas_call | solution.py:753
  12.6 0.6 collective-permute-done.top
  13.2 34.4 %forward.1 = (bf16[8,512,2048]{2,1,0:T(8,128)(2,1)}, bf16[8,512,2048]{2,1,0:T(8,128)(2,1)}, bf16[8,512,2048]{2,1,0:T(8,128)(2,1)}, bf16[8,512,2048]{2,1,0:T(8,12...) custom-call(f32[12,4,16,256]{3,2,1,0:T(8,128)} %images.1, ...), custom_call_target="tpu_custom_call" | custom-call | flops 13153337344 | bytes 67108864 | tf_op jit(solution)/shard_map/forward/pallas_call | solution.py:788
  47.6 4.4 %collective-permute-start.3 = (bf16[16,16,256]{2,1,0:T(8,128)(2,1)}, bf16[16,16,256]{2,1,0:T(8,128)(2,1)S(1)}, u32[]{:S(2)}, u32[]{:S(2)}) collective-permute-start(bf16[16,16,256]{2,1,0:T(8,128)(2,1)} %get-tuple-element.108), channel_id=1, source_target_pairs={{0,1},{1,2},{2,3},{4,5},{5,6},{6,7},{8,9},{9,10},{10,11},{12,13},{... | collective-permute-start | bytes 393224 | tf_op jit(solution)/shard_map/ppermute | solution.py:720
  52.0 1.3 collective-permute-start.4
  53.3 2.7 %collective-permute-start.7 = (f32[16,128]{1,0:T(8,128)S(1)}, f32[16,128]{1,0:T(8,128)S(1)}, u32[]{:S(2)}, u32[]{:S(2)}) collective-permute-start(f32[16,128]{1,0:T(8,128)S(1)} %get-tuple-element.114.refs_0_), channel_id=1, source_target_pairs={{0,24},{4,28},{8,16},{12,20},{16,8},{20,12},{24,0},{28,4},{1,25},{... | collective-permute-start | bytes 24584 | tf_op jit(solution)/shard_map/ppermute | solution.py:745
  56.0 0.5 collective-permute-start.6
  56.9 1.1 collective-permute-done.7.refs_3_
  57.9 1.7 %collective-permute-done.6.refs_2_ = f32[16,128]{1,0:T(8,128)S(1)} collective-permute-done((f32[16,128]{1,0:T(8,128)S(1)}, f32[16,128]{1,0:T(8,128)S(1)}, u32[]{:S(2)}, u32[]{:S(2)}) %collective-permute-start.6) | collective-permute-done | bytes 8224 | tf_op jit(solution)/shard_map/ppermute | solution.py:745
  59.6 0.5 collective-permute-done.5.refs_1_
  60.2 3.7 %coupling.1 = (bf16[4,16,16,256]{3,2,1,0:T(8,128)(2,1)}, bf16[16,16,256]{2,1,0:T(8,128)(2,1)}, bf16[16,16,256]{2,1,0:T(8,128)(2,1)}, f32[2,64,2048]{2,1,0:T(8,12...) custom-call(f32[4,16,16,256]{3,2,1,0:T(8,128)} %get-tuple-element.107.nn, ...), custom_call_target="tpu_custom_call" | custom-call | tf_op jit(solution)/shard_map/coupling/pallas_call | solution.py:825
  63.9 4.5 %collective-permute-start.8 = (bf16[16,16,256]{2,1,0:T(8,128)(2,1)}, bf16[16,16,256]{2,1,0:T(8,128)(2,1)S(1)}, u32[]{:S(2)}, u32[]{:S(2)}) collective-permute-start(bf16[16,16,256]{2,1,0:T(8,128)(2,1)} %get-tuple-element.116), channel_id=1, source_target_pairs={{0,1},{1,2},{2,3},{4,5},{5,6},{6,7},{8,9},{9,10},{10,11},{12,13},{... | collective-permute-start | bytes 393224 | tf_op jit(solution)/shard_map/ppermute | solution.py:720
  68.4 1.5 collective-permute-start.9
  70.0 5.1 %prior_grads.1 = (f32[288,128]{1,0:T(8,128)}, f32[16,512]{1,0:T(8,128)}) custom-call(bf16[4,16,16,256]{3,2,1,0:T(8,128)(2,1)} %get-tuple-element.115.dn, f32[2,64,2048]{2,1,0:T(8,128)} %get-tuple-element.123.dstats, bf16[4,8,16,256]{3,2,1,0:T(8,128)(2,1)} %get-tuple-element.124.dxb, f32[8,256]{1,0:T(8,128)} %get-tuple-element.125.loss_part, ...), custom_call_target="tpu_custom_call" | custom-call | tf_op jit(solution)/shard_map/prior_grads/pallas_call | solution.py:825
  75.0 0.4 collective-permute-done.9.dn_bottom
  75.7 39.0 %backward.1 = (f32[16,24,512]{2,1,0:T(8,128)S(1)}, bf16[16,32,512]{2,1,0:T(8,128)(2,1)S(1)}) custom-call(bf16[8,512,2048]{2,1,0:T(8,128)(2,1)} %get-tuple-element.103.act1, bf16[8,512,2048]{2,1,0:T(8,128)(2,1)} %get-tuple-element.104.sg1, bf16[8,512,2048]{2,1,0:T(8,128)(2,1)} %get-tuple-element.105.act2, bf16[8,512,2048]{2,1,0:T(8,128)(2,1)} %get-tuple-element.106.sg2, ...), custom_call_target="tpu_custom_call" | custom-call | tf_op jit(solution)/shard_map/backward/pallas_call | solution.py:886
  114.9 1.9 %collective-permute-done.10.got = bf16[16,32,512]{2,1,0:T(8,128)(2,1)S(1)} collective-permute-done((bf16[16,32,512]{2,1,0:T(8,128)(2,1)S(1)}, bf16[16,32,512]{2,1,0:T(8,128)(2,1)S(1)}, u32[]{:S(2)}, u32[]{:S(2)}) %collective-permute-start.10) | collective-permute-done | bytes 524320 | tf_op jit(solution)/shard_map/ppermute | solution.py:745
  116.8 0.7 halve.1
  117.4 0.4 collective-permute-start.11
  117.9 1.7 %collective-permute-start.12 = (bf16[4,32,512]{2,1,0:T(8,128)(2,1)S(1)}, bf16[4,32,512]{2,1,0:T(8,128)(2,1)S(1)}, u32[]{:S(2)}, u32[]{:S(2)}) collective-permute-start(bf16[4,32,512]{2,1,0:T(8,128)(2,1)S(1)} %get-tuple-element.135), channel_id=1, source_target_pairs={{0,16},{4,20},{8,24},{12,28},{16,0},{20,4},{24,8},{28,12},{1,17},{... | collective-permute-start | bytes 393224 | tf_op jit(solution)/shard_map/ppermute | solution.py:745
  119.5 1.4 collective-permute-start.13
  121.0 2.9 %collective-permute-done.11.refs_1_ = bf16[4,32,512]{2,1,0:T(8,128)(2,1)S(1)} collective-permute-done((bf16[4,32,512]{2,1,0:T(8,128)(2,1)S(1)}, bf16[4,32,512]{2,1,0:T(8,128)(2,1)S(1)}, u32[]{:S(2)}, u32[]{:S(2)}) %collective-permute-start.11) | collective-permute-done | bytes 131104 | tf_op jit(solution)/shard_map/ppermute | solution.py:745
  123.8 1.3 collective-permute-done.12.refs_2_
  125.2 1.6 %collective-permute-done.13.refs_3_ = bf16[4,32,512]{2,1,0:T(8,128)(2,1)S(1)} collective-permute-done((bf16[4,32,512]{2,1,0:T(8,128)(2,1)S(1)}, bf16[4,32,512]{2,1,0:T(8,128)(2,1)S(1)}, u32[]{:S(2)}, u32[]{:S(2)}) %collective-permute-start.13) | collective-permute-done | bytes 131104 | tf_op jit(solution)/shard_map/ppermute | solution.py:745
  126.8 0.6 spread.1
  127.4 2.3 %collective-permute-start.14 = (bf16[32,512]{1,0:T(8,128)(2,1)S(1)}, bf16[32,512]{1,0:T(8,128)(2,1)S(1)}, u32[]{:S(2)}, u32[]{:S(2)}) collective-permute-start(bf16[32,512]{1,0:T(8,128)(2,1)S(1)} %get-tuple-element.138), channel_id=1, source_target_pairs={{0,1},{1,2},{2,3},{3,0},{4,5},{5,6},{6,7},{7,4},{8,9},{9,10},{10,1... | collective-permute-start | bytes 98312 | tf_op jit(solution)/shard_map/ppermute | solution.py:919
  129.7 2.6 %collective-permute-start.15 = (bf16[32,512]{1,0:T(8,128)(2,1)S(1)}, bf16[32,512]{1,0:T(8,128)(2,1)S(1)}, u32[]{:S(2)}, u32[]{:S(2)}) collective-permute-start(bf16[32,512]{1,0:T(8,128)(2,1)S(1)} %get-tuple-element.139), channel_id=1, source_target_pairs={{0,2},{1,3},{2,0},{3,1},{4,6},{5,7},{6,4},{7,5},{8,10},{9,11},{10,... | collective-permute-start | bytes 98312 | tf_op jit(solution)/shard_map/ppermute | solution.py:919
  132.3 1.3 collective-permute-start.16
  133.7 0.4 collective-permute-done.14.refs_0_
  134.1 0.6 collective-permute-done.15.refs_1_
  134.7 1.6 collective-permute-done.16.refs_2_
  136.3 3.2 %collective-permute-start.19 = (bf16[32,512]{1,0:T(8,128)(2,1)S(1)}, bf16[32,512]{1,0:T(8,128)(2,1)S(1)}, u32[]{:S(2)}, u32[]{:S(2)}) collective-permute-start(bf16[32,512]{1,0:T(8,128)(2,1)S(1)} %total.1.refs_0_), channel_id=1, source_target_pairs={{0,3},{1,0},{2,1},{3,2},{4,7},{5,4},{6,5},{7,6},{8,11},{9,8},{10,9... | collective-permute-start | bytes 98312 | tf_op jit(solution)/shard_map/ppermute | solution.py:919
  139.5 0.6 collective-permute-start.17
  140.1 1.0 collective-permute-done.19.refs_3_
  141.0 3.2 %collective-permute-done.18.refs_2_ = bf16[32,512]{1,0:T(8,128)(2,1)S(1)} collective-permute-done((bf16[32,512]{1,0:T(8,128)(2,1)S(1)}, bf16[32,512]{1,0:T(8,128)(2,1)S(1)}, u32[]{:S(2)}, u32[]{:S(2)}) %collective-permute-start.18) | collective-permute-done | bytes 32800 | tf_op jit(solution)/shard_map/ppermute | solution.py:919
  144.3 0.9 collective-permute-done.17.refs_1_
  145.2 0.6 gather_band.1.refs_0_
  145.7 1.8 %collective-permute-start.22 = (bf16[4,32,512]{2,1,0:T(8,128)(2,1)S(1)}, bf16[4,32,512]{2,1,0:T(8,128)(2,1)S(1)}, u32[]{:S(2)}, u32[]{:S(2)}) collective-permute-start(bf16[4,32,512]{2,1,0:T(8,128)(2,1)S(1)} %gather_band.1.refs_0_), channel_id=1, source_target_pairs={{0,24},{4,28},{8,16},{12,20},{16,8},{20,12},{24,0},{28,4},{1,25},{... | collective-permute-start | bytes 393224 | tf_op jit(solution)/shard_map/ppermute | solution.py:745
  147.5 0.5 collective-permute-start.21
  148.0 1.2 collective-permute-start.20
  149.3 2.4 %collective-permute-done.22.refs_3_ = bf16[4,32,512]{2,1,0:T(8,128)(2,1)S(1)} collective-permute-done((bf16[4,32,512]{2,1,0:T(8,128)(2,1)S(1)}, bf16[4,32,512]{2,1,0:T(8,128)(2,1)S(1)}, u32[]{:S(2)}, u32[]{:S(2)}) %collective-permute-start.22) | collective-permute-done | bytes 131104 | tf_op jit(solution)/shard_map/ppermute | solution.py:745
  151.7 1.3 collective-permute-done.21.refs_2_
  153.1 0.6 gather_chips.1
  153.7 1.9 %collective-permute-done.23.refs_2_ = bf16[16,32,512]{2,1,0:T(8,128)(2,1)S(1)} collective-permute-done((bf16[16,32,512]{2,1,0:T(8,128)(2,1)S(1)}, bf16[16,32,512]{2,1,0:T(8,128)(2,1)S(1)}, u32[]{:S(2)}, u32[]{:S(2)}) %collective-permute-start.23) | collective-permute-done | bytes 524320 | tf_op jit(solution)/shard_map/ppermute | solution.py:745
  155.9 6.2 %update.1 = (f32[1,1]{1,0:T(1,128)}, f32[1,1]{1,0:T(1,128)}, f32[9,6,512]{2,1,0:T(8,128)}, f32[512,512]{1,0:T(8,128)}, f32[9,12,512]{2,1,0:T(8,128)}, /*index=5*...) custom-call(s32[3]{0:T(128)S(1)} %pad_add_fusion.place.p.refs_0_, ...), custom_call_target="tpu_custom_call" | custom-call | tf_op jit(solution)/shard_map/update/pallas_call | solution.py:955
  (68 shorter events, 0.9 us)
Async XLA Ops:
  2.2 10.4 %collective-permute-start.1 = (bf16[12,2,16,256]{3,2,1,0:T(8,128)(2,1)S(1)}, bf16[12,2,16,256]{3,2,1,0:T(8,128)(2,1)S(1)}, u32[]{:S(2)}, u32[]{:S(2)}) collective-permute-start(bf16[12,2,16,256]{3,2,1,0:T(8,128)(2,1)S(1)} %get-tuple-element.168), channel_id=1, source_target_pairs={{1,0},{2,1},{3,2},{5,4},{6,5},{7,6},{9,8},{10,9},{11,10},{13,12},{... | collective-permute-start | bytes 589832 | tf_op jit(solution)/shard_map/ppermute | solution.py:721
  3.5 9.7 %collective-permute-start = (bf16[12,2,16,256]{3,2,1,0:T(8,128)(2,1)S(1)}, bf16[12,2,16,256]{3,2,1,0:T(8,128)(2,1)S(1)}, u32[]{:S(2)}, u32[]{:S(2)}) collective-permute-start(bf16[12,2,16,256]{3,2,1,0:T(8,128)(2,1)S(1)} %get-tuple-element.169), channel_id=1, source_target_pairs={{0,1},{1,2},{2,3},{4,5},{5,6},{6,7},{8,9},{9,10},{10,11},{12,13},{... | collective-permute-start | bytes 589832 | tf_op jit(solution)/shard_map/ppermute | solution.py:720
  9.0 3.5 %collective-permute-start.2 = (s32[1,256]{1,0:T(1,128)}, s32[1,256]{1,0:T(1,128)S(1)}, u32[]{:S(2)}, u32[]{:S(2)}) collective-permute-start(s32[1,256]{1,0:T(1,128)} %bitcast.31), channel_id=1, source_target_pairs={{0,4},{4,0},{8,12},{12,8},{16,20},{20,16},{24,28},{28,24},{1,5},{5... | collective-permute-start | bytes 3080 | tf_op jit(solution)/shard_map/ppermute | solution.py:745
  47.6 12.5 %collective-permute-start.3 = (bf16[16,16,256]{2,1,0:T(8,128)(2,1)}, bf16[16,16,256]{2,1,0:T(8,128)(2,1)S(1)}, u32[]{:S(2)}, u32[]{:S(2)}) collective-permute-start(bf16[16,16,256]{2,1,0:T(8,128)(2,1)} %get-tuple-element.108), channel_id=1, source_target_pairs={{0,1},{1,2},{2,3},{4,5},{5,6},{6,7},{8,9},{9,10},{10,11},{12,13},{... | collective-permute-start | bytes 393224 | tf_op jit(solution)/shard_map/ppermute | solution.py:720
  52.0 8.1 %collective-permute-start.4 = (bf16[16,16,256]{2,1,0:T(8,128)(2,1)}, bf16[16,16,256]{2,1,0:T(8,128)(2,1)S(1)}, u32[]{:S(2)}, u32[]{:S(2)}) collective-permute-start(bf16[16,16,256]{2,1,0:T(8,128)(2,1)} %get-tuple-element.109), channel_id=1, source_target_pairs={{1,0},{2,1},{3,2},{5,4},{6,5},{7,6},{9,8},{10,9},{11,10},{13,12},{... | collective-permute-start | bytes 393224 | tf_op jit(solution)/shard_map/ppermute | solution.py:721
  53.3 4.6 %collective-permute-start.7 = (f32[16,128]{1,0:T(8,128)S(1)}, f32[16,128]{1,0:T(8,128)S(1)}, u32[]{:S(2)}, u32[]{:S(2)}) collective-permute-start(f32[16,128]{1,0:T(8,128)S(1)} %get-tuple-element.114.refs_0_), channel_id=1, source_target_pairs={{0,24},{4,28},{8,16},{12,20},{16,8},{20,12},{24,0},{28,4},{1,25},{... | collective-permute-start | bytes 24584 | tf_op jit(solution)/shard_map/ppermute | solution.py:745
  56.0 3.7 %collective-permute-start.6 = (f32[16,128]{1,0:T(8,128)S(1)}, f32[16,128]{1,0:T(8,128)S(1)}, u32[]{:S(2)}, u32[]{:S(2)}) collective-permute-start(f32[16,128]{1,0:T(8,128)S(1)} %get-tuple-element.114.refs_0_), channel_id=1, source_target_pairs={{0,16},{4,20},{8,24},{12,28},{16,0},{20,4},{24,8},{28,12},{1,17},{... | collective-permute-start | bytes 24584 | tf_op jit(solution)/shard_map/ppermute | solution.py:745
  56.5 3.7 %collective-permute-start.5 = (f32[16,128]{1,0:T(8,128)S(1)}, f32[16,128]{1,0:T(8,128)S(1)}, u32[]{:S(2)}, u32[]{:S(2)}) collective-permute-start(f32[16,128]{1,0:T(8,128)S(1)} %get-tuple-element.114.refs_0_), channel_id=1, source_target_pairs={{0,8},{4,12},{8,0},{12,4},{16,24},{20,28},{24,16},{28,20},{1,9},{5... | collective-permute-start | bytes 24584 | tf_op jit(solution)/shard_map/ppermute | solution.py:745
  63.9 11.2 %collective-permute-start.8 = (bf16[16,16,256]{2,1,0:T(8,128)(2,1)}, bf16[16,16,256]{2,1,0:T(8,128)(2,1)S(1)}, u32[]{:S(2)}, u32[]{:S(2)}) collective-permute-start(bf16[16,16,256]{2,1,0:T(8,128)(2,1)} %get-tuple-element.116), channel_id=1, source_target_pairs={{0,1},{1,2},{2,3},{4,5},{5,6},{6,7},{8,9},{9,10},{10,11},{12,13},{... | collective-permute-start | bytes 393224 | tf_op jit(solution)/shard_map/ppermute | solution.py:720
  68.4 7.1 %collective-permute-start.9 = (bf16[16,16,256]{2,1,0:T(8,128)(2,1)}, bf16[16,16,256]{2,1,0:T(8,128)(2,1)S(1)}, u32[]{:S(2)}, u32[]{:S(2)}) collective-permute-start(bf16[16,16,256]{2,1,0:T(8,128)(2,1)} %get-tuple-element.117), channel_id=1, source_target_pairs={{1,0},{2,1},{3,2},{5,4},{6,5},{7,6},{9,8},{10,9},{11,10},{13,12},{... | collective-permute-start | bytes 393224 | tf_op jit(solution)/shard_map/ppermute | solution.py:721
  75.5 80.2 %copy-start = (f32[512,512]{1,0:T(8,128)S(1)}, f32[512,512]{1,0:T(8,128)}, u32[]{:S(2)}) copy-start(f32[512,512]{1,0:T(8,128)} %refs_5_.1) | copy-start | bytes 3145732
  75.5 80.2 %copy-start.1 = (f32[9,12,512]{2,1,0:T(8,128)S(1)}, f32[9,12,512]{2,1,0:T(8,128)}, u32[]{:S(2)}) copy-start(f32[9,12,512]{2,1,0:T(8,128)} %refs_6_.1) | copy-start | bytes 663556
  75.5 80.2 %copy-start.2 = (f32[512,512]{1,0:T(8,128)S(1)}, f32[512,512]{1,0:T(8,128)}, u32[]{:S(2)}) copy-start(f32[512,512]{1,0:T(8,128)} %refs_13_.1) | copy-start | bytes 3145732
  75.5 80.2 %copy-start.3 = (f32[512,512]{1,0:T(8,128)S(1)}, f32[512,512]{1,0:T(8,128)}, u32[]{:S(2)}) copy-start(f32[512,512]{1,0:T(8,128)} %refs_21_.1) | copy-start | bytes 3145732
  75.5 80.2 %copy-start.4 = (f32[9,512,6]{1,2,0:T(8,128)S(1)}, f32[9,512,6]{1,2,0:T(8,128)}, u32[]{:S(2)}) copy-start(f32[9,512,6]{1,2,0:T(8,128)} %param.30) | copy-start | bytes 331780
  75.5 80.2 %copy-start.5 = (f32[9,48,24]{1,2,0:T(8,128)S(1)}, f32[9,48,24]{1,2,0:T(8,128)}, u32[]{:S(2)}) copy-start(f32[9,48,24]{1,2,0:T(8,128)} %param.33) | copy-start | bytes 124420
  75.5 80.2 %copy-start.6 = (f32[9,12,512]{2,1,0:T(8,128)S(1)}, f32[9,12,512]{2,1,0:T(8,128)}, u32[]{:S(2)}) copy-start(f32[9,12,512]{2,1,0:T(8,128)} %refs_14_.1) | copy-start | bytes 663556
  75.5 80.2 %copy-start.7 = (f32[9,12,512]{2,1,0:T(8,128)S(1)}, f32[9,12,512]{2,1,0:T(8,128)}, u32[]{:S(2)}) copy-start(f32[9,12,512]{2,1,0:T(8,128)} %refs_22_.1) | copy-start | bytes 663556
  75.5 80.2 %copy-start.8 = (f32[9,512,6]{1,2,0:T(8,128)S(1)}, f32[9,512,6]{1,2,0:T(8,128)}, u32[]{:S(2)}) copy-start(f32[9,512,6]{1,2,0:T(8,128)} %param.38) | copy-start | bytes 331780
  75.5 80.2 %copy-start.9 = (f32[9,512,6]{1,2,0:T(8,128)S(1)}, f32[9,512,6]{1,2,0:T(8,128)}, u32[]{:S(2)}) copy-start(f32[9,512,6]{1,2,0:T(8,128)} %param.46) | copy-start | bytes 331780
  75.6 80.2 %copy-start.10 = (f32[9,48,24]{1,2,0:T(8,128)S(1)}, f32[9,48,24]{1,2,0:T(8,128)}, u32[]{:S(2)}) copy-start(f32[9,48,24]{1,2,0:T(8,128)} %param.41) | copy-start | bytes 124420
  75.6 80.2 %copy-start.11 = (f32[9,48,24]{1,2,0:T(8,128)S(1)}, f32[9,48,24]{1,2,0:T(8,128)}, u32[]{:S(2)}) copy-start(f32[9,48,24]{1,2,0:T(8,128)} %param.49) | copy-start | bytes 124420
  75.6 80.2 %copy-start.12 = (f32[12,12]{1,0:T(8,128)S(1)}, f32[12,12]{1,0:T(8,128)}, u32[]{:S(2)}) copy-start(f32[12,12]{1,0:T(8,128)} %refs_10_.1) | copy-start | bytes 1732
  75.6 80.1 %copy-start.13 = (f32[10,96]{1,0:T(8,128)S(1)}, f32[10,96]{1,0:T(8,128)}, u32[]{:S(2)}) copy-start(f32[10,96]{1,0:T(8,128)} %refs_11_.1) | copy-start | bytes 11524
  75.6 80.1 %copy-start.14 = (f32[2,512]{1,0:T(2,128)S(1)}, f32[2,512]{1,0:T(2,128)}, u32[]{:S(2)}) copy-start(f32[2,512]{1,0:T(2,128)} %refs_8_.1) | copy-start | bytes 12292
  75.6 80.1 %copy-start.15 = (f32[3,12]{1,0:T(4,128)S(1)}, f32[3,12]{1,0:T(4,128)}, u32[]{:S(2)}) copy-start(f32[3,12]{1,0:T(4,128)} %refs_9_.1) | copy-start | bytes 436
  75.6 80.1 %copy-start.16 = (f32[12,12]{1,0:T(8,128)S(1)}, f32[12,12]{1,0:T(8,128)}, u32[]{:S(2)}) copy-start(f32[12,12]{1,0:T(8,128)} %refs_18_.1) | copy-start | bytes 1732
  75.6 80.1 %copy-start.17 = (f32[10,96]{1,0:T(8,128)S(1)}, f32[10,96]{1,0:T(8,128)}, u32[]{:S(2)}) copy-start(f32[10,96]{1,0:T(8,128)} %refs_19_.1) | copy-start | bytes 11524
  75.7 80.1 %copy-start.18 = (f32[12,12]{1,0:T(8,128)S(1)}, f32[12,12]{1,0:T(8,128)}, u32[]{:S(2)}) copy-start(f32[12,12]{1,0:T(8,128)} %refs_26_.1) | copy-start | bytes 1732
  75.7 80.1 %copy-start.19 = (f32[10,96]{1,0:T(8,128)S(1)}, f32[10,96]{1,0:T(8,128)}, u32[]{:S(2)}) copy-start(f32[10,96]{1,0:T(8,128)} %refs_27_.1) | copy-start | bytes 11524
  75.7 80.1 %copy-start.20 = (f32[16,128]{1,0:T(8,128)S(1)}, f32[16,128]{1,0:T(8,128)}, u32[]{:S(2)}) copy-start(f32[16,128]{1,0:T(8,128)} %get-tuple-element.141.refs_3_) | copy-start | bytes 24580
  75.7 80.1 %copy-start.23 = (f32[2,512]{1,0:T(2,128)S(1)}, f32[2,512]{1,0:T(2,128)}, u32[]{:S(2)}) copy-start(f32[2,512]{1,0:T(2,128)} %refs_16_.1) | copy-start | bytes 12292
  75.7 80.1 %copy-start.24 = (f32[2,512]{1,0:T(2,128)S(1)}, f32[2,512]{1,0:T(2,128)}, u32[]{:S(2)}) copy-start(f32[2,512]{1,0:T(2,128)} %refs_24_.1) | copy-start | bytes 12292
  75.7 80.1 %copy-start.25 = (f32[3,12]{1,0:T(4,128)S(1)}, f32[3,12]{1,0:T(4,128)}, u32[]{:S(2)}) copy-start(f32[3,12]{1,0:T(4,128)} %refs_17_.1) | copy-start | bytes 436
  114.8 2.0 %collective-permute-start.10 = (bf16[16,32,512]{2,1,0:T(8,128)(2,1)S(1)}, bf16[16,32,512]{2,1,0:T(8,128)(2,1)S(1)}, u32[]{:S(2)}, u32[]{:S(2)}) collective-permute-start(bf16[16,32,512]{2,1,0:T(8,128)(2,1)S(1)} %get-tuple-element.132), channel_id=1, source_target_pairs={{0,4},{4,0},{8,12},{12,8},{16,20},{20,16},{24,28},{28,24},{1,5},{5... | collective-permute-start | bytes 1572872 | tf_op jit(solution)/shard_map/ppermute | solution.py:745
  117.4 6.4 %collective-permute-start.11 = (bf16[4,32,512]{2,1,0:T(8,128)(2,1)S(1)}, bf16[4,32,512]{2,1,0:T(8,128)(2,1)S(1)}, u32[]{:S(2)}, u32[]{:S(2)}) collective-permute-start(bf16[4,32,512]{2,1,0:T(8,128)(2,1)S(1)} %get-tuple-element.134), channel_id=1, source_target_pairs={{0,8},{4,12},{8,0},{12,4},{16,24},{20,28},{24,16},{28,20},{1,9},{5... | collective-permute-start | bytes 393224 | tf_op jit(solution)/shard_map/ppermute | solution.py:745
  117.9 7.3 %collective-permute-start.12 = (bf16[4,32,512]{2,1,0:T(8,128)(2,1)S(1)}, bf16[4,32,512]{2,1,0:T(8,128)(2,1)S(1)}, u32[]{:S(2)}, u32[]{:S(2)}) collective-permute-start(bf16[4,32,512]{2,1,0:T(8,128)(2,1)S(1)} %get-tuple-element.135), channel_id=1, source_target_pairs={{0,16},{4,20},{8,24},{12,28},{16,0},{20,4},{24,8},{28,12},{1,17},{... | collective-permute-start | bytes 393224 | tf_op jit(solution)/shard_map/ppermute | solution.py:745
  119.5 7.3 %collective-permute-start.13 = (bf16[4,32,512]{2,1,0:T(8,128)(2,1)S(1)}, bf16[4,32,512]{2,1,0:T(8,128)(2,1)S(1)}, u32[]{:S(2)}, u32[]{:S(2)}) collective-permute-start(bf16[4,32,512]{2,1,0:T(8,128)(2,1)S(1)} %get-tuple-element.136), channel_id=1, source_target_pairs={{0,24},{4,28},{8,16},{12,20},{16,8},{20,12},{24,0},{28,4},{1,25},{... | collective-permute-start | bytes 393224 | tf_op jit(solution)/shard_map/ppermute | solution.py:745
  127.4 6.7 %collective-permute-start.14 = (bf16[32,512]{1,0:T(8,128)(2,1)S(1)}, bf16[32,512]{1,0:T(8,128)(2,1)S(1)}, u32[]{:S(2)}, u32[]{:S(2)}) collective-permute-start(bf16[32,512]{1,0:T(8,128)(2,1)S(1)} %get-tuple-element.138), channel_id=1, source_target_pairs={{0,1},{1,2},{2,3},{3,0},{4,5},{5,6},{6,7},{7,4},{8,9},{9,10},{10,1... | collective-permute-start | bytes 98312 | tf_op jit(solution)/shard_map/ppermute | solution.py:919
  129.7 4.9 %collective-permute-start.15 = (bf16[32,512]{1,0:T(8,128)(2,1)S(1)}, bf16[32,512]{1,0:T(8,128)(2,1)S(1)}, u32[]{:S(2)}, u32[]{:S(2)}) collective-permute-start(bf16[32,512]{1,0:T(8,128)(2,1)S(1)} %get-tuple-element.139), channel_id=1, source_target_pairs={{0,2},{1,3},{2,0},{3,1},{4,6},{5,7},{6,4},{7,5},{8,10},{9,11},{10,... | collective-permute-start | bytes 98312 | tf_op jit(solution)/shard_map/ppermute | solution.py:919
  132.3 3.9 %collective-permute-start.16 = (bf16[32,512]{1,0:T(8,128)(2,1)S(1)}, bf16[32,512]{1,0:T(8,128)(2,1)S(1)}, u32[]{:S(2)}, u32[]{:S(2)}) collective-permute-start(bf16[32,512]{1,0:T(8,128)(2,1)S(1)} %get-tuple-element.140), channel_id=1, source_target_pairs={{0,3},{1,0},{2,1},{3,2},{4,7},{5,4},{6,5},{7,6},{8,11},{9,8},{10,9... | collective-permute-start | bytes 98312 | tf_op jit(solution)/shard_map/ppermute | solution.py:919
  136.3 4.8 %collective-permute-start.19 = (bf16[32,512]{1,0:T(8,128)(2,1)S(1)}, bf16[32,512]{1,0:T(8,128)(2,1)S(1)}, u32[]{:S(2)}, u32[]{:S(2)}) collective-permute-start(bf16[32,512]{1,0:T(8,128)(2,1)S(1)} %total.1.refs_0_), channel_id=1, source_target_pairs={{0,3},{1,0},{2,1},{3,2},{4,7},{5,4},{6,5},{7,6},{8,11},{9,8},{10,9... | collective-permute-start | bytes 98312 | tf_op jit(solution)/shard_map/ppermute | solution.py:919
  139.4 4.8 %collective-permute-start.18 = (bf16[32,512]{1,0:T(8,128)(2,1)S(1)}, bf16[32,512]{1,0:T(8,128)(2,1)S(1)}, u32[]{:S(2)}, u32[]{:S(2)}) collective-permute-start(bf16[32,512]{1,0:T(8,128)(2,1)S(1)} %total.1.refs_0_), channel_id=1, source_target_pairs={{0,2},{1,3},{2,0},{3,1},{4,6},{5,7},{6,4},{7,5},{8,10},{9,11},{10,... | collective-permute-start | bytes 98312 | tf_op jit(solution)/shard_map/ppermute | solution.py:919
  139.5 5.7 %collective-permute-start.17 = (bf16[32,512]{1,0:T(8,128)(2,1)S(1)}, bf16[32,512]{1,0:T(8,128)(2,1)S(1)}, u32[]{:S(2)}, u32[]{:S(2)}) collective-permute-start(bf16[32,512]{1,0:T(8,128)(2,1)S(1)} %total.1.refs_0_), channel_id=1, source_target_pairs={{0,1},{1,2},{2,3},{3,0},{4,5},{5,6},{6,7},{7,4},{8,9},{9,10},{10,1... | collective-permute-start | bytes 98312 | tf_op jit(solution)/shard_map/ppermute | solution.py:919
  145.7 6.0 %collective-permute-start.22 = (bf16[4,32,512]{2,1,0:T(8,128)(2,1)S(1)}, bf16[4,32,512]{2,1,0:T(8,128)(2,1)S(1)}, u32[]{:S(2)}, u32[]{:S(2)}) collective-permute-start(bf16[4,32,512]{2,1,0:T(8,128)(2,1)S(1)} %gather_band.1.refs_0_), channel_id=1, source_target_pairs={{0,24},{4,28},{8,16},{12,20},{16,8},{20,12},{24,0},{28,4},{1,25},{... | collective-permute-start | bytes 393224 | tf_op jit(solution)/shard_map/ppermute | solution.py:745
  147.5 5.5 %collective-permute-start.21 = (bf16[4,32,512]{2,1,0:T(8,128)(2,1)S(1)}, bf16[4,32,512]{2,1,0:T(8,128)(2,1)S(1)}, u32[]{:S(2)}, u32[]{:S(2)}) collective-permute-start(bf16[4,32,512]{2,1,0:T(8,128)(2,1)S(1)} %gather_band.1.refs_0_), channel_id=1, source_target_pairs={{0,16},{4,20},{8,24},{12,28},{16,0},{20,4},{24,8},{28,12},{1,17},{... | collective-permute-start | bytes 393224 | tf_op jit(solution)/shard_map/ppermute | solution.py:745
  148.0 5.0 %collective-permute-start.20 = (bf16[4,32,512]{2,1,0:T(8,128)(2,1)S(1)}, bf16[4,32,512]{2,1,0:T(8,128)(2,1)S(1)}, u32[]{:S(2)}, u32[]{:S(2)}) collective-permute-start(bf16[4,32,512]{2,1,0:T(8,128)(2,1)S(1)} %gather_band.1.refs_0_), channel_id=1, source_target_pairs={{0,8},{4,12},{8,0},{12,4},{16,24},{20,28},{24,16},{28,20},{1,9},{5... | collective-permute-start | bytes 393224 | tf_op jit(solution)/shard_map/ppermute | solution.py:745
  153.7 2.0 %collective-permute-start.23 = (bf16[16,32,512]{2,1,0:T(8,128)(2,1)S(1)}, bf16[16,32,512]{2,1,0:T(8,128)(2,1)S(1)}, u32[]{:S(2)}, u32[]{:S(2)}) collective-permute-start(bf16[16,32,512]{2,1,0:T(8,128)(2,1)S(1)} %bitcast.21), channel_id=1, source_target_pairs={{0,4},{4,0},{8,12},{12,8},{16,20},{20,16},{24,28},{28,24},{1,5},{5... | collective-permute-start | bytes 1572872 | tf_op jit(solution)/shard_map/ppermute | solution.py:745
  (3 other events, 174.1 us)
